TPU v7x, 32 devices: a whole 2x2x4 slice. The times are simulated.
32 devices in a mesh: section: 2 (over core), batch: 16 (over z, y, x).
Axes of the slice: x: 2, y: 2, z: 4, core: 2. Of those that a mesh axis runs over, the one named last changes fastest.
Arguments:
- params: float32 [2, 3673088], P('section', 'batch'), may hold values from -1.5 to 1.5, as said below
- first_moment: float32 [2, 3673088], P('section', 'batch'), may hold values from -5.340576e-05 to 5.340576e-05
- second_moment: float32 [2, 3673088], P('section', 'batch'), may hold values from 1.9057533e-11 to 1.9057535e-10
- inputs: bfloat16 [2, 24576, 512], P('section', 'batch'), may hold values from -6 to 6
- segments: int32 [24576], P('batch'), may hold values from 0 to 191, never falling along the last dimension, each value on 1 to 250 neighbouring positions
- live_mask: int32 [2, 24576], P(None, 'batch'), may hold values 0 or 1
- out_grad: bfloat16 [24576, 512], P('batch'), may hold values from -6 to 6
Outputs:
- param_step: float32 [2, 3673088], P('section', 'batch')
- new_first: float32 [2, 3673088], P('section', 'batch')
- new_second: float32 [2, 3673088], P('section', 'batch')
- param_grad: float32 [2, 3673088], P('section', 'batch')
- layer_out: bfloat16 [2, 24576, 512], P('section', 'batch')
- input_grad: bfloat16 [2, 24576, 512], P('section', 'batch')
- grad_norm: float32 [], replicated
Inputs may be any that keep to these rules, and one draw needn't show every extreme that they name: `params`: weights are scaled by their fan-in, gains lie near 1 and shifts near 0.
All inputs are finite; a program needn't handle non-finite values. No bound on the sum of `live_mask` on one device may be relied on, other than what follows from the above.
Results may differ from a plain program's by a relative error of at most 0.02.
Values may be sent and summed in bfloat16 or wider, within the bound.
No kernel may reach another device: no remote copies, remote signals or barrier semaphores. Data moves between devices by JAX's collectives and lax.ppermute only.
A program may use at most 256 MiB of HBM per device.

v0:
```python
import jax
import jax.numpy as jnp
from jax import lax
from jax.sharding import PartitionSpec as P

D = 512
FF = 2048
HEADS = 8
HD = 64
ROW = 512
MICRO = 3
STEP = 1000
WARMUP = 4000


NEG = -1e30
LN_EPS = 1e-05
BETA_ONE = 0.9
BETA_TWO = 0.98
ADAM_EPS = 1e-09
MAXNORM = 0.1


def passed_along(value, axis, steps):
    count = lax.axis_size(axis)
    first, last = (max(0, -steps), min(count, count - steps))
    return lax.ppermute(value, axis, [(source, source + steps) for source in range(first, last)])


def layer_norm(residual, gain_vec, shift_vec):
    center = residual - jnp.mean(residual, axis=-1, keepdims=True)
    spread = jnp.mean(center * center, axis=-1, keepdims=True)
    return center * lax.rsqrt(spread + LN_EPS) * gain_vec + shift_vec


def gelu_exact(pre_value):
    return jax.nn.gelu(pre_value, approximate=False)


def dot_plain(lhs_mat, rhs_mat):
    return jnp.dot(lhs_mat, rhs_mat, preferred_element_type=jnp.float32)


def dot_left(lhs_mat, rhs_mat):
    return lax.dot_general(
        lhs_mat, rhs_mat, (((0,), (0,)), ((), ())), preferred_element_type=jnp.float32
    )


def dot_right(lhs_mat, rhs_mat):
    return lax.dot_general(
        lhs_mat, rhs_mat, (((1,), (1,)), ((), ())), preferred_element_type=jnp.float32
    )


def unpack(flat_vec):
    pieces = []
    offset = 0
    for rows_n, cols_n in ((D, 3 * D), (D, D), (D, 2 * D), (D, FF), (FF, D), (6, D)):
        pieces.append(flat_vec[offset : offset + rows_n * cols_n].reshape(rows_n, cols_n))
        offset = offset + rows_n * cols_n
    return pieces


def pack(pieces):
    return jnp.concatenate([part_mat.reshape(-1) for part_mat in pieces])


def build_masks(seg_rows, live_src, live_tgt):
    places = jnp.arange(seg_rows.shape[0])
    same_seg = seg_rows[:, None] == seg_rows[None, :]
    diagonal = places[:, None] == places[None, :]
    causal = places[None, :] <= places[:, None]
    enc_mask = same_seg & ((live_src[None, :] == 1) | diagonal)
    dec_mask = same_seg & causal & ((live_tgt[None, :] == 1) | diagonal)
    return (enc_mask, dec_mask)


def split_heads(tensor):
    return tensor.reshape(tensor.shape[0], HEADS, HD)


def attend_scores(head_q, head_k, allowed):
    scores = jnp.einsum(
        "qhd,khd->hqk", head_q, head_k, preferred_element_type=jnp.float32
    ) * HD ** (-0.5)
    return jnp.where(allowed[None], scores, NEG)


def attend_forward(queries, key_rows, values, allowed):
    scores = attend_scores(split_heads(queries), split_heads(key_rows), allowed)
    row_top = jnp.max(scores, axis=-1, keepdims=True)
    log_total = row_top + jnp.log(jnp.sum(jnp.exp(scores - row_top), axis=-1, keepdims=True))
    attn_probs = jnp.exp(scores - log_total)
    context = jnp.einsum(
        "hqk,khd->qhd",
        attn_probs.astype(jnp.bfloat16),
        split_heads(values),
        preferred_element_type=jnp.float32,
    )
    return (context.reshape(queries.shape[0], D).astype(jnp.bfloat16), log_total)


def attend_backward(queries, key_rows, values, allowed, log_total, grad_context):
    head_q = split_heads(queries)
    head_k = split_heads(key_rows)
    head_g = split_heads(grad_context)
    attn_probs = jnp.exp(attend_scores(head_q, head_k, allowed) - log_total)
    grad_probs = jnp.einsum(
        "qhd,khd->hqk", head_g, split_heads(values), preferred_element_type=jnp.float32
    )
    grad_values = jnp.einsum(
        "hqk,qhd->khd", attn_probs.astype(jnp.bfloat16), head_g, preferred_element_type=jnp.float32
    )
    grad_scores = (
        attn_probs * (grad_probs - jnp.sum(grad_probs * attn_probs, axis=-1, keepdims=True))
    ).astype(jnp.bfloat16)
    score_scale = HD ** (-0.5)
    grad_query = (
        jnp.einsum("hqk,khd->qhd", grad_scores, head_k, preferred_element_type=jnp.float32)
        * score_scale
    )
    grad_keys = (
        jnp.einsum("hqk,qhd->khd", grad_scores, head_q, preferred_element_type=jnp.float32)
        * score_scale
    )
    rows_n = queries.shape[0]
    return (
        grad_query.reshape(rows_n, D),
        grad_keys.reshape(rows_n, D),
        grad_values.reshape(rows_n, D),
    )


def self_forward(w_qkv, w_out, vectors, block_in, allowed):
    projected = dot_plain(block_in, w_qkv).astype(jnp.bfloat16)
    context, log_total = attend_forward(
        projected[:, :D], projected[:, D : 2 * D], projected[:, 2 * D :], allowed
    )
    residual = block_in.astype(jnp.float32) + dot_plain(context, w_out)
    return (layer_norm(residual, vectors[0], vectors[1]), (projected, log_total, context, residual))


def self_backward(w_qkv, w_out, vectors, block_in, allowed, kept_state, grad_hidden):
    projected, log_total, context, residual = kept_state
    _, norm_back = jax.vjp(layer_norm, residual, vectors[0], vectors[1])
    grad_resid, grad_gain, grad_shift = norm_back(grad_hidden)
    grad_branch = grad_resid.astype(jnp.bfloat16)
    grad_out = dot_left(context, grad_branch)
    grad_context = dot_right(grad_branch, w_out).astype(jnp.bfloat16)
    grad_query, grad_keys, grad_values = attend_backward(
        projected[:, :D],
        projected[:, D : 2 * D],
        projected[:, 2 * D :],
        allowed,
        log_total,
        grad_context,
    )
    grad_proj = jnp.concatenate([grad_query, grad_keys, grad_values], axis=1).astype(jnp.bfloat16)
    grad_qkv = dot_left(block_in, grad_proj)
    grad_in = grad_resid + dot_right(grad_proj, w_qkv)
    return (grad_in, grad_qkv, grad_out, grad_gain, grad_shift)


def ffn_forward(w_up, w_down, gain_vec, shift_vec, hidden):
    hidden_b = hidden.astype(jnp.bfloat16)
    pre_act = dot_plain(hidden_b, w_up)
    act_b = gelu_exact(pre_act).astype(jnp.bfloat16)
    residual = hidden + dot_plain(act_b, w_down)
    return (layer_norm(residual, gain_vec, shift_vec), (hidden_b, pre_act, act_b, residual))


def ffn_backward(w_up, w_down, gain_vec, shift_vec, kept_state, grad_result):
    hidden_b, pre_act, act_b, residual = kept_state
    _, norm_back = jax.vjp(layer_norm, residual, gain_vec, shift_vec)
    grad_resid, grad_gain, grad_shift = norm_back(grad_result)
    grad_branch = grad_resid.astype(jnp.bfloat16)
    grad_down = dot_left(act_b, grad_branch)
    grad_act = dot_right(grad_branch, w_down)
    _, gelu_back = jax.vjp(gelu_exact, pre_act)
    grad_pre = gelu_back(grad_act)[0].astype(jnp.bfloat16)
    grad_up = dot_left(hidden_b, grad_pre)
    grad_hidden = grad_resid + dot_right(grad_pre, w_up)
    return (grad_hidden, grad_up, grad_down, grad_gain, grad_shift)


def encoder_forward(weights, vectors, source, enc_mask):
    w_qkv, w_out, w_cross, w_up, w_down = weights
    hidden_one, kept_self = self_forward(w_qkv, w_out, vectors, source, enc_mask)
    memory, kept_ffn = ffn_forward(w_up, w_down, vectors[2], vectors[3], hidden_one)
    memory_b = memory.astype(jnp.bfloat16)
    key_value = dot_plain(memory_b, w_cross).astype(jnp.bfloat16)
    return (memory_b, key_value, (kept_self, kept_ffn))


def encoder_blank(rows_n):
    kept_self = (
        jnp.zeros((rows_n, 3 * D), jnp.bfloat16),
        jnp.zeros((HEADS, rows_n, 1), jnp.float32),
        jnp.zeros((rows_n, D), jnp.bfloat16),
        jnp.zeros((rows_n, D), jnp.float32),
    )
    kept_ffn = (
        jnp.zeros((rows_n, D), jnp.bfloat16),
        jnp.zeros((rows_n, FF), jnp.float32),
        jnp.zeros((rows_n, FF), jnp.bfloat16),
        jnp.zeros((rows_n, D), jnp.float32),
    )
    return (
        jnp.zeros((rows_n, D), jnp.bfloat16),
        jnp.zeros((rows_n, 2 * D), jnp.bfloat16),
        (kept_self, kept_ffn),
    )


def encoder_backward(weights, vectors, source, enc_mask, memory_b, kept_state, grad_kv):
    w_qkv, w_out, w_cross, w_up, w_down = weights
    kept_self, kept_ffn = kept_state
    grad_cross = dot_left(memory_b, grad_kv)
    grad_memory = dot_right(grad_kv, w_cross)
    grad_hidden, grad_up, grad_down, gain_two, shift_two = ffn_backward(
        w_up, w_down, vectors[2], vectors[3], kept_ffn, grad_memory
    )
    grad_in, grad_qkv, grad_out, gain_one, shift_one = self_backward(
        w_qkv, w_out, vectors, source, enc_mask, kept_self, grad_hidden
    )
    unused = jnp.zeros((D,), jnp.float32)
    vector_grad = jnp.stack([gain_one, shift_one, gain_two, shift_two, unused, unused])
    return (pack([grad_qkv, grad_out, grad_cross, grad_up, grad_down, vector_grad]), grad_in)


def decoder_step(weights, vectors, target, key_value, enc_mask, dec_mask, grad_result):
    w_qkv, w_out, w_cross, w_up, w_down = weights
    hidden_one, kept_self = self_forward(w_qkv, w_out, vectors, target, dec_mask)
    hidden_one_b = hidden_one.astype(jnp.bfloat16)
    cross_query = dot_plain(hidden_one_b, w_cross[:, :D]).astype(jnp.bfloat16)
    cross_context, cross_total = attend_forward(
        cross_query, key_value[:, :D], key_value[:, D:], enc_mask
    )
    resid_two = hidden_one + dot_plain(cross_context, w_cross[:, D:])
    hidden_two = layer_norm(resid_two, vectors[2], vectors[3])
    result, kept_ffn = ffn_forward(w_up, w_down, vectors[4], vectors[5], hidden_two)
    grad_hidden_two, grad_up, grad_down, gain_three, shift_three = ffn_backward(
        w_up, w_down, vectors[4], vectors[5], kept_ffn, grad_result.astype(jnp.float32)
    )
    _, norm_back = jax.vjp(layer_norm, resid_two, vectors[2], vectors[3])
    grad_resid_two, gain_two, shift_two = norm_back(grad_hidden_two)
    grad_branch = grad_resid_two.astype(jnp.bfloat16)
    grad_cross_out = dot_left(cross_context, grad_branch)
    grad_context = dot_right(grad_branch, w_cross[:, D:]).astype(jnp.bfloat16)
    grad_query, grad_keys, grad_values = attend_backward(
        cross_query, key_value[:, :D], key_value[:, D:], enc_mask, cross_total, grad_context
    )
    grad_key_value = jnp.concatenate([grad_keys, grad_values], axis=1).astype(jnp.bfloat16)
    grad_query_b = grad_query.astype(jnp.bfloat16)
    grad_cross_query = dot_left(hidden_one_b, grad_query_b)
    grad_hidden_one = grad_resid_two + dot_right(grad_query_b, w_cross[:, :D])
    grad_in, grad_qkv, grad_out, gain_one, shift_one = self_backward(
        w_qkv, w_out, vectors, target, dec_mask, kept_self, grad_hidden_one
    )
    vector_grad = jnp.stack([gain_one, shift_one, gain_two, shift_two, gain_three, shift_three])
    grad_cross = jnp.concatenate([grad_cross_query, grad_cross_out], axis=1)
    return (
        result.astype(jnp.bfloat16),
        pack([grad_qkv, grad_out, grad_cross, grad_up, grad_down, vector_grad]),
        grad_in,
        grad_key_value,
    )


def decoder_blank(rows_n, total_n):
    return (
        jnp.zeros((rows_n, D), jnp.bfloat16),
        jnp.zeros((total_n,), jnp.float32),
        jnp.zeros((rows_n, D), jnp.float32),
        jnp.zeros((rows_n, 2 * D), jnp.bfloat16),
    )


def send_memory(key_value):
    return passed_along(key_value, "section", 1)


def return_grad(grad_kv):
    return passed_along(grad_kv, "section", -1)


def add_grad(grad_total, step_grad):
    return grad_total + step_grad


def put_rows(whole_rows, new_rows, row_index):
    row_start = row_index * new_rows.shape[0]
    old_rows = lax.dynamic_slice_in_dim(whole_rows, row_start, new_rows.shape[0], 0)
    return lax.dynamic_update_slice_in_dim(
        whole_rows, jnp.where(True, new_rows, old_rows), row_start, 0
    )


def shards(params, first_moment, second_moment, inputs, segments, live_mask, out_grad):
    is_decoder = lax.axis_index("section") == 1
    flat_b = lax.all_gather(params[0].astype(jnp.bfloat16), "batch", axis=0, tiled=True)
    pieces = unpack(flat_b)
    weights = tuple(pieces[:5])
    vectors = pieces[5].astype(jnp.float32)
    block_in = inputs[0]
    rows_n = ROW
    total_n = flat_b.shape[0]

    def row_data(row_index):
        row_start = row_index * rows_n
        rows_in = lax.dynamic_slice_in_dim(block_in, row_start, rows_n, 0)
        seg_rows = lax.dynamic_slice_in_dim(segments, row_start, rows_n, 0)
        live_rows = lax.dynamic_slice_in_dim(live_mask, row_start, rows_n, 1)
        cot_rows = lax.dynamic_slice_in_dim(out_grad, row_start, rows_n, 0)
        enc_mask, dec_mask = build_masks(seg_rows, live_rows[0], live_rows[1])
        return (rows_in, cot_rows, enc_mask, dec_mask)

    def zero_encoder_grad():
        return (jnp.zeros((total_n,), jnp.float32), jnp.zeros((rows_n, D), jnp.float32))

    grad_start = jnp.zeros((total_n,), jnp.float32)
    layer_start = jnp.zeros(block_in.shape, jnp.bfloat16)

    def micro_step(micro_index, carry):
        grad_total, layer_rows, grad_rows = carry
        rows_in, cot_rows, enc_mask, dec_mask = row_data(micro_index)
        memory_b, key_value, kept_state = lax.cond(
            is_decoder,
            lambda: encoder_blank(rows_n),
            lambda: encoder_forward(weights, vectors, rows_in, enc_mask),
        )
        arrived = send_memory(key_value)
        result_b, dec_grad, grad_target, grad_kv = lax.cond(
            is_decoder,
            lambda: decoder_step(weights, vectors, rows_in, arrived, enc_mask, dec_mask, cot_rows),
            lambda: decoder_blank(rows_n, total_n),
        )
        returned = return_grad(grad_kv)
        enc_grad, grad_source = lax.cond(
            is_decoder,
            zero_encoder_grad,
            lambda: encoder_backward(
                weights, vectors, rows_in, enc_mask, memory_b, kept_state, returned
            ),
        )
        grad_total = add_grad(grad_total, enc_grad + dec_grad)
        layer_rows = put_rows(layer_rows, jnp.where(is_decoder, result_b, memory_b), micro_index)
        grad_rows = put_rows(
            grad_rows,
            jnp.where(is_decoder, grad_target, grad_source).astype(jnp.bfloat16),
            micro_index,
        )
        return (grad_total, layer_rows, grad_rows)

    grad_total, layer_rows, grad_rows = lax.fori_loop(
        0, MICRO, micro_step, (grad_start, layer_start, layer_start)
    )
    grad_share = lax.psum_scatter(grad_total, "batch", scatter_dimension=0, tiled=True)
    square_sum = lax.psum(jnp.sum(grad_share * grad_share), ("section", "batch"))
    grad_norm = jnp.sqrt(square_sum)
    clip_factor = MAXNORM / jnp.maximum(grad_norm, MAXNORM)
    scaled = grad_share * clip_factor
    new_first = BETA_ONE * first_moment[0] + (1.0 - BETA_ONE) * scaled
    new_second = BETA_TWO * second_moment[0] + (1.0 - BETA_TWO) * scaled * scaled
    learn_rate = D ** (-0.5) * min(STEP ** (-0.5), STEP * WARMUP ** (-1.5))
    first_hat = new_first / (1.0 - BETA_ONE**STEP)
    second_hat = new_second / (1.0 - BETA_TWO**STEP)
    param_step = learn_rate * first_hat / (jnp.sqrt(second_hat) + ADAM_EPS)
    return (
        param_step[None],
        new_first[None],
        new_second[None],
        grad_share[None],
        layer_rows[None],
        grad_rows[None],
        grad_norm,
    )


def solution(mesh):
    in_specs = (
        P("section", "batch"),
        P("section", "batch"),
        P("section", "batch"),
        P("section", "batch", None),
        P("batch"),
        P(None, "batch"),
        P("batch", None),
    )
    out_specs = (
        P("section", "batch"),
        P("section", "batch"),
        P("section", "batch"),
        P("section", "batch"),
        P("section", "batch", None),
        P("section", "batch", None),
        P(),
    )
    return jax.shard_map(shards, mesh=mesh, in_specs=in_specs, out_specs=out_specs, check_vma=False)
```

profile of v0, /device:TPU:0, one launch (start us, length us, event | category | flops | bytes accessed | tf_op | source)
XLA Modules:
  0.0 1863.5 jit_solution(1870522413162418681)
XLA Ops:
  7.2 7.7 convert_reduce_fusion.1
  20.3 8.3 dynamic-update-slice
  30.6 235.8 %all-reduce.5.cloned.1.call-done = bf16[3673088]{0:T(1024)(128)(2,1)} async-done(((bf16[3673088]{0:T(1024)(128)(2,1)}), bf16[3673088]{0:T(1024)(128)(2,1)}) %all-reduce.5.cloned.1.call-update) | async-done | bytes 7346192
  266.4 71.1 %reshape.471 = bf16[1,3673088]{1,0:T(2,128)(2,1)} reshape(bf16[3673088]{0:T(1024)(128)(2,1)} %all-reduce.5.cloned.1.call-done) | data formatting | bytes 14692352
  337.4 47.0 %slice_reduce_fusion = (bf16[1048576]{0:T(1024)(128)(2,1)S(1)}, bf16[1048576]{0:T(1024)(128)(2,1)}) fusion(bf16[1,3673088]{1,0:T(2,128)(2,1)} %reshape.471), kind=kLoop, calls=%fused_computation.245 | loop fusion | bytes 8388608 | tf_op jit(solution)/shard_map/slice | solution.py:60
  384.4 28.9 %slice_reduce_fusion.2 = bf16[786432]{0:T(1024)(128)(2,1)} fusion(bf16[1,3673088]{1,0:T(2,128)(2,1)} %reshape.471), kind=kLoop, calls=%fused_computation.247 | loop fusion | bytes 3145728 | tf_op jit(solution)/shard_map/slice | solution.py:60
  413.4 18.5 slice_reduce_fusion.3
  431.9 10.7 slice_reduce_fusion.4
  458.6 925.7 %while.18 = (s32[]{:T(128)}, f32[3673088]{0:T(1024)}, bf16[1536,512]{1,0:T(8,128)(2,1)}, bf16[1536,512]{1,0:T(8,128)(2,1)}, pred[]{:T(512)}, /*index=5*/bf16[153...) while((s32[]{:T(128)}, f32[3673088]{0:T(1024)}, ...), condition=%wide.region_50.51_spmd.clone, body=%wide.region_0.50_spmd.clone.sunk | while | flops 28136960000 | bytes 1194668160 | solution.py:356
  462.4 40.3 %conditional.9 = (bf16[512,512]{0,1:T(8,128)(2,1)}, bf16[512,1024]{1,0:T(8,128)(2,1)}, bf16[512,1536]{1,0:T(8,128)(2,1)}, f32[8,512,1]{1,0,2:T(8,128)S(1)}, bf16...) conditional(s32[]{:T(128)} %convert_element_type.288, ...), branch_computations={%region_1.7_spmd, %region_8.8_spmd} | conditional | flops 4394316800 | bytes 119460040 | solution.py:328
  472.9 6.3 fusion.13
  482.4 12.9 fusion.3
  511.6 10.3 conditional.10
  511.6 5.5 broadcast.552
  526.9 127.6 %collective-permute-done.1 = bf16[512,1024]{1,0:T(8,128)(2,1)} collective-permute-done((bf16[512,1024]{1,0:T(8,128)(2,1)S(1)}, bf16[512,1024]{1,0:T(8,128)(2,1)}, u32[]{:S(2)}, u32[]{:S(2)}) %collective-permute-start.1) | collective-permute-done | bytes 1048608 | tf_op jit(solution)/shard_map/while/body/eval_jaxpr/ppermute | solution.py:27
  654.6 90.7 %conditional.11 = (f32[3673088]{0:T(1024)}, bf16[512,512]{1,0:T(8,128)(2,1)S(1)}) conditional(s32[]{:T(128)} %convert_element_type.288, (pred[512,512]{0,1:T(8,128)(4,1)S(1)}, bf16[512,1536]{1,0:T(8,128)(2,1)}, f32[8,512,1]{1,0,2:T(8,128)}, bf16[512,1024]{1,0:T(8,128)(2,1)}, bf16[512,1024]{1,0:T(8,128)(2,1)}, /*index=5*/f32[6,512]{1,0:T(8,128)S(1)}, ...), branch_computations={%region_35.48_spmd, %region_49.0_spmd} | conditional | flops 8989705216 | bytes 290533952 | solution.py:340
  661.3 13.1 fusion.22
  715.1 5.4 copy.118
  730.8 5.5 copy.119
  745.3 16.3 select_add_fusion.2
  766.8 40.3 %conditional.9 = (bf16[512,512]{0,1:T(8,128)(2,1)}, bf16[512,1024]{1,0:T(8,128)(2,1)}, bf16[512,1536]{1,0:T(8,128)(2,1)}, f32[8,512,1]{1,0,2:T(8,128)S(1)}, bf16...) conditional(s32[]{:T(128)} %convert_element_type.288, ...), branch_computations={%region_1.7_spmd, %region_8.8_spmd} | conditional | flops 4394316800 | bytes 119460040 | solution.py:328
  777.2 6.3 fusion.13
  786.7 13.1 fusion.3
  815.9 10.5 conditional.10
  815.9 5.5 broadcast.552
  831.5 127.4 %collective-permute-done.1 = bf16[512,1024]{1,0:T(8,128)(2,1)} collective-permute-done((bf16[512,1024]{1,0:T(8,128)(2,1)S(1)}, bf16[512,1024]{1,0:T(8,128)(2,1)}, u32[]{:S(2)}, u32[]{:S(2)}) %collective-permute-start.1) | collective-permute-done | bytes 1048608 | tf_op jit(solution)/shard_map/while/body/eval_jaxpr/ppermute | solution.py:27
  958.9 90.9 %conditional.11 = (f32[3673088]{0:T(1024)}, bf16[512,512]{1,0:T(8,128)(2,1)S(1)}) conditional(s32[]{:T(128)} %convert_element_type.288, (pred[512,512]{0,1:T(8,128)(4,1)S(1)}, bf16[512,1536]{1,0:T(8,128)(2,1)}, f32[8,512,1]{1,0,2:T(8,128)}, bf16[512,1024]{1,0:T(8,128)(2,1)}, bf16[512,1024]{1,0:T(8,128)(2,1)}, /*index=5*/f32[6,512]{1,0:T(8,128)S(1)}, ...), branch_computations={%region_35.48_spmd, %region_49.0_spmd} | conditional | flops 8989705216 | bytes 290533952 | solution.py:340
  965.6 12.8 fusion.22
  1019.2 5.4 copy.118
  1029.9 5.0 convolution_bitcast_fusion
  1034.9 5.6 copy.119
  1049.8 20.3 %select_add_fusion.2 = f32[3673088]{0:T(1024)} fusion(f32[3673088]{0:T(1024)} %get-tuple-element.997, f32[3673088]{0:T(1024)} %get-tuple-element.938, f32[3673088]{0:T(1024)} %get-tuple-element.939, pred[]{:T(512)S(6)} %compare.3), kind=kLoop, calls=%fused_computation.235.clone.1 | loop fusion | flops 11019264 | bytes 58769408 | tf_op jit(solution)/shard_map/while/body/eval_jaxpr/add | solution.py:289
  1075.1 40.2 %conditional.9 = (bf16[512,512]{0,1:T(8,128)(2,1)}, bf16[512,1024]{1,0:T(8,128)(2,1)}, bf16[512,1536]{1,0:T(8,128)(2,1)}, f32[8,512,1]{1,0,2:T(8,128)S(1)}, bf16...) conditional(s32[]{:T(128)} %convert_element_type.288, ...), branch_computations={%region_1.7_spmd, %region_8.8_spmd} | conditional | flops 4394316800 | bytes 119460040 | solution.py:328
  1085.6 6.3 fusion.13
  1095.0 12.8 fusion.3
  1124.2 10.3 conditional.10
  1124.2 5.5 broadcast.552
  1139.5 127.6 %collective-permute-done.1 = bf16[512,1024]{1,0:T(8,128)(2,1)} collective-permute-done((bf16[512,1024]{1,0:T(8,128)(2,1)S(1)}, bf16[512,1024]{1,0:T(8,128)(2,1)}, u32[]{:S(2)}, u32[]{:S(2)}) %collective-permute-start.1) | collective-permute-done | bytes 1048608 | tf_op jit(solution)/shard_map/while/body/eval_jaxpr/ppermute | solution.py:27
  1267.1 90.7 %conditional.11 = (f32[3673088]{0:T(1024)}, bf16[512,512]{1,0:T(8,128)(2,1)S(1)}) conditional(s32[]{:T(128)} %convert_element_type.288, (pred[512,512]{0,1:T(8,128)(4,1)S(1)}, bf16[512,1536]{1,0:T(8,128)(2,1)}, f32[8,512,1]{1,0,2:T(8,128)}, bf16[512,1024]{1,0:T(8,128)(2,1)}, bf16[512,1024]{1,0:T(8,128)(2,1)}, /*index=5*/f32[6,512]{1,0:T(8,128)S(1)}, ...), branch_computations={%region_35.48_spmd, %region_49.0_spmd} | conditional | flops 8989705216 | bytes 290533952 | solution.py:340
  1273.8 13.1 fusion.22
  1327.6 5.4 copy.118
  1343.4 5.5 copy.119
  1357.9 20.3 %select_add_fusion.2 = f32[3673088]{0:T(1024)} fusion(f32[3673088]{0:T(1024)} %get-tuple-element.997, f32[3673088]{0:T(1024)} %get-tuple-element.938, f32[3673088]{0:T(1024)} %get-tuple-element.939, pred[]{:T(512)S(6)} %compare.3), kind=kLoop, calls=%fused_computation.235.clone.1 | loop fusion | flops 11019264 | bytes 58769408 | tf_op jit(solution)/shard_map/while/body/eval_jaxpr/add | solution.py:289
  1385.5 10.6 multiply_reduce_fusion.19
  1396.1 396.1 %all-reduce.7.cloned.1.call-done = f32[3673088]{0:T(1024)} async-done(((f32[3673088]{0:T(1024)}), f32[3673088]{0:T(1024)}) %all-reduce.7.cloned.1.call-update) | async-done | bytes 14692368
  1794.2 39.7 %psum.7 = f32[]{:T(128)} all-reduce(f32[]{:T(128)} %get-tuple-element.747), channel_id=1, replica_groups=mesh['section'=2,'batch'=16] {'section','batch'}, use_global_device_ids=true, to_apply=%region_53.54 | all-reduce | flops 1 | bytes 8 | tf_op jit(solution)/shard_map/psum | solution.py:360
  1834.7 5.1 broadcast_in_dim.155
  1840.3 5.1 broadcast_in_dim.152
  (467 shorter events, 352.9 us)
Async XLA Ops:
  7.2 259.2 %all-reduce.5.cloned.1.call-start = ((), (), s32[]{:S(2)}) async-start(), calls=%async_computation | async-start | bytes 14692352
  20.3 8.7 copy-start.75
  28.6 1763.5 %all-reduce.7.cloned.1.call-start = ((), (), s32[]{:S(2)}) async-start(), calls=%async_computation.1 | async-start | bytes 29384704
  450.2 5.6 copy-start.69
  458.8 52.8 %copy-start.13 = (bf16[512,512]{1,0:T(8,128)(2,1)}, bf16[512,512]{1,0:T(8,128)(2,1)S(1)}, u32[]{:S(2)}) copy-start(bf16[512,512]{1,0:T(8,128)(2,1)S(1)} %get-tuple-element.1024) | copy-start | bytes 1572868 | tf_op jit(solution)/shard_map/while
  461.4 50.2 %copy-start.27 = (bf16[512,512]{1,0:T(8,128)(2,1)}, bf16[512,512]{1,0:T(8,128)(2,1)S(1)}, u32[]{:S(2)}) copy-start(bf16[512,512]{1,0:T(8,128)(2,1)S(1)} %constant_dynamic-slice_fusion.4) | copy-start | bytes 1572868 | tf_op jit(solution)/shard_map/while
  482.4 12.9 copy-start.73
  495.2 4.3 copy-start.52
  502.7 8.8 copy-start.6
  502.7 8.8 copy-start.67
  505.4 3.9 collective-permute-start
  521.9 132.7 %copy-start.47 = (bf16[512,512]{1,0:T(8,128)(2,1)}, bf16[512,512]{1,0:T(8,128)(2,1)S(1)}, u32[]{:S(2)}) copy-start(bf16[512,512]{1,0:T(8,128)(2,1)S(1)} %get-tuple-element.942) | copy-start | bytes 1572868 | tf_op jit(solution)/shard_map/while
  523.6 131.0 %collective-permute-start.1 = (bf16[512,1024]{1,0:T(8,128)(2,1)S(1)}, bf16[512,1024]{1,0:T(8,128)(2,1)}, u32[]{:S(2)}, u32[]{:S(2)}) collective-permute-start(bf16[512,1024]{1,0:T(8,128)(2,1)S(1)} %copy.172), channel_id=1, source_target_pairs={{16,0},{17,1},{18,2},{19,3},{20,4},{21,5},{22,6},{23,7},{24,8},{25... | collective-permute-start | bytes 3145736 | tf_op jit(solution)/shard_map/while/body/eval_jaxpr/ppermute | solution.py:27
  660.5 13.8 copy-start.33
  661.3 13.1 copy-start.72
  699.4 3.8 copy-start.8
  745.3 16.3 copy-start.45
  745.3 16.3 copy-start.48
  745.3 17.6 copy-start.14
  763.1 52.8 %copy-start.13 = (bf16[512,512]{1,0:T(8,128)(2,1)}, bf16[512,512]{1,0:T(8,128)(2,1)S(1)}, u32[]{:S(2)}) copy-start(bf16[512,512]{1,0:T(8,128)(2,1)S(1)} %get-tuple-element.1024) | copy-start | bytes 1572868 | tf_op jit(solution)/shard_map/while
  765.7 50.2 %copy-start.27 = (bf16[512,512]{1,0:T(8,128)(2,1)}, bf16[512,512]{1,0:T(8,128)(2,1)S(1)}, u32[]{:S(2)}) copy-start(bf16[512,512]{1,0:T(8,128)(2,1)S(1)} %constant_dynamic-slice_fusion.4) | copy-start | bytes 1572868 | tf_op jit(solution)/shard_map/while
  786.7 13.1 copy-start.73
  799.9 4.3 copy-start.52
  807.1 8.8 copy-start.6
  807.1 8.8 copy-start.67
  809.8 3.9 collective-permute-start
  826.4 132.4 %copy-start.47 = (bf16[512,512]{1,0:T(8,128)(2,1)}, bf16[512,512]{1,0:T(8,128)(2,1)S(1)}, u32[]{:S(2)}) copy-start(bf16[512,512]{1,0:T(8,128)(2,1)S(1)} %get-tuple-element.942) | copy-start | bytes 1572868 | tf_op jit(solution)/shard_map/while
  828.1 130.7 %collective-permute-start.1 = (bf16[512,1024]{1,0:T(8,128)(2,1)S(1)}, bf16[512,1024]{1,0:T(8,128)(2,1)}, u32[]{:S(2)}, u32[]{:S(2)}) collective-permute-start(bf16[512,1024]{1,0:T(8,128)(2,1)S(1)} %copy.172), channel_id=1, source_target_pairs={{16,0},{17,1},{18,2},{19,3},{20,4},{21,5},{22,6},{23,7},{24,8},{25... | collective-permute-start | bytes 3145736 | tf_op jit(solution)/shard_map/while/body/eval_jaxpr/ppermute | solution.py:27
  964.8 13.6 copy-start.33
  965.6 12.8 copy-start.72
  1003.5 3.8 copy-start.8
  1049.7 20.3 %copy-start.45 = (bf16[512,512]{1,0:T(8,128)(2,1)S(1)}, bf16[512,512]{1,0:T(8,128)(2,1)}, u32[]{:S(2)}) copy-start(bf16[512,512]{1,0:T(8,128)(2,1)} %copy.173) | copy-start | bytes 1572868 | tf_op jit(solution)/shard_map/while
  1049.7 20.3 %copy-start.48 = (bf16[512,512]{1,0:T(8,128)(2,1)S(1)}, bf16[512,512]{1,0:T(8,128)(2,1)}, u32[]{:S(2)}) copy-start(bf16[512,512]{1,0:T(8,128)(2,1)} %copy-done.47) | copy-start | bytes 1572868 | tf_op jit(solution)/shard_map/while
  1049.7 21.5 %copy-start.14 = (bf16[512,512]{1,0:T(8,128)(2,1)S(1)}, bf16[512,512]{1,0:T(8,128)(2,1)}, u32[]{:S(2)}) copy-start(bf16[512,512]{1,0:T(8,128)(2,1)} %copy-done.13) | copy-start | bytes 1572868 | tf_op jit(solution)/shard_map/while
  1071.4 52.7 %copy-start.13 = (bf16[512,512]{1,0:T(8,128)(2,1)}, bf16[512,512]{1,0:T(8,128)(2,1)S(1)}, u32[]{:S(2)}) copy-start(bf16[512,512]{1,0:T(8,128)(2,1)S(1)} %get-tuple-element.1024) | copy-start | bytes 1572868 | tf_op jit(solution)/shard_map/while
  1074.1 50.1 %copy-start.27 = (bf16[512,512]{1,0:T(8,128)(2,1)}, bf16[512,512]{1,0:T(8,128)(2,1)S(1)}, u32[]{:S(2)}) copy-start(bf16[512,512]{1,0:T(8,128)(2,1)S(1)} %constant_dynamic-slice_fusion.4) | copy-start | bytes 1572868 | tf_op jit(solution)/shard_map/while
  1095.0 12.8 copy-start.73
  1107.9 4.3 copy-start.52
  1115.3 8.8 copy-start.6
  1115.3 8.8 copy-start.67
  1118.0 3.9 collective-permute-start
  1134.5 132.7 %copy-start.47 = (bf16[512,512]{1,0:T(8,128)(2,1)}, bf16[512,512]{1,0:T(8,128)(2,1)S(1)}, u32[]{:S(2)}) copy-start(bf16[512,512]{1,0:T(8,128)(2,1)S(1)} %get-tuple-element.942) | copy-start | bytes 1572868 | tf_op jit(solution)/shard_map/while
  1136.2 131.0 %collective-permute-start.1 = (bf16[512,1024]{1,0:T(8,128)(2,1)S(1)}, bf16[512,1024]{1,0:T(8,128)(2,1)}, u32[]{:S(2)}, u32[]{:S(2)}) collective-permute-start(bf16[512,1024]{1,0:T(8,128)(2,1)S(1)} %copy.172), channel_id=1, source_target_pairs={{16,0},{17,1},{18,2},{19,3},{20,4},{21,5},{22,6},{23,7},{24,8},{25... | collective-permute-start | bytes 3145736 | tf_op jit(solution)/shard_map/while/body/eval_jaxpr/ppermute | solution.py:27
  1273.1 13.8 copy-start.33
  1273.8 13.1 copy-start.72
  1357.8 20.3 %copy-start.45 = (bf16[512,512]{1,0:T(8,128)(2,1)S(1)}, bf16[512,512]{1,0:T(8,128)(2,1)}, u32[]{:S(2)}) copy-start(bf16[512,512]{1,0:T(8,128)(2,1)} %copy.173) | copy-start | bytes 1572868 | tf_op jit(solution)/shard_map/while
  1357.8 20.3 %copy-start.48 = (bf16[512,512]{1,0:T(8,128)(2,1)S(1)}, bf16[512,512]{1,0:T(8,128)(2,1)}, u32[]{:S(2)}) copy-start(bf16[512,512]{1,0:T(8,128)(2,1)} %copy-done.47) | copy-start | bytes 1572868 | tf_op jit(solution)/shard_map/while
  1357.9 21.5 %copy-start.14 = (bf16[512,512]{1,0:T(8,128)(2,1)S(1)}, bf16[512,512]{1,0:T(8,128)(2,1)}, u32[]{:S(2)}) copy-start(bf16[512,512]{1,0:T(8,128)(2,1)} %copy-done.13) | copy-start | bytes 1572868 | tf_op jit(solution)/shard_map/while
  (50 other events, 123.6 us)
Sparse Core Ops, SparseCore 0:
  28.7 237.5 all-reduce.4
  1384.4 407.6 all-reduce.6
where the time goes:
time: 1870 us; the launch traced here: 1860 us
  waiting for transfers between devices  1010 us (54%)
  local copies, waits for them, and re-layouts  413 us (22%)
  matrix products  229 us (12%)
  other arithmetic  120 us (6%)
  blocking collectives  39.7 us (2%)
    unnamed x4, waiting for transfers between devices  632 us
    ppermute x6, waiting for transfers between devices, passed_along(): lax.ppermute(value, axis, [(source, source + steps) for source in range(f...  383 us
    slice x7, local copies, waits for them, and re-layouts, unpack(): flat_vec[offset:offset + rows_n * cols_n].reshape(rows_n, cols_n)  109 us
    unnamed x11, local copies, waits for them, and re-layouts  86.2 us
    dot_general x15, matrix products, dot_plain(): return jnp.dot(lhs_mat, rhs_mat, preferred_element_type=jnp.float32)  72 us
    cond x153, local copies, waits for them, and re-layouts  64 us
    dot_general x15, matrix products, dot_right(): lax.dot_general(lhs_mat, rhs_mat, (((1,), (1,)), ((), ())), preferred_ele...  59.5 us
    add x3, other arithmetic, add_grad(): return grad_total + step_grad  56.8 us
  transfers between devices with their start and end apart: 8, of which 8 were waited for; matrix products, arithmetic and copies ran while one was open for 1% of the time, Pallas kernels for 0%

commit v1 on v0

v1 whole, which is shorter than its diff:
```python
import functools

import jax
import jax.numpy as jnp
from jax import lax
from jax.experimental import pallas as pl
from jax.experimental.pallas import tpu as pltpu
from jax.sharding import PartitionSpec as P

D = 512
FF = 2048
HEADS = 8
HD = 64
ROW = 512
STEP = 1000
WARMUP = 4000

BIG = 1e30
LN_EPS = 1e-05
BETA_ONE = 0.9
BETA_TWO = 0.98
ADAM_EPS = 1e-09
MAXNORM = 0.1

F32 = jnp.float32
BF = jnp.bfloat16
TILE = 16 * 128
CHUNK = 512
SEG_BITS = 12
POS_BITS = 9

MATS = {}
_at = 0
for _name, _rows, _cols in (("qkv", D, 3 * D), ("out", D, D), ("cross", D, 2 * D), ("up", D, FF), ("down", FF, D)):
    _width = _cols // 128
    MATS[_name] = (_rows, _cols, _at, {12: 16, 4: 64, 8: 32, 16: 16}[_width])
    _at += _rows * _width
VEC_AT = _at
FLAT_ROWS = _at + 24


def dot_nn(lhs, rhs):
    return jnp.dot(lhs, rhs, preferred_element_type=F32)


def dot_nt(lhs, rhs):
    return lax.dot_general(lhs, rhs, (((1,), (1,)), ((), ())), preferred_element_type=F32)


def dot_tn(lhs, rhs):
    return lax.dot_general(lhs, rhs, (((0,), (0,)), ((), ())), preferred_element_type=F32)


def params_of(mib):
    return pltpu.CompilerParams(vmem_limit_bytes=mib * 2**20)


def row_spec(rows, cols):
    return pl.BlockSpec((rows, cols), lambda i: (i, 0))


def whole_spec(shape):
    return pl.BlockSpec(shape, lambda i: (0,) * len(shape), pipeline_mode=pl.Buffered(1))


def shape_of(shape, dtype):
    return jax.ShapeDtypeStruct(shape, dtype)


def ln_parts(resid):
    center = resid - jnp.mean(resid, axis=-1, keepdims=True)
    rstd = lax.rsqrt(jnp.mean(center * center, axis=-1, keepdims=True) + LN_EPS)
    return center * rstd, rstd


def ln_back(grad, hat, rstd, gain):
    scaled = grad * gain
    first = jnp.mean(scaled, axis=-1, keepdims=True)
    second = jnp.mean(scaled * hat, axis=-1, keepdims=True)
    grad_resid = rstd * (scaled - first - hat * second)
    return grad_resid, jnp.sum(grad * hat, axis=0, keepdims=True), jnp.sum(grad, axis=0, keepdims=True)


def gelu_both(pre):
    size = jnp.abs(pre)
    near = 1.0 / (1.0 + (0.3275911 * 0.7071067811865476) * size)
    bell = jnp.exp(-0.5 * pre * pre)
    poly = near * (0.127414796 + near * (-0.142248368 + near * (0.7107068705 + near * (-0.7265760135 + near * 0.5307027145))))
    tail = poly * bell
    phi = jnp.where(pre >= 0.0, 1.0 - tail, tail)
    return pre * phi, phi + pre * bell * 0.3989422804014327


def low_lanes(rows):
    return lax.broadcasted_iota(jnp.int32, (rows, 128), 1) < HD


def triangle(keys_first):
    row = lax.broadcasted_iota(jnp.int32, (256, 256), 0)
    col = lax.broadcasted_iota(jnp.int32, (256, 256), 1)
    keep = (row <= col) if keys_first else (col <= row)
    return jnp.where(keep, 0.0, -BIG).astype(F32)


def attend_fwd(causal, q_ref, q_at, k_ref, k_at, v_ref, v_at, fq, fk, ctx_ref, lse_ref):
    low = low_lanes(ROW)
    lane = lax.broadcasted_iota(jnp.int32, (ROW, 128), 1)
    one = jnp.asarray(1.0, BF)
    tri = triangle(False) if causal else None
    lse_all = jnp.zeros((ROW, 128), F32)
    for pair in range(HEADS // 2):
        q_pair = q_ref[:, q_at + 128 * pair : q_at + 128 * pair + 128] * jnp.asarray(HD**-0.5, BF)
        k_pair = k_ref[:, k_at + 128 * pair : k_at + 128 * pair + 128]
        v_pair = v_ref[:, v_at + 128 * pair : v_at + 128 * pair + 128]
        halves = []
        for e in range(2):
            sel = low if e == 0 else ~low
            qa = jnp.where(sel, q_pair, fq)
            ka = jnp.where(sel, k_pair, fk)
            va = jnp.where(sel, v_pair, one)
            outs, tops = [], []
            for half in range(2):
                keys = 256 * (half + 1) if causal else ROW
                s = dot_nt(qa[256 * half : 256 * half + 256], ka[:keys])
                if causal:
                    s = s + tri if half == 0 else jnp.concatenate([s[:, :256], s[:, 256:] + tri], axis=1)
                top = jnp.max(s, axis=1, keepdims=True)
                p = jnp.exp(s - top)
                outs.append(dot_nn(p.astype(BF), va[:keys]))
                tops.append(top)
            o = jnp.concatenate(outs, axis=0)
            total = pltpu.roll(o, 64, 1)
            halves.append(o / total)
            lse = jnp.concatenate(tops, axis=0) + jnp.log(jnp.where(sel, total, o))
            lse_all = jnp.where(lane == 2 * pair + e, lse, lse_all)
        ctx_ref[:, 128 * pair : 128 * pair + 128] = jnp.where(low, halves[0], halves[1]).astype(BF)
    lse_ref[...] = lse_all.T[0:HEADS, :]


def attend_bwd(causal, q_ref, q_at, k_ref, k_at, v_ref, v_at, fq, fk, lse_ref, do_ref, outs, dqt_ref):
    low = low_lanes(ROW)
    zero = jnp.zeros((ROW, 128), BF)
    scale = jnp.asarray(HD**-0.5, BF)
    tri = triangle(True) if causal else None
    k_t = k_ref[:, k_at : k_at + D].T
    for pair in range(HEADS // 2):
        q_pair = q_ref[:, q_at + 128 * pair : q_at + 128 * pair + 128] * scale
        k_pair = k_ref[:, k_at + 128 * pair : k_at + 128 * pair + 128]
        v_pair = v_ref[:, v_at + 128 * pair : v_at + 128 * pair + 128]
        do_pair = do_ref[:, 128 * pair : 128 * pair + 128]
        dks, dvs = [], []
        for e in range(2):
            head = 2 * pair + e
            sel = low if e == 0 else ~low
            qa = jnp.where(sel, q_pair, fq)
            ka = jnp.where(sel, k_pair, fk)
            va = jnp.where(sel, v_pair, zero)
            probs, prods = [], []
            for half in range(2):
                first = 256 * half if causal else 0
                keys = slice(256 * half, 256 * half + 256)
                s = dot_nt(ka[keys], qa[first:])
                if causal:
                    s = s + tri if half == 1 else jnp.concatenate([s[:, :256] + tri, s[:, 256:]], axis=1)
                p = jnp.exp(s - lse_ref[head : head + 1, first:])
                probs.append(p)
                prods.append(p * dot_nt(va[keys], do_pair[first:]))
            if causal:
                top = jnp.sum(prods[0], axis=0, keepdims=True)
                rest = top[:, 256:] + jnp.sum(prods[1], axis=0, keepdims=True)
                deltas = [jnp.concatenate([top[:, :256], rest], axis=1), rest]
            else:
                delta = jnp.sum(prods[0], axis=0, keepdims=True) + jnp.sum(prods[1], axis=0, keepdims=True)
                deltas = [delta, delta]
            ds = [(prods[i] - probs[i] * deltas[i]).astype(BF) for i in range(2)]
            firsts = (0, 256) if causal else (0, 0)
            dvs.append(jnp.concatenate([dot_nn(probs[i].astype(BF), do_pair[firsts[i] :]) for i in range(2)], axis=0))
            dks.append(jnp.concatenate([dot_nn(ds[i], q_pair[firsts[i] :]) for i in range(2)], axis=0))
            k_head = k_t[HD * head : HD * head + HD]
            if causal:
                dqt_ref[HD * head : HD * head + HD, :256] = dot_nn(k_head[:, :256], ds[0][:, :256])
                dqt_ref[HD * head : HD * head + HD, 256:] = dot_nn(k_head, jnp.concatenate([ds[0][:, 256:], ds[1]], axis=0))
            else:
                dqt_ref[HD * head : HD * head + HD, :] = dot_nn(k_head, jnp.concatenate(ds, axis=0))
        for (ref, at), parts in ((outs[1], dks), (outs[2], dvs)):
            ref[:, at + 128 * pair : at + 128 * pair + 128] = jnp.where(low, parts[0], parts[1]).astype(BF)
    ref, at = outs[0]
    ref[:, at : at + D] = (dqt_ref[...] * HD**-0.5).T.astype(BF)


def group_perm(name, to_flat):
    _, cols, _, group = MATS[name]
    width = cols // 128
    size = group * width
    row = lax.broadcasted_iota(jnp.int32, (size, size), 0)
    col = lax.broadcasted_iota(jnp.int32, (size, size), 1)
    blocked, flat = (col, row) if to_flat else (row, col)
    source = width * (blocked & (group - 1)) + lax.shift_right_logical(blocked, group.bit_length() - 1)
    return jnp.where(source == flat, 1.0, 0.0).astype(BF)


def to_matrix(name, flat_ref, at, mat_ref):
    rows, cols, _, group = MATS[name]
    width = cols // 128
    size = group * width
    perm = group_perm(name, False)
    for g in range(rows // group):
        got = dot_nn(perm, flat_ref[at + g * size : at + (g + 1) * size, :]).astype(BF)
        for c in range(width):
            mat_ref[g * group : (g + 1) * group, 128 * c : 128 * c + 128] = got[c * group : (c + 1) * group]


def to_flat(name, mat_ref, flat_ref, at):
    rows, cols, _, group = MATS[name]
    width = cols // 128
    size = group * width
    perm = group_perm(name, True)
    for g in range(rows // group):
        blocked = jnp.concatenate(
            [mat_ref[g * group : (g + 1) * group, 128 * c : 128 * c + 128].astype(BF) for c in range(width)], axis=0
        )
        flat_ref[at + g * size : at + (g + 1) * size, :] = dot_nn(perm, blocked).astype(BF)


def ffn_fwd(hidden_b, w_up, w_down, act_ref, slope_ref):
    total = None
    for c in range(FF // CHUNK):
        cols = slice(c * CHUNK, (c + 1) * CHUNK)
        act, slope = gelu_both(dot_nn(hidden_b, w_up[:, cols]))
        act_b = act.astype(BF)
        act_ref[:, cols] = act_b
        slope_ref[:, cols] = slope.astype(slope_ref.dtype)
        part = dot_nn(act_b, w_down[cols, :])
        total = part if total is None else total + part
    return total


def ffn_bwd(hidden_b, branch_b, w_up, w_down, act_ref, slope_ref, g_up, g_down):
    total = None
    hidden_t = hidden_b.T
    for c in range(FF // CHUNK):
        cols = slice(c * CHUNK, (c + 1) * CHUNK)
        grad_act = dot_nt(branch_b, w_down[cols, :])
        grad_pre = (grad_act * slope_ref[:, cols].astype(F32)).astype(BF)
        g_down[cols, :] += dot_tn(act_ref[:, cols], branch_b)
        g_up[:, cols] += dot_nn(hidden_t, grad_pre)
        part = dot_nt(grad_pre, w_up[:, cols])
        total = part if total is None else total + part
    return total


def weights_kernel(n, share, flat_in, *refs):
    outs, flat = refs[:6], refs[6]
    for b in range(n):
        tile = share * b // TILE
        last = -(-share * (b + 1) // TILE)
        start, count = 16 * tile, 16 * (last - tile)
        if (share * b) % TILE:
            flat[start : start + 16, :] += flat_in[b, 0:16, :]
        else:
            flat[start : start + 16, :] = flat_in[b, 0:16, :]
        flat[start + 16 : start + count, :] = flat_in[b, 16:count, :]
    for name, ref in zip(MATS, outs):
        to_matrix(name, flat, MATS[name][2], ref)
    outs[5][...] = flat[VEC_AT : VEC_AT + 32, :]


def self_fwd_kernel(causal, x_ref, wqkv, wout, fq, fk, qkv_ref, ctx_ref, lse_ref, r1_ref):
    x = x_ref[...]
    qkv_ref[...] = dot_nn(x, wqkv[...]).astype(BF)
    attend_fwd(causal, qkv_ref, 0, qkv_ref, D, qkv_ref, 2 * D, fq[...], fk[...], ctx_ref, lse_ref)
    r1_ref[...] = x.astype(F32) + dot_nn(ctx_ref[...], wout[...])


def enc_ffn_kernel(r1_ref, vec, w_up, w_down, w_cross, mem_ref, kv_ref, act_ref, slope_ref, r2_ref):
    hat, _ = ln_parts(r1_ref[...])
    y1 = hat * vec[0:1, :] + vec[1:2, :]
    r2 = y1 + ffn_fwd(y1.astype(BF), w_up, w_down, act_ref, slope_ref)
    r2_ref[...] = r2
    hat, _ = ln_parts(r2)
    mem = (hat * vec[2:3, :] + vec[3:4, :]).astype(BF)
    mem_ref[...] = mem
    kv_ref[...] = dot_nn(mem, w_cross[...]).astype(BF)


def dec_kernel(
    r1_ref, kv_ref, go_ref, vec, w_cross, w_up, w_down, fq, fk,
    out_ref, gkv_ref, dy1_ref, fl_cross, fl_up, fl_down, gvec,
    cq_s, ctx_s, lse_s, dctx_s, dcq_s, dqt_s, act_s, slope_s, g_cross, g_up, g_down,
):
    step = pl.program_id(0)

    @pl.when(step == 0)
    def _():
        g_cross[...] = jnp.zeros_like(g_cross)
        g_up[...] = jnp.zeros_like(g_up)
        g_down[...] = jnp.zeros_like(g_down)
        gvec[...] = jnp.zeros_like(gvec)

    hat1, _ = ln_parts(r1_ref[...])
    y1 = hat1 * vec[0:1, :] + vec[1:2, :]
    y1_b = y1.astype(BF)
    cq_s[...] = dot_nn(y1_b, w_cross[:, :D]).astype(BF)
    attend_fwd(False, cq_s, 0, kv_ref, 0, kv_ref, D, fq[...], fk[...], ctx_s, lse_s)
    r2 = y1 + dot_nn(ctx_s[...], w_cross[:, D:])
    hat2, rstd2 = ln_parts(r2)
    y2 = hat2 * vec[2:3, :] + vec[3:4, :]
    y2_b = y2.astype(BF)
    r3 = y2 + ffn_fwd(y2_b, w_up, w_down, act_s, slope_s)
    hat3, rstd3 = ln_parts(r3)
    out_ref[...] = (hat3 * vec[4:5, :] + vec[5:6, :]).astype(BF)

    dr3, gain3, shift3 = ln_back(go_ref[...].astype(F32), hat3, rstd3, vec[4:5, :])
    dy2 = dr3 + ffn_bwd(y2_b, dr3.astype(BF), w_up, w_down, act_s, slope_s, g_up, g_down)
    dr2, gain2, shift2 = ln_back(dy2, hat2, rstd2, vec[2:3, :])
    dr2_b = dr2.astype(BF)
    g_cross[:, D:] += dot_tn(ctx_s[...], dr2_b)
    dctx_s[...] = dot_nt(dr2_b, w_cross[:, D:]).astype(BF)
    attend_bwd(
        False, cq_s, 0, kv_ref, 0, kv_ref, D, fq[...], fk[...], lse_s, dctx_s,
        ((dcq_s, 0), (gkv_ref, 0), (gkv_ref, D)), dqt_s,
    )
    dcq = dcq_s[...]
    g_cross[:, :D] += dot_tn(y1_b, dcq)
    dy1_ref[...] = dr2 + dot_nt(dcq, w_cross[:, :D])
    gvec[2:3, :] += gain2
    gvec[3:4, :] += shift2
    gvec[4:5, :] += gain3
    gvec[5:6, :] += shift3

    @pl.when(step == pl.num_programs(0) - 1)
    def _():
        to_flat("cross", g_cross, fl_cross, 0)
        to_flat("up", g_up, fl_up, 0)
        to_flat("down", g_down, fl_down, 0)


def enc_back_kernel(
    gkv_ref, mem_ref, r1_ref, r2_ref, act_ref, slope_ref, vec, w_cross, w_up, w_down,
    dy1_ref, fl_cross, fl_up, fl_down, gvec, g_cross, g_up, g_down,
):
    step = pl.program_id(0)

    @pl.when(step == 0)
    def _():
        g_cross[...] = jnp.zeros_like(g_cross)
        g_up[...] = jnp.zeros_like(g_up)
        g_down[...] = jnp.zeros_like(g_down)
        gvec[...] = jnp.zeros_like(gvec)

    gkv = gkv_ref[...]
    g_cross[...] += dot_tn(mem_ref[...], gkv)
    dmem = dot_nt(gkv, w_cross[...])
    hat2, rstd2 = ln_parts(r2_ref[...])
    dr2, gain2, shift2 = ln_back(dmem, hat2, rstd2, vec[2:3, :])
    hat1, _ = ln_parts(r1_ref[...])
    y1_b = (hat1 * vec[0:1, :] + vec[1:2, :]).astype(BF)
    dy1_ref[...] = dr2 + ffn_bwd(y1_b, dr2.astype(BF), w_up, w_down, act_ref, slope_ref, g_up, g_down)
    gvec[2:3, :] += gain2
    gvec[3:4, :] += shift2

    @pl.when(step == pl.num_programs(0) - 1)
    def _():
        to_flat("cross", g_cross, fl_cross, 0)
        to_flat("up", g_up, fl_up, 0)
        to_flat("down", g_down, fl_down, 0)


def self_back_kernel(
    causal, x_ref, r1_ref, dy1_ref, qkv_ref, ctx_ref, lse_ref, vec, wqkv, wout, fq, fk,
    dx_ref, fl_qkv, fl_out, gvec, dctx_s, dqkv_s, dqt_s, g_qkv, g_out,
):
    step = pl.program_id(0)

    @pl.when(step == 0)
    def _():
        g_qkv[...] = jnp.zeros_like(g_qkv)
        g_out[...] = jnp.zeros_like(g_out)
        gvec[...] = jnp.zeros_like(gvec)

    hat1, rstd1 = ln_parts(r1_ref[...])
    dr1, gain1, shift1 = ln_back(dy1_ref[...], hat1, rstd1, vec[0:1, :])
    dr1_b = dr1.astype(BF)
    g_out[...] += dot_tn(ctx_ref[...], dr1_b)
    dctx_s[...] = dot_nt(dr1_b, wout[...]).astype(BF)
    attend_bwd(
        causal, qkv_ref, 0, qkv_ref, D, qkv_ref, 2 * D, fq[...], fk[...], lse_ref, dctx_s,
        ((dqkv_s, 0), (dqkv_s, D), (dqkv_s, 2 * D)), dqt_s,
    )
    dqkv = dqkv_s[...]
    g_qkv[...] += dot_tn(x_ref[...], dqkv)
    dx_ref[...] = (dr1 + dot_nt(dqkv, wqkv[...])).astype(BF)
    gvec[0:1, :] += gain1
    gvec[1:2, :] += shift1

    @pl.when(step == pl.num_programs(0) - 1)
    def _():
        to_flat("qkv", g_qkv, fl_qkv, 0)
        to_flat("out", g_out, fl_out, 0)


def kernel_call(body, **options):
    call = pl.pallas_call(body, **options)
    return lambda *operands: tuple(call(*operands))


def split_weights(pieces, n, share):
    shapes = [(rows, cols) for rows, cols, _, _ in MATS.values()] + [(32, 128)]
    rows = 16 * (-(-share * n // TILE) + 2)
    return kernel_call(
        functools.partial(weights_kernel, n, share),
        in_specs=[pl.BlockSpec(memory_space=pltpu.VMEM)],
        out_specs=[pl.BlockSpec(memory_space=pltpu.VMEM)] * 6,
        out_shape=[shape_of(s, BF) for s in shapes],
        scratch_shapes=[pltpu.VMEM((rows, 128), BF)],
        compiler_params=params_of(48),
    )(pieces)


def self_fwd(causal, x, w, fq, fk):
    t = x.shape[0]
    return kernel_call(
        functools.partial(self_fwd_kernel, causal),
        grid=(t // ROW,),
        in_specs=[
            row_spec(ROW, D), whole_spec((D, 3 * D)), whole_spec((D, D)), row_spec(ROW, 128), row_spec(ROW, 128),
        ],
        out_specs=[row_spec(ROW, 3 * D), row_spec(ROW, D), row_spec(HEADS, ROW), row_spec(ROW, D)],
        out_shape=[
            shape_of((t, 3 * D), BF), shape_of((t, D), BF), shape_of((t // ROW * HEADS, ROW), F32), shape_of((t, D), F32),
        ],
        compiler_params=params_of(48),
    )(x, w["qkv"], w["out"], fq, fk)


def enc_ffn(r1, w, vec):
    t = r1.shape[0]
    return kernel_call(
        enc_ffn_kernel,
        grid=(t // ROW,),
        in_specs=[
            row_spec(ROW, D), whole_spec((6, D)), whole_spec((D, FF)), whole_spec((FF, D)), whole_spec((D, 2 * D)),
        ],
        out_specs=[row_spec(ROW, D), row_spec(ROW, 2 * D), row_spec(ROW, FF), row_spec(ROW, FF), row_spec(ROW, D)],
        out_shape=[
            shape_of((t, D), BF), shape_of((t, 2 * D), BF), shape_of((t, FF), BF), shape_of((t, FF), BF),
            shape_of((t, D), F32),
        ],
        compiler_params=params_of(48),
    )(r1, vec, w["up"], w["down"], w["cross"])


FLAT_FFN = [shape_of((4096, 128), BF), shape_of((8192, 128), BF), shape_of((8192, 128), BF)]


def dec_call(r1, kv, go, w, vec, fq, fk):
    t = r1.shape[0]
    vm = pltpu.VMEM
    return kernel_call(
        dec_kernel,
        grid=(t // ROW,),
        in_specs=[
            row_spec(ROW, D), row_spec(ROW, 2 * D), row_spec(ROW, D), whole_spec((6, D)), whole_spec((D, 2 * D)),
            whole_spec((D, FF)), whole_spec((FF, D)), row_spec(ROW, 128), row_spec(ROW, 128),
        ],
        out_specs=[
            row_spec(ROW, D), row_spec(ROW, 2 * D), row_spec(ROW, D),
            whole_spec((4096, 128)), whole_spec((8192, 128)), whole_spec((8192, 128)), whole_spec((8, D)),
        ],
        out_shape=[shape_of((t, D), BF), shape_of((t, 2 * D), BF), shape_of((t, D), F32)] + FLAT_FFN + [shape_of((8, D), F32)],
        scratch_shapes=[
            vm((ROW, D), BF), vm((ROW, D), BF), vm((HEADS, ROW), F32), vm((ROW, D), BF), vm((ROW, D), BF),
            vm((D, ROW), F32), vm((ROW, FF), BF), vm((ROW, FF), BF), vm((D, 2 * D), F32), vm((D, FF), F32), vm((FF, D), F32),
        ],
        compiler_params=params_of(60),
    )(r1, kv, go, vec, w["cross"], w["up"], w["down"], fq, fk)


def enc_back(gkv, mem, r1, r2, act, slope, w, vec):
    t = r1.shape[0]
    vm = pltpu.VMEM
    return kernel_call(
        enc_back_kernel,
        grid=(t // ROW,),
        in_specs=[
            row_spec(ROW, 2 * D), row_spec(ROW, D), row_spec(ROW, D), row_spec(ROW, D), row_spec(ROW, FF), row_spec(ROW, FF),
            whole_spec((6, D)), whole_spec((D, 2 * D)), whole_spec((D, FF)), whole_spec((FF, D)),
        ],
        out_specs=[
            row_spec(ROW, D), whole_spec((4096, 128)), whole_spec((8192, 128)), whole_spec((8192, 128)), whole_spec((8, D)),
        ],
        out_shape=[shape_of((t, D), F32)] + FLAT_FFN + [shape_of((8, D), F32)],
        scratch_shapes=[vm((D, 2 * D), F32), vm((D, FF), F32), vm((FF, D), F32)],
        compiler_params=params_of(60),
    )(gkv, mem, r1, r2, act, slope, vec, w["cross"], w["up"], w["down"])


def self_back(causal, x, r1, dy1, qkv, ctx, lse, w, vec, fq, fk):
    t = r1.shape[0]
    vm = pltpu.VMEM
    return kernel_call(
        functools.partial(self_back_kernel, causal),
        grid=(t // ROW,),
        in_specs=[
            row_spec(ROW, D), row_spec(ROW, D), row_spec(ROW, D), row_spec(ROW, 3 * D), row_spec(ROW, D), row_spec(HEADS, ROW),
            whole_spec((6, D)), whole_spec((D, 3 * D)), whole_spec((D, D)), row_spec(ROW, 128), row_spec(ROW, 128),
        ],
        out_specs=[row_spec(ROW, D), whole_spec((6144, 128)), whole_spec((2048, 128)), whole_spec((8, D))],
        out_shape=[
            shape_of((t, D), BF), shape_of((6144, 128), BF), shape_of((2048, 128), BF), shape_of((8, D), F32),
        ],
        scratch_shapes=[vm((ROW, D), BF), vm((ROW, 3 * D), BF), vm((D, ROW), F32), vm((D, 3 * D), F32), vm((D, D), F32)],
        compiler_params=params_of(60),
    )(x, r1, dy1, qkv, ctx, lse, vec, w["qkv"], w["out"], fq, fk)


def blanks(*shapes):
    return tuple(jnp.zeros(shape, dtype) for shape, dtype in shapes)


def mask_features(segments, live):
    t = segments.shape[0]
    lane = (jnp.arange(128, dtype=jnp.int32) % HD)[None, :]
    pair = lane // 2
    odd = lane % 2 == 1
    is_seg = pair < SEG_BITS
    is_pos = (pair >= SEG_BITS) & (pair < SEG_BITS + POS_BITS)
    place = (jnp.arange(t, dtype=jnp.int32) % ROW)[:, None]
    bit = jnp.where(
        is_seg,
        (segments[:, None] >> jnp.minimum(pair, SEG_BITS)) & 1,
        (place >> jnp.clip(pair - SEG_BITS, 0, POS_BITS)) & 1,
    )
    query = jnp.where(odd, 1 - bit, bit) * (is_seg | is_pos)
    key = jnp.where(odd, bit, 1 - bit)
    keys = [jnp.where(is_seg | (is_pos & (live[i][:, None] != 1)), key.astype(F32) * -BIG, 0.0).astype(BF) for i in range(2)]
    return query.astype(BF), keys[0], keys[1]


def passed_along(value, axis, steps):
    count = lax.axis_size(axis)
    first, last = (max(0, -steps), min(count, count - steps))
    return lax.ppermute(value, axis, [(source, source + steps) for source in range(first, last)])


def shards(params, first_moment, second_moment, inputs, segments, live_mask, out_grad):
    is_decoder = lax.axis_index("section") == 1
    me = lax.axis_index("batch")
    n = lax.axis_size("batch")
    share = params.shape[1]
    rows = 16 * (share // TILE + 2)
    shift = lax.rem(me * (share % TILE), TILE)
    x = inputs[0]
    t = x.shape[0]

    own = lax.dynamic_update_slice(jnp.zeros((rows * 128,), F32), params[0], (shift,)).reshape(rows, 128).astype(BF)
    pieces = lax.all_gather(own, "batch", axis=0, tiled=False)
    fq, fk_src, fk_tgt = mask_features(segments, live_mask)
    fk_self = jnp.where(is_decoder, fk_tgt, fk_src)
    *mats, vec_rows = split_weights(pieces, n, share)
    w = dict(zip(MATS, mats))
    vec = vec_rows[:24].astype(F32).reshape(6, D)

    qkv, ctx, lse, r1 = lax.cond(
        is_decoder,
        lambda: self_fwd(True, x, w, fq, fk_self),
        lambda: self_fwd(False, x, w, fq, fk_self),
    )
    mem, kv, act, slope, r2 = lax.cond(
        is_decoder,
        lambda: blanks(((t, D), BF), ((t, 2 * D), BF), ((t, FF), BF), ((t, FF), BF), ((t, D), F32)),
        lambda: enc_ffn(r1, w, vec),
    )
    kv_in = passed_along(kv, "section", 1)
    out, gkv, dy1_d, *rest_d = lax.cond(
        is_decoder,
        lambda: dec_call(r1, kv_in, out_grad, w, vec, fq, fk_src),
        lambda: blanks(
            ((t, D), BF), ((t, 2 * D), BF), ((t, D), F32), *((s.shape, s.dtype) for s in FLAT_FFN), ((8, D), F32)
        ),
    )
    gkv_in = passed_along(gkv, "section", -1)
    dy1, fl_cross, fl_up, fl_down, gvec_a = lax.cond(
        is_decoder,
        lambda: (dy1_d, *rest_d),
        lambda: enc_back(gkv_in, mem, r1, r2, act, slope, w, vec),
    )
    dx, fl_qkv, fl_out, gvec_b = lax.cond(
        is_decoder,
        lambda: self_back(True, x, r1, dy1, qkv, ctx, lse, w, vec, fq, fk_self),
        lambda: self_back(False, x, r1, dy1, qkv, ctx, lse, w, vec, fq, fk_self),
    )
    fl_vec = (gvec_a + gvec_b)[:6].reshape(24, 128).astype(BF)
    spare = 16 * (share * (n - 1) // TILE) + rows - FLAT_ROWS
    flat = jnp.concatenate([fl_qkv, fl_out, fl_cross, fl_up, fl_down, fl_vec, jnp.zeros((spare, 128), BF)], axis=0)
    stacked = jnp.concatenate([flat[16 * (share * b // TILE) :][:rows] for b in range(n)], axis=0)
    mine = lax.psum_scatter(stacked, "batch", scatter_dimension=0, tiled=True)
    grad_share = lax.dynamic_slice(mine.astype(F32).reshape(-1), (shift,), (share,))

    square_sum = lax.psum(jnp.sum(grad_share * grad_share), ("section", "batch"))
    grad_norm = jnp.sqrt(square_sum)
    clip_factor = MAXNORM / jnp.maximum(grad_norm, MAXNORM)
    scaled = grad_share * clip_factor
    new_first = BETA_ONE * first_moment[0] + (1.0 - BETA_ONE) * scaled
    new_second = BETA_TWO * second_moment[0] + (1.0 - BETA_TWO) * scaled * scaled
    learn_rate = D ** (-0.5) * min(STEP ** (-0.5), STEP * WARMUP ** (-1.5))
    first_hat = new_first / (1.0 - BETA_ONE**STEP)
    second_hat = new_second / (1.0 - BETA_TWO**STEP)
    param_step = learn_rate * first_hat / (jnp.sqrt(second_hat) + ADAM_EPS)
    layer_out = jnp.where(is_decoder, out, mem)
    return (param_step[None], new_first[None], new_second[None], grad_share[None], layer_out[None], dx[None], grad_norm)


def solution(mesh):
    in_specs = (
        P("section", "batch"),
        P("section", "batch"),
        P("section", "batch"),
        P("section", "batch", None),
        P("batch"),
        P(None, "batch"),
        P("batch", None),
    )
    out_specs = (
        P("section", "batch"),
        P("section", "batch"),
        P("section", "batch"),
        P("section", "batch"),
        P("section", "batch", None),
        P("section", "batch", None),
        P(),
    )
    return jax.shard_map(shards, mesh=mesh, in_specs=in_specs, out_specs=out_specs, check_vma=False)
```

time: 1870 us -> 611 us (0.33)
  waiting for transfers between devices: 1010 us -> 314 us
  local copies, waits for them, and re-layouts: 413 us -> 56 us
  matrix products: 229 us -> 0 us
  Pallas kernels: 0 us -> 118 us
  other arithmetic: 120 us -> 41.5 us
    unnamed x4 -> x2, waiting for transfers between devices: 632 us -> 0.03 us
    ppermute x6 -> x2, waiting for transfers between devices: 383 us -> 71.2 us  [passed_along(): lax.ppermute(value, axis, [(source, source + steps) for source in range(f...]
    dot_general x66 -> x0, matrix products: 229 us -> none  [the longest x15 72 us: dot_plain(): return jnp.dot(lhs_mat, rhs_mat, preferred_element_type=jnp.float32)]
    reduce_scatter x0 -> x1, waiting for transfers between devices: none -> 139 us  [shards(): mine = lax.psum_scatter(stacked, 'batch', scatter_dimension=0, tiled=True)]
    pallas_call x0 -> x5, Pallas kernels: none -> 118 us  [kernel_call(): return lambda *operands: tuple(call(*operands))]
    slice x28 -> x4, local copies, waits for them, and re-layouts: 116 us -> 6.11 us  [shards(): flat[16 * (share * b // TILE):][:rows]]
    all_gather x0 -> x1, waiting for transfers between devices: none -> 104 us  [shards(): pieces = lax.all_gather(own, 'batch', axis=0, tiled=False)]
    cond x162 -> x0, local copies, waits for them, and re-layouts: 83.1 us -> none
  transfers between devices with their start and end apart: 8 -> 4, of which waited for: 8 -> 4; matrix products, arithmetic and copies ran while one was open for 1% -> 3% of each run, Pallas kernels for 0% -> 0%
where the time goes in v1:
time: 611 us; the launch traced here: 603 us
  waiting for transfers between devices  314 us (51%)
  Pallas kernels  118 us (19%)
  local copies, waits for them, and re-layouts  56 us (9%)
  other arithmetic  41.5 us (7%)
  blocking collectives  39.9 us (7%)
  between operations  16.5 us (3%)
  loops' own time  13.8 us (2%)
    reduce_scatter x1, waiting for transfers between devices, shards(): mine = lax.psum_scatter(stacked, 'batch', scatter_dimension=0, tiled=True)  139 us
    pallas_call x5, Pallas kernels, kernel_call(): return lambda *operands: tuple(call(*operands))  118 us
    all_gather x1, waiting for transfers between devices, shards(): pieces = lax.all_gather(own, 'batch', axis=0, tiled=False)  104 us
    ppermute x2, waiting for transfers between devices, passed_along(): lax.ppermute(value, axis, [(source, source + steps) for source in range(f...  71.2 us
    psum x1, blocking collectives, shards(): lax.psum(jnp.sum(grad_share * grad_share), ('section', 'batch'))  39.9 us
    unnamed x5, other arithmetic  15.7 us
    unnamed x79, local copies, waits for them, and re-layouts  15 us
  transfers between devices with their start and end apart: 4, of which 4 were waited for; matrix products, arithmetic and copies ran while one was open for 3% of the time, Pallas kernels for 0%

profile of v1, /device:TPU:0, one launch (start us, length us, event | category | flops | bytes accessed | tf_op | source)
XLA Modules:
  0.0 603.3 jit_solution(470024226901486680)
XLA Ops:
  7.2 10.5 %reduce.1 = bf16[229568]{0:T(1024)(128)(2,1)S(1)} reduce(f32[1,229568]{1,0:T(1,128)} %param.17, f32[]{:T(128)} %constant.125), dimensions={0}, to_apply=%param.17.reduce_sub_computation | reduce | bytes 1377412 | tf_op args[0]
  17.8 4.3 dynamic_update_slice.3
  23.2 0.9 fusion.2
  24.2 2.4 fusion.11
  26.6 103.9 %all-gather.2.cloned.1.call-done.flat_in = bf16[16,1824,128]{2,1,0:T(8,128)(2,1)} async-done(((bf16[1,1824,128]{2,1,0:T(8,128)(2,1)}), bf16[16,1824,128]{2,1,0:T(8,128)(2,1)}) %all-gather.2.cloned.1.call-update) | async-done | bytes 7471120 | tf_op jit(solution)/shard_map/all_gather | solution.py:557
  130.4 8.4 %shard_map.127 = (bf16[512,1536]{1,0:T(8,128)(2,1)}, bf16[512,512]{1,0:T(8,128)(2,1)}, bf16[512,1024]{1,0:T(8,128)(2,1)}, bf16[512,2048]{1,0:T(8,128)(2,1)}, bf1...) custom-call(bf16[16,1824,128]{2,1,0:T(8,128)(2,1)} %all-gather.2.cloned.1.call-done.flat_in), custom_call_target="tpu_custom_call" | custom-call | tf_op jit(solution)/shard_map/pallas_call | solution.py:404
  139.0 23.0 %conditional.5 = ((bf16[1536,1536]{1,0:T(8,128)(2,1)}, bf16[1536,512]{1,0:T(8,128)(2,1)}, f32[24,512]{1,0:T(8,128)}, f32[1536,512]{1,0:T(8,128)S(1)})) conditional(s32[]{:T(128)} %convert_element_type.47, (bf16[1536,512]{1,0:T(8,128)(2,1)}, bf16[512,1536]{1,0:T(8,128)(2,1)}, bf16[512,512]{1,0:T(8,128)(2,1)}, bf16[1536,128]{1,0:T(8,128)(2,1)S(1)}, ...), branch_computations={%region_0.1_spmd, %region_1.2_spmd} | conditional | bytes 8 | solution.py:564
  139.1 22.8 %branch_0_fun.4 = (bf16[1536,1536]{1,0:T(8,128)(2,1)}, bf16[1536,512]{1,0:T(8,128)(2,1)}, f32[24,512]{1,0:T(8,128)}, f32[1536,512]{1,0:T(8,128)S(1)}) custom-call(bf16[1536,512]{1,0:T(8,128)(2,1)} %get-tuple-element.152.x_ref, bf16[512,1536]{1,0:T(8,128)(2,1)} %get-tuple-element.153.wqkv, bf16[512,512]{1,0:T(8,128)(2,1)} %get-tuple-element.154.wout, ...), custom_call_target="tpu_custom_call" | custom-call | tf_op jit(solution)/shard_map/cond/branch_0_fun/pallas_call | solution.py:404
  161.9 23.0 %conditional.6 = ((bf16[1536,512]{1,0:T(8,128)(2,1)}, bf16[1536,1024]{1,0:T(8,128)(2,1)}, bf16[1536,2048]{1,0:T(8,128)(2,1)}, bf16[1536,2048]{1,0:T(8,128)(2,1)}, f32[1536,512]{1,0:T(8,128)})) conditional(s32[]{:T(128)} %convert_element_type.47, (f32[1536,512]{1,0:T(8,128)S(1)}, f32[6,512]{1,0:T(8,128)S(1)}, bf16[512,2048]{1,0:T(8,128)(2,1)}, ...), branch_computations={%region_2.3_spmd, %region_3.4_spmd} | conditional | bytes 20447292 | solution.py:569
  162.3 22.6 %branch_0_fun.5 = (bf16[1536,512]{1,0:T(8,128)(2,1)}, bf16[1536,1024]{1,0:T(8,128)(2,1)}, bf16[1536,2048]{1,0:T(8,128)(2,1)}, bf16[1536,2048]{1,0:T(8,128)(2,1)}, f32[1536,512]{1,0:T(8,128)}) custom-call(f32[1536,512]{1,0:T(8,128)S(1)} %get-tuple-element.162.r1_ref, f32[6,512]{1,0:T(8,128)S(1)} %get-tuple-element.163.vec, ...), custom_call_target="tpu_custom_call" | custom-call | tf_op jit(solution)/shard_map/cond/branch_0_fun/pallas_call | solution.py:404
  184.9 2.9 collective-permute-start
  187.8 3.3 select_convert_fusion
  191.8 17.5 %conditional.7 = ((bf16[1536,512]{1,0:T(8,128)(2,1)}, bf16[1536,1024]{1,0:T(8,128)(2,1)}, f32[1536,512]{1,0:T(8,128)}, bf16[4096,128]{1,0:T(8,128)(2,1)}, bf16[8...) conditional(s32[]{:T(128)} %convert_element_type.47, () %tuple.55, ...), branch_computations={%region_4.5_spmd, %region_5.6_spmd} | conditional | bytes 13123666 | solution.py:575
  191.8 2.1 broadcast.347
  193.9 2.1 broadcast.348
  196.0 1.6 broadcast.350
  197.5 1.6 broadcast.350.clone
  199.2 1.3 broadcast.346
  200.4 1.1 broadcast.349
  209.3 1.3 collective-permute-start.1
  211.3 70.5 %collective-permute-done.1 = bf16[1536,1024]{1,0:T(8,128)(2,1)} collective-permute-done((bf16[1536,1024]{1,0:T(8,128)(2,1)}, bf16[1536,1024]{1,0:T(8,128)(2,1)}, u32[]{:S(2)}, u32[]{:S(2)}) %collective-permute-start.1) | collective-permute-done | bytes 3145760 | tf_op jit(solution)/shard_map/ppermute | solution.py:543
  281.8 33.4 %conditional.8 = (f32[1536,512]{1,0:T(8,128)}, bf16[4096,128]{1,0:T(8,128)(2,1)}, bf16[8192,128]{1,0:T(8,128)(2,1)}, bf16[8192,128]{1,0:T(8,128)(2,1)}, f32[8,51...) conditional(s32[]{:T(128)} %convert_element_type.47, ...), branch_computations={%region_6.7_spmd, %region_7.8_spmd} | conditional | bytes 7471208 | solution.py:583
  281.8 30.2 %branch_0_fun.6 = (f32[1536,512]{1,0:T(8,128)}, bf16[4096,128]{1,0:T(8,128)(2,1)}, bf16[8192,128]{1,0:T(8,128)(2,1)}, bf16[8192,128]{1,0:T(8,128)(2,1)}, f32[8,512]{1,0:T(8,128)}) custom-call(bf16[1536,1024]{1,0:T(8,128)(2,1)} %get-tuple-element.176.gkv_ref, bf16[1536,512]{1,0:T(8,128)(2,1)} %get-tuple-element.177.mem_ref, ...), custom_call_target="tpu_custom_call" | custom-call | tf_op jit(solution)/shard_map/cond/branch_0_fun/pallas_call | solution.py:404
  312.0 2.1 fusion.18
  314.1 1.1 slice.128
  317.1 42.1 %conditional.9 = (bf16[6144,128]{1,0:T(8,128)(2,1)}, bf16[2048,128]{1,0:T(8,128)(2,1)}, f32[8,512]{1,0:T(8,128)S(1)}, bf16[1,1536,512]{2,1,0:T(8,128)(2,1)}, bf1...) conditional(s32[]{:T(128)} %convert_element_type.47, ...), branch_computations={%region_8.9_spmd, %region_9.10_spmd} | conditional | bytes 2801720 | solution.py:588
  317.2 33.8 %branch_0_fun.7 = (bf16[1536,512]{1,0:T(8,128)(2,1)}, bf16[6144,128]{1,0:T(8,128)(2,1)}, bf16[2048,128]{1,0:T(8,128)(2,1)}, f32[8,512]{1,0:T(8,128)S(1)}) custom-call(bf16[1536,512]{1,0:T(8,128)(2,1)} %get-tuple-element.196.x_ref, f32[1536,512]{1,0:T(8,128)S(1)} %get-tuple-element.197.r1_ref, f32[1536,512]{1,0:T(8,128)} %get-tuple-element.198.dy1_ref, ...), custom_call_target="tpu_custom_call" | custom-call | tf_op jit(solution)/shard_map/cond/branch_0_fun/pallas_call | solution.py:404
  351.0 2.3 fusion.22
  360.0 0.9 fusion.12
  360.9 1.9 constant_dynamic-update-slice_fusion.9
  362.8 2.0 constant_dynamic-update-slice_fusion.8
  364.7 1.8 fusion.10
  366.5 1.8 fusion.9
  372.4 0.9 constant_dynamic-update-slice_fusion.3
  374.9 0.8 constant_dynamic-update-slice_fusion.1
  376.5 1.1 fusion.6
  377.6 1.2 copy-done.23
  378.8 10.7 %multiply_reduce_fusion.1 = (f32[229568]{0:T(1024)S(1)}, f32[229568]{0:T(1024)S(1)}) fusion(f32[1,229568]{1,0:T(1,128)S(1)} %copy-done.23, f32[1,229568]{1,0:T(1,128)} %param.18), kind=kLoop, calls=%fused_computation.8 | loop fusion | flops 459136 | bytes 3673088 | tf_op jit(solution)/shard_map/mul | solution.py:605
  389.5 1.3 select_bitcast_fusion
  390.8 138.6 %reduce-scatter.2.cloned.1.call-done = bf16[1824,128]{1,0:T(8,128)(2,1)} async-done(((bf16[29184,128]{1,0:T(8,128)(2,1)}), bf16[1824,128]{1,0:T(8,128)(2,1)}) %reduce-scatter.2.cloned.1.call-update) | async-done | bytes 466960 | tf_op jit(solution)/shard_map/reduce_scatter | solution.py:597
  529.4 2.0 multiply_reduce_fusion
  531.4 1.3 dynamic-slice_convert_fusion
  532.7 39.9 %psum.7 = f32[]{:T(128)} all-reduce(f32[]{:T(128)} %multiply_reduce_fusion), channel_id=1, replica_groups=mesh['section'=2,'batch'=16] {'section','batch'}, use_global_device_ids=true, to_apply=%region_12.13 | all-reduce | flops 1 | bytes 8 | tf_op jit(solution)/shard_map/psum | solution.py:600
  573.3 1.8 add_divide_fusion
  575.1 5.1 broadcast_in_dim.63
  580.1 5.0 broadcast_in_dim.64
  585.1 5.0 broadcast_in_dim.65
  590.2 5.0 broadcast_in_dim.66
  (93 shorter events, 12.1 us)
Async XLA Ops:
  7.2 16.0 %copy-start.28 = (s32[2,1536]{1,0:T(2,128)S(1)}, s32[2,1536]{1,0:T(2,128)}, u32[]{:S(2)}) copy-start(s32[2,1536]{1,0:T(2,128)} %param.22) | copy-start | bytes 36868
  7.2 16.1 %copy-start.25 = (s32[1536]{0:T(1024)S(1)}, s32[1536]{0:T(1024)}, u32[]{:S(2)}) copy-start(s32[1536]{0:T(1024)} %param.21) | copy-start | bytes 18436
  7.2 123.3 %all-gather.2.cloned.1.call-start = ((), (), s32[]{:S(2)}) async-start(), calls=%async_computation.1 | async-start | bytes 7938048 | tf_op jit(solution)/shard_map/all_gather | solution.py:557
  22.2 0.8 copy-start.22
  23.0 506.4 %reduce-scatter.2.cloned.1.call-start = ((), (), s32[]{:S(2)}) async-start(), calls=%async_computation.2 | async-start | bytes 7938048 | tf_op jit(solution)/shard_map/reduce_scatter | solution.py:597
  23.1 115.8 %copy-start.29 = (pred[128]{0:T(512)(128)(4,1)}, pred[128]{0:T(512)(128)(4,1)S(1)}, u32[]{:S(2)}) copy-start(pred[128]{0:T(512)(128)(4,1)S(1)} %get-tuple-element.353) | copy-start | bytes 388
  23.1 115.8 %copy-start.30 = (s32[128]{0:T(128)}, s32[128]{0:T(128)S(1)}, u32[]{:S(2)}) copy-start(s32[128]{0:T(128)S(1)} %get-tuple-element.354) | copy-start | bytes 1540
  23.1 115.8 %copy-start.31 = (s32[128]{0:T(128)}, s32[128]{0:T(128)S(1)}, u32[]{:S(2)}) copy-start(s32[128]{0:T(128)S(1)} %get-tuple-element.355) | copy-start | bytes 1540
  23.1 115.8 %copy-start.32 = (pred[128]{0:T(512)(128)(4,1)}, pred[128]{0:T(512)(128)(4,1)S(1)}, u32[]{:S(2)}) copy-start(pred[128]{0:T(512)(128)(4,1)S(1)} %get-tuple-element.357) | copy-start | bytes 388
  23.1 115.8 %copy-start.33 = (pred[128]{0:T(512)(128)(4,1)}, pred[128]{0:T(512)(128)(4,1)S(1)}, u32[]{:S(2)}) copy-start(pred[128]{0:T(512)(128)(4,1)S(1)} %get-tuple-element.356) | copy-start | bytes 388
  23.2 1.0 copy-start.24
  23.2 115.7 %copy-start.26 = (pred[1536]{0:T(1024)(128)(4,1)}, pred[1536]{0:T(1024)(128)(4,1)S(1)}, u32[]{:S(2)}) copy-start(pred[1536]{0:T(1024)(128)(4,1)S(1)} %get-tuple-element.319) | copy-start | bytes 4612
  184.9 6.9 %collective-permute-start = (bf16[1536,1024]{1,0:T(8,128)(2,1)}, bf16[1536,1024]{1,0:T(8,128)(2,1)}, u32[]{:S(2)}, u32[]{:S(2)}) collective-permute-start(bf16[1536,1024]{1,0:T(8,128)(2,1)} %get-tuple-element.282), channel_id=1, source_target_pairs={{0,16},{1,17},{2,18},{3,19},{4,20},{5,21},{6,22},{7,23},{8,24},{9,... | collective-permute-start | bytes 9437192 | tf_op jit(solution)/shard_map/ppermute | solution.py:543
  209.3 72.5 %collective-permute-start.1 = (bf16[1536,1024]{1,0:T(8,128)(2,1)}, bf16[1536,1024]{1,0:T(8,128)(2,1)}, u32[]{:S(2)}, u32[]{:S(2)}) collective-permute-start(bf16[1536,1024]{1,0:T(8,128)(2,1)} %get-tuple-element.283), channel_id=1, source_target_pairs={{16,0},{17,1},{18,2},{19,3},{20,4},{21,5},{22,6},{23,7},{24,8},{25... | collective-permute-start | bytes 9437192 | tf_op jit(solution)/shard_map/ppermute | solution.py:543
  315.2 0.8 copy-start.6
  315.2 0.9 copy-start.8
  315.2 1.1 copy-start.10
  315.2 1.2 copy-start.12
  315.2 1.3 copy-start.14
  315.2 1.5 copy-start.16
  315.2 1.7 copy-start.18
  315.2 1.8 copy-start.20
  359.2 5.6 copy-start.3
  359.2 7.3 %copy-start.2 = (bf16[4096,128]{1,0:T(8,128)(2,1)S(1)}, bf16[4096,128]{1,0:T(8,128)(2,1)}, u32[]{:S(2)}) copy-start(bf16[4096,128]{1,0:T(8,128)(2,1)} %get-tuple-element.302) | copy-start | bytes 3145732
  360.9 7.5 %copy-start.21 = (bf16[1824,128]{1,0:T(8,128)(2,1)S(1)}, bf16[1824,128]{1,0:T(8,128)(2,1)}, u32[]{:S(2)}) copy-start(bf16[1824,128]{1,0:T(8,128)(2,1)} %copy-done.20) | copy-start | bytes 1400836
  362.8 6.4 %copy-start = (bf16[8192,128]{1,0:T(8,128)(2,1)S(1)}, bf16[8192,128]{1,0:T(8,128)(2,1)}, u32[]{:S(2)}) copy-start(bf16[8192,128]{1,0:T(8,128)(2,1)} %get-tuple-element.304) | copy-start | bytes 6291460
  366.5 3.5 copy-start.17
  368.3 2.4 copy-start.19
  368.3 3.2 copy-start.15
  369.1 3.2 copy-start.13
  369.1 4.1 copy-start.1
  371.6 2.5 copy-start.7
  372.4 2.5 copy-start.9
  373.2 2.4 copy-start.11
  373.2 3.2 copy-start.27
  377.6 1.2 copy-start.23
  378.7 10.8 %copy-start.4 = (bf16[1536,512]{1,0:T(8,128)(2,1)S(1)}, bf16[1536,512]{1,0:T(8,128)(2,1)}, u32[]{:S(2)}) copy-start(bf16[1536,512]{1,0:T(8,128)(2,1)} %get-tuple-element.284) | copy-start | bytes 4718596
  378.7 10.8 %copy-start.5 = (bf16[1536,512]{1,0:T(8,128)(2,1)S(1)}, bf16[1536,512]{1,0:T(8,128)(2,1)}, u32[]{:S(2)}) copy-start(bf16[1536,512]{1,0:T(8,128)(2,1)} %get-tuple-element.315) | copy-start | bytes 4718596
Sparse Core Ops, SparseCore 0:
  23.1 107.2 all-gather.1
  377.7 151.6 reduce-scatter.1

commit v2 on v1

v2 whole, which is shorter than its diff:
```python
import functools

import jax
import jax.numpy as jnp
from jax import lax
from jax.experimental import pallas as pl
from jax.experimental.pallas import tpu as pltpu
from jax.sharding import PartitionSpec as P

D = 512
FF = 2048
HEADS = 8
HD = 64
ROW = 512
STEP = 1000
WARMUP = 4000

BIG = 1e30
LN_EPS = 1e-05
BETA_ONE = 0.9
BETA_TWO = 0.98
ADAM_EPS = 1e-09
MAXNORM = 0.1

F32 = jnp.float32
BF = jnp.bfloat16
TILE = 16 * 128
CHUNK = 512
SEG_BITS = 12
POS_BITS = 9
LOOP = False

MATS = {}
_at = 0
for _name, _rows, _cols in (("qkv", D, 3 * D), ("out", D, D), ("cross", D, 2 * D), ("up", D, FF), ("down", FF, D)):
    _width = _cols // 128
    MATS[_name] = (_rows, _cols, _at, {12: 16, 4: 64, 8: 32, 16: 16}[_width])
    _at += _rows * _width
VEC_AT = _at
FLAT_ROWS = _at + 24
REST_AT = MATS["out"][2]


def dot_nn(lhs, rhs):
    return jnp.dot(lhs, rhs, preferred_element_type=F32)


def dot_nt(lhs, rhs):
    return lax.dot_general(lhs, rhs, (((1,), (1,)), ((), ())), preferred_element_type=F32)


def dot_tn(lhs, rhs):
    return lax.dot_general(lhs, rhs, (((0,), (0,)), ((), ())), preferred_element_type=F32)


def params_of(mib):
    return pltpu.CompilerParams(vmem_limit_bytes=mib * 2**20)


def row_spec(rows, cols):
    return pl.BlockSpec((rows, cols), lambda i: (i, 0))


def whole_spec(shape):
    return pl.BlockSpec(shape, lambda i: (0,) * len(shape), pipeline_mode=pl.Buffered(1))


def shape_of(shape, dtype):
    return jax.ShapeDtypeStruct(shape, dtype)


def ln_parts(resid):
    center = resid - jnp.mean(resid, axis=-1, keepdims=True)
    rstd = lax.rsqrt(jnp.mean(center * center, axis=-1, keepdims=True) + LN_EPS)
    return center * rstd, rstd


def ln_back(grad, hat, rstd, gain):
    scaled = grad * gain
    first = jnp.mean(scaled, axis=-1, keepdims=True)
    second = jnp.mean(scaled * hat, axis=-1, keepdims=True)
    grad_resid = rstd * (scaled - first - hat * second)
    return grad_resid, jnp.sum(grad * hat, axis=0, keepdims=True), jnp.sum(grad, axis=0, keepdims=True)


def gelu_both(pre):
    size = jnp.abs(pre)
    near = 1.0 / (1.0 + (0.3275911 * 0.7071067811865476) * size)
    bell = jnp.exp(-0.5 * pre * pre)
    poly = near * (0.127414796 + near * (-0.142248368 + near * (0.7107068705 + near * (-0.7265760135 + near * 0.5307027145))))
    tail = poly * bell
    phi = jnp.where(pre >= 0.0, 1.0 - tail, tail)
    return pre * phi, phi + pre * bell * 0.3989422804014327


def low_lanes(rows):
    return lax.broadcasted_iota(jnp.int32, (rows, 128), 1) < HD


def triangle(size, keys_first, causal):
    row = lax.broadcasted_iota(jnp.int32, (size, size), 0)
    col = lax.broadcasted_iota(jnp.int32, (size, size), 1)
    keep = (row <= col) if keys_first else (col <= row)
    return jnp.where(keep | (causal == 0), 0.0, -BIG).astype(F32)


def over_pairs(body):
    if LOOP:

        def step(pair, _):
            body(pair)
            return 0

        lax.fori_loop(0, HEADS // 2, step, 0)
    else:
        for pair in range(HEADS // 2):
            body(pair)


def lanes(at, pair):
    first = at + 128 * pair
    return pl.ds(first if isinstance(pair, int) else pl.multiple_of(first, 128), 128)


def attend_fwd(causal, q_ref, q_at, k_ref, k_at, v_ref, v_at, fq, fk, ctx_ref, lse_ref, lse_s, tri_s):
    low = low_lanes(ROW)
    lane = lax.broadcasted_iota(jnp.int32, (ROW, 128), 1)
    one = jnp.asarray(1.0, BF)
    if causal is not None:
        tri_s[...] = triangle(ROW, False, causal)

    def body(pair):
        q_pair = q_ref[:, lanes(q_at, pair)] * jnp.asarray(HD**-0.5, BF)
        k_pair = k_ref[:, lanes(k_at, pair)]
        v_pair = v_ref[:, lanes(v_at, pair)]
        halves = []
        for e in range(2):
            sel = low if e == 0 else ~low
            s = dot_nt(jnp.where(sel, q_pair, fq), jnp.where(sel, k_pair, fk))
            if causal is not None:
                s = s + tri_s[...]
            top = jnp.max(s, axis=1, keepdims=True)
            p = jnp.exp(s - top)
            o = dot_nn(p.astype(BF), jnp.where(sel, v_pair, one))
            total = pltpu.roll(o, 64, 1)
            halves.append(o / total)
            lse = top + jnp.log(jnp.where(sel, total, o))
            lse_s[...] = jnp.where(lane == 2 * pair + e, lse, lse_s[...])
        ctx_ref[:, lanes(0, pair)] = jnp.where(low, halves[0], halves[1]).astype(BF)

    over_pairs(body)
    lse_ref[...] = lse_s[...].T[0:HEADS, :]


def attend_bwd(causal, q_ref, q_at, k_ref, k_at, v_ref, v_at, fq, fk, lse_ref, do_ref, outs, dqt_ref, kt_ref, tri_s):
    low = low_lanes(ROW)
    zero = jnp.zeros((ROW, 128), BF)
    scale = jnp.asarray(HD**-0.5, BF)
    kt_ref[...] = k_ref[:, k_at : k_at + D].T
    if causal is not None:
        tri_s[...] = triangle(ROW, True, causal)

    def body(pair):
        q_pair = q_ref[:, lanes(q_at, pair)] * scale
        k_pair = k_ref[:, lanes(k_at, pair)]
        v_pair = v_ref[:, lanes(v_at, pair)]
        do_pair = do_ref[:, lanes(0, pair)]
        dks, dvs = [], []
        for e in range(2):
            head = 2 * pair + e
            sel = low if e == 0 else ~low
            s = dot_nt(jnp.where(sel, k_pair, fk), jnp.where(sel, q_pair, fq))
            if causal is not None:
                s = s + tri_s[...]
            p = jnp.exp(s - lse_ref[pl.ds(head, 1), :])
            prod = p * dot_nt(jnp.where(sel, v_pair, zero), do_pair)
            ds = (prod - p * jnp.sum(prod, axis=0, keepdims=True)).astype(BF)
            dvs.append(dot_nn(p.astype(BF), do_pair))
            dks.append(dot_nn(ds, q_pair))
            rows = pl.ds(HD * head if isinstance(pair, int) else pl.multiple_of(HD * head, HD), HD)
            dqt_ref[rows, :] = dot_nn(kt_ref[rows, :], ds)
        for (ref, at), parts in ((outs[1], dks), (outs[2], dvs)):
            ref[:, lanes(at, pair)] = jnp.where(low, parts[0], parts[1]).astype(BF)

    over_pairs(body)
    ref, at = outs[0]
    ref[:, at : at + D] = (dqt_ref[...] * HD**-0.5).T.astype(BF)


def group_perm(name, to_flat):
    _, cols, _, group = MATS[name]
    width = cols // 128
    size = group * width
    row = lax.broadcasted_iota(jnp.int32, (size, size), 0)
    col = lax.broadcasted_iota(jnp.int32, (size, size), 1)
    blocked, flat = (col, row) if to_flat else (row, col)
    source = width * (blocked & (group - 1)) + lax.shift_right_logical(blocked, group.bit_length() - 1)
    return jnp.where(source == flat, 1.0, 0.0).astype(BF)


def to_matrix(name, flat_ref, at, mat_ref):
    rows, cols, _, group = MATS[name]
    width = cols // 128
    size = group * width
    perm = group_perm(name, False)

    def move(g, _):
        got = dot_nn(perm, flat_ref[at + g * size : at + (g + 1) * size, :]).astype(BF)
        for c in range(width):
            mat_ref[g * group : (g + 1) * group, 128 * c : 128 * c + 128] = got[c * group : (c + 1) * group]
        return 0

    for g in range(rows // group):
        move(g, 0)


def to_flat(name, mat_ref, flat_ref, at):
    rows, cols, _, group = MATS[name]
    width = cols // 128
    size = group * width
    perm = group_perm(name, True)

    def move(g, _):
        block = mat_ref[g * group : (g + 1) * group, :].astype(BF)
        blocked = jnp.concatenate([block[:, 128 * c : 128 * c + 128] for c in range(width)], axis=0)
        flat_ref[at + g * size : at + (g + 1) * size, :] = dot_nn(perm, blocked).astype(BF)
        return 0

    for g in range(rows // group):
        move(g, 0)


def chunks(body, total_s, loop):
    if not loop:
        parts = [body(slice(c * CHUNK, (c + 1) * CHUNK)) for c in range(FF // CHUNK)]
        return sum(parts[1:], parts[0])

    def step(c, _):
        part = body(pl.ds(pl.multiple_of(c * CHUNK, CHUNK), CHUNK))
        total_s[...] = jnp.where(c == 0, 0.0, total_s[...]) + part
        return 0

    lax.fori_loop(0, FF // CHUNK, step, 0)
    return total_s[...]


def ffn_fwd(hidden_ref, w_up, w_down, act_ref, slope_ref, total_s, loop):
    def body(cols):
        act, slope = gelu_both(dot_nn(hidden_ref[...], w_up[:, cols]))
        act_b = act.astype(BF)
        act_ref[:, cols] = act_b
        slope_ref[:, cols] = slope.astype(slope_ref.dtype)
        return dot_nn(act_b, w_down[cols, :])

    return chunks(body, total_s, loop)


def ffn_bwd(branch_ref, w_up, w_down, slope_ref, dz_ref, total_s, loop):
    def body(cols):
        grad_act = dot_nt(branch_ref[...], w_down[cols, :])
        grad_pre = (grad_act * slope_ref[:, cols].astype(F32)).astype(BF)
        dz_ref[:, cols] = grad_pre
        return dot_nt(grad_pre, w_up[:, cols])

    return chunks(body, total_s, loop)


def self_head(dy1, r1_ref, vec, w_out, dr1_ref, dctx_ref, gvec):
    hat1, rstd1 = ln_parts(r1_ref[...])
    dr1, gain1, shift1 = ln_back(dy1, hat1, rstd1, vec[0:1, :])
    dr1_ref[...] = dr1
    dctx_ref[...] = dot_nt(dr1.astype(BF), w_out[...]).astype(BF)
    gvec[0:1, :] = gain1
    gvec[1:2, :] = shift1


def copies(sources, targets, sems):
    made = [pltpu.make_async_copy(s, t, sems.at[i]) for i, (s, t) in enumerate(zip(sources, targets))]
    for one in made:
        one.start()
    return made


def piece_row(share, b):
    return 16 * (share * b // TILE)


def shift_kernel(share, shift_ref, params_ref, out_ref, rows_s):
    rows = out_ref.shape[0]
    full = share // 1024
    rows_s[0:16, :] = jnp.zeros((16, 128), F32)
    rows_s[16 + 8 * full :, :] = jnp.zeros((rows_s.shape[0] - 16 - 8 * full, 128), F32)

    def fill(k, _):
        at = pl.multiple_of(1024 * k, 1024)
        rows_s[pl.ds(pl.multiple_of(8 * k + 16, 8), 8), :] = params_ref[:, pl.ds(at, 1024)].reshape(8, 128)
        return 0

    lax.fori_loop(0, full, fill, 0, unroll=8)
    for r in range(-(-(share - 1024 * full) // 128)):
        at = 1024 * full + 128 * r
        width = min(128, share - at)
        rows_s[16 + 8 * full + r : 17 + 8 * full + r, 0:width] = params_ref[:, at : at + width]
    shift = shift_ref[0]
    down, right = shift // 128, lax.rem(shift, 128)
    lane = lax.broadcasted_iota(jnp.int32, (16, 128), 1)

    def move(k, _):
        same = rows_s[pl.ds(16 * k + 16 - down, 16), :]
        above = rows_s[pl.ds(16 * k + 15 - down, 16), :]
        got = jnp.where(lane >= right, pltpu.roll(same, right, 1), pltpu.roll(above, right, 1))
        out_ref[pl.ds(pl.multiple_of(16 * k, 16), 16), :] = got.astype(BF)
        return 0

    lax.fori_loop(0, rows // 16, move, 0, unroll=6)


def unshift_kernel(share, shift_ref, sums_ref, grad_ref, square_ref):
    shift = shift_ref[0]
    down, left = shift // 128, lax.rem(shift, 128)
    lane = lax.broadcasted_iota(jnp.int32, (8, 128), 1)
    full = share // 1024

    def block(at):
        same = sums_ref[pl.ds(at + down, 8), :]
        below = sums_ref[pl.ds(at + down + 1, 8), :]
        back = lax.rem(128 - left, 128)
        return jnp.where(lane < 128 - left, pltpu.roll(same, back, 1), pltpu.roll(below, back, 1))

    def move(k, total):
        got = block(8 * k)
        grad_ref[:, pl.ds(pl.multiple_of(1024 * k, 1024), 1024)] = got.reshape(1, 1024)
        return total + got * got

    total = lax.fori_loop(0, full, move, jnp.zeros((8, 128), F32), unroll=8)
    rest = share - 1024 * full
    if rest:
        got = block(8 * full)
        place = lax.broadcasted_iota(jnp.int32, (8, 128), 0) * 128 + lane
        got = jnp.where(place < rest, got, 0.0)
        total = total + got * got
        for r in range(-(-rest // 128)):
            width = min(128, rest - 128 * r)
            at = 1024 * full + 128 * r
            grad_ref[:, at : at + width] = got[r : r + 1, 0:width]
    square_ref[...] = total


def adam_kernel(share, clip_ref, grad_ref, first_ref, second_ref, step_ref, new_first_ref, new_second_ref):
    clip = clip_ref[0]
    rate = D ** (-0.5) * min(STEP ** (-0.5), STEP * WARMUP ** (-1.5))

    def update(at, width, fold):
        shape = (8, 128) if fold else (1, width)
        scaled = grad_ref[:, pl.ds(at, width)].reshape(shape) * clip
        first = BETA_ONE * first_ref[:, pl.ds(at, width)].reshape(shape) + (1.0 - BETA_ONE) * scaled
        second = BETA_TWO * second_ref[:, pl.ds(at, width)].reshape(shape) + (1.0 - BETA_TWO) * scaled * scaled
        first_hat = first / (1.0 - BETA_ONE**STEP)
        second_hat = second / (1.0 - BETA_TWO**STEP)
        step = rate * first_hat / (jnp.sqrt(second_hat) + ADAM_EPS)
        step_ref[:, pl.ds(at, width)] = step.reshape(1, width)
        new_first_ref[:, pl.ds(at, width)] = first.reshape(1, width)
        new_second_ref[:, pl.ds(at, width)] = second.reshape(1, width)

    def move(k, _):
        update(pl.multiple_of(1024 * k, 1024), 1024, True)
        return 0

    full = share // 1024
    lax.fori_loop(0, full, move, 0, unroll=4)
    for at in range(1024 * full, share, 128):
        update(at, min(128, share - at), False)


def weights_kernel(n, share, flat_in, *refs):
    outs, flat = refs[:6], refs[6]
    for b in range(n):
        tile = share * b // TILE
        last = -(-share * (b + 1) // TILE)
        start, count = 16 * tile, 16 * (last - tile)
        if (share * b) % TILE:
            flat[start : start + 16, :] += flat_in[b, 0:16, :]
        else:
            flat[start : start + 16, :] = flat_in[b, 0:16, :]
        flat[start + 16 : start + count, :] = flat_in[b, 16:count, :]
    for name, ref in zip(MATS, outs):
        to_matrix(name, flat, MATS[name][2], ref)
    outs[5][...] = flat[VEC_AT : VEC_AT + 32, :]


def self_fwd_kernel(causal_ref, x_ref, wqkv, wout, fq, fk, qkv_ref, ctx_ref, lse_ref, r1_ref, lse_s, tri_s):
    x = x_ref[...]
    qkv_ref[...] = dot_nn(x, wqkv[...]).astype(BF)
    attend_fwd(
        causal_ref[0], qkv_ref, 0, qkv_ref, D, qkv_ref, 2 * D, fq[...], fk[...], ctx_ref, lse_ref, lse_s, tri_s
    )
    r1_ref[...] = x.astype(F32) + dot_nn(ctx_ref[...], wout[...])


def enc_ffn_kernel(r1_ref, vec, w_up, w_down, w_cross, mem_ref, kv_ref, act_ref, slope_ref, r2_ref, hid_s, total_s):
    hat, _ = ln_parts(r1_ref[...])
    y1 = hat * vec[0:1, :] + vec[1:2, :]
    hid_s[...] = y1.astype(BF)
    r2_ref[...] = y1
    r2 = r2_ref[...] + ffn_fwd(hid_s, w_up, w_down, act_ref, slope_ref, total_s, True)
    r2_ref[...] = r2
    hat, _ = ln_parts(r2)
    mem = (hat * vec[2:3, :] + vec[3:4, :]).astype(BF)
    mem_ref[:, :D] = mem
    mem_ref[:, D:] = mem
    kv_ref[...] = dot_nn(mem, w_cross[...]).astype(BF)


def dec_kernel(
    row, r1_ref, kv_ref, go_any, vec, w_cross, w_out_any, w_up_any, w_down_any, fq, fk,
    out_any, gkv_ref, dr1_ref, dctx1_ref, act_any, dz_any, hid_any, br_any, left_any, right_ref, gvec,
    cq_s, lse_s, wide_s, dctx_s, dcq_s, dqt_s, kt_s, slope_s, act_s, dz_s, hid_s, br_s, left_s, out_s,
    go_ref, w_out, w_up, w_down, keep_s, total_s, in_sems, out_sems,
):
    up_copy, down_copy, go_copy, out_copy = copies(
        (w_up_any, w_down_any, go_any.at[pl.ds(row * ROW, ROW)], w_out_any), (w_up, w_down, go_ref, w_out), in_sems
    )
    sent = []

    def emit(source, target):
        sent.append(pltpu.make_async_copy(source, target, out_sems.at[len(sent)]))
        sent[-1].start()

    hat1, _ = ln_parts(r1_ref[...])
    y1 = hat1 * vec[0:1, :] + vec[1:2, :]
    y1_b = y1.astype(BF)
    left_s[:, :D] = y1_b
    cq_s[...] = dot_nn(y1_b, w_cross[:, :D]).astype(BF)
    ctx_s = left_s.at[:, D:]
    attend_fwd(None, cq_s, 0, kv_ref, 0, kv_ref, D, fq[...], fk[...], ctx_s, lse_s, wide_s, None)
    emit(left_s, left_any)
    r2 = y1 + dot_nn(ctx_s[...], w_cross[:, D:])
    hat2, rstd2 = ln_parts(r2)
    y2 = hat2 * vec[2:3, :] + vec[3:4, :]
    hid_s[...] = y2.astype(BF)
    keep_s[...] = y2
    emit(hid_s, hid_any)
    up_copy.wait()
    down_copy.wait()
    r3 = keep_s[...] + ffn_fwd(hid_s, w_up, w_down, act_s, slope_s, total_s, False)
    emit(act_s, act_any)
    hat3, rstd3 = ln_parts(r3)
    out_s[...] = (hat3 * vec[4:5, :] + vec[5:6, :]).astype(BF)
    emit(out_s, out_any)

    go_copy.wait()
    dr3, gain3, shift3 = ln_back(go_ref[...].astype(F32), hat3, rstd3, vec[4:5, :])
    br_s[...] = dr3.astype(BF)
    emit(br_s, br_any)
    keep_s[...] = dr3
    dy2 = keep_s[...] + ffn_bwd(br_s, w_up, w_down, slope_s, dz_s, total_s, False)
    emit(dz_s, dz_any)
    dr2, gain2, shift2 = ln_back(dy2, hat2, rstd2, vec[2:3, :])
    dr2_b = dr2.astype(BF)
    right_ref[:, D:] = dr2_b
    dctx_s[...] = dot_nt(dr2_b, w_cross[:, D:]).astype(BF)
    attend_bwd(
        None, cq_s, 0, kv_ref, 0, kv_ref, D, fq[...], fk[...], lse_s, dctx_s,
        ((dcq_s, 0), (gkv_ref, 0), (gkv_ref, D)), dqt_s, kt_s, None,
    )
    dcq = dcq_s[...]
    right_ref[:, :D] = dcq
    out_copy.wait()
    self_head(dr2 + dot_nt(dcq, w_cross[:, :D]), r1_ref, vec, w_out, dr1_ref, dctx1_ref, gvec)
    gvec[2:3, :] = gain2
    gvec[3:4, :] = shift2
    gvec[4:5, :] = gain3
    gvec[5:6, :] = shift3
    for one in sent:
        one.wait()


def enc_back_kernel(
    gkv_ref, r1_ref, r2_ref, slope_ref, vec, w_cross, w_out, w_up, w_down,
    dr1_ref, dctx1_ref, dz_ref, hid_ref, br_ref, gvec, keep_s, total_s,
):
    dmem = dot_nt(gkv_ref[...], w_cross[...])
    hat2, rstd2 = ln_parts(r2_ref[...])
    dr2, gain2, shift2 = ln_back(dmem, hat2, rstd2, vec[2:3, :])
    hat1, _ = ln_parts(r1_ref[...])
    hid_ref[...] = (hat1 * vec[0:1, :] + vec[1:2, :]).astype(BF)
    br_ref[...] = dr2.astype(BF)
    keep_s[...] = dr2
    dy1 = keep_s[...] + ffn_bwd(br_ref, w_up, w_down, slope_ref, dz_ref, total_s, True)
    self_head(dy1, r1_ref, vec, w_out, dr1_ref, dctx1_ref, gvec)
    gvec[2:3, :] = gain2
    gvec[3:4, :] = shift2
    gvec[4:8, :] = jnp.zeros((4, D), F32)


KINDS = ("hid", "dz", "ctx", "dr1", "left", "right", "act", "branch")


def rest_kernel(rows, dec_ref, *refs):
    count = len(KINDS) * rows
    sources, flat, refs = (refs[:count], refs[count : 2 * count]), refs[2 * count], refs[2 * count + 1 :]
    kept, (hid_t, g_big, g_cross, g_out, sems) = dict(zip(KINDS, refs)), refs[len(KINDS) :]

    def fetch(ins, i):
        target = kept[KINDS[i // rows]].at[pl.ds((i % rows) * ROW, ROW)]
        return pltpu.make_async_copy(ins[i], target, sems.at[i])

    for which, ins in enumerate(sources):

        @pl.when(dec_ref[0] == which)
        def _(ins=ins):
            for i in range(count):
                fetch(ins, i).start()

    def ready(*kinds):
        for kind in kinds:
            for r in range(rows):
                fetch(sources[0], KINDS.index(kind) * rows + r).wait()

    base = {name: MATS[name][2] - REST_AT for name in MATS}
    ready("hid", "dz")
    hid_t[...] = kept["hid"][...].T

    def up(c, _):
        cols = pl.ds(pl.multiple_of(c * CHUNK, CHUNK), CHUNK)
        g_big[:, cols] = dot_nn(hid_t[...], kept["dz"][:, cols])
        return 0

    lax.fori_loop(0, FF // CHUNK, up, 0)
    to_flat("up", g_big, flat, base["up"])
    ready("ctx", "dr1")
    g_out[...] = dot_tn(kept["ctx"][...], kept["dr1"][...].astype(BF))
    to_flat("out", g_out, flat, base["out"])
    ready("left", "right")
    for at in (0, D):
        g_cross[:, at : at + D] = dot_tn(kept["left"][:, at : at + D], kept["right"][:, at : at + D])
    to_flat("cross", g_cross, flat, base["cross"])
    ready("act", "branch")
    rows_n, _, _, group = MATS["down"]
    perm = group_perm("down", True)

    for c in range(rows_n // D):
        cols = slice(c * D, (c + 1) * D)
        g_out[...] = dot_tn(kept["act"][:, cols], kept["branch"][...])
        for g in range(D // group):
            block = g_out[g * group : (g + 1) * group, :].astype(BF)
            blocked = jnp.concatenate([block[:, 128 * j : 128 * j + 128] for j in range(4)], axis=0)
            at = base["down"] + (c * (D // group) + g) * 4 * group
            flat[at : at + 4 * group, :] = dot_nn(perm, blocked).astype(BF)


def self_back_kernel(causal_ref, dr1_ref, dctx_ref, qkv_ref, lse_ref, wqkv, fq, fk, dx_ref, dqkv, dqt_s, kt_s, tri_s):
    attend_bwd(
        causal_ref[0], qkv_ref, 0, qkv_ref, D, qkv_ref, 2 * D, fq[...], fk[...], lse_ref, dctx_ref,
        ((dqkv, 0), (dqkv, D), (dqkv, 2 * D)), dqt_s, kt_s, tri_s,
    )
    dx_ref[...] = (dr1_ref[...] + dot_nt(dqkv[...], wqkv[...])).astype(BF)


def qkv_kernel(rows, x_ref, *refs):
    ins, fl_qkv, dqkv, x_t, g_qkv, sems = refs[:rows], *refs[rows:]
    made = copies(ins, [dqkv.at[pl.ds(r * ROW, ROW)] for r in range(rows)], sems)
    x_t[...] = x_ref[...].T
    for one in made:
        one.wait()

    def step(c, _):
        cols = pl.ds(pl.multiple_of(c * D, D), D)
        g_qkv[:, cols] = dot_nn(x_t[...], dqkv[:, cols])
        return 0

    lax.fori_loop(0, 3, step, 0)
    to_flat("qkv", g_qkv, fl_qkv, 0)


def pack_kernel(share, planes, base, place_ref, *refs):
    parts, outs, flat = refs[:-5], refs[-5:-1], refs[-1]
    send_a, keep_a, send_b, keep_b = outs
    at = 0
    for part in parts:
        flat[at : at + part.shape[0], :] = part[...]
        at += part.shape[0]
    y, x = place_ref[0], place_ref[1]
    half = send_a.shape[2]
    for i, z in enumerate(planes):
        for j in range(2):
            for ref, y_to, x_to, skip in (
                (send_a, 1 - y, j, 0), (keep_a, y, j, 0), (send_b, j, 1 - x, half), (keep_b, j, x, half),
            ):
                b = 4 * z + 2 * y_to + x_to
                start = pl.multiple_of(16 * ((share * b) // TILE) - base + skip, 16)
                ref[i, j] = flat[pl.ds(start, half), :]


def kernel_call(body, micros=1, **options):
    cost = pl.CostEstimate(flops=micros * 10**9, bytes_accessed=0, transcendentals=0)
    call = pl.pallas_call(body, cost_estimate=cost, **options)
    return lambda *operands: tuple(call(*operands))


IN_VMEM = pl.BlockSpec(memory_space=pltpu.VMEM)
IN_SMEM = pl.BlockSpec(memory_space=pltpu.SMEM)
ANYWHERE = pl.BlockSpec(memory_space=pl.ANY)


def at_row(row, cols, rows=ROW):
    return pl.BlockSpec((rows, cols), lambda i: (row, 0), pipeline_mode=pl.Buffered(1))


def shifted(shift, params, share, rows):
    return kernel_call(
        functools.partial(shift_kernel, share),
        in_specs=[IN_SMEM, IN_VMEM],
        out_specs=[IN_VMEM],
        out_shape=[shape_of((rows, 128), BF)],
        scratch_shapes=[pltpu.VMEM((rows + 32, 128), F32)],
        compiler_params=params_of(16),
    )(shift, params)[0]


def unshifted(shift, sums, share):
    return kernel_call(
        functools.partial(unshift_kernel, share),
        in_specs=[IN_SMEM, IN_VMEM],
        out_specs=[IN_VMEM] * 2,
        out_shape=[shape_of((1, share), F32), shape_of((8, 128), F32)],
        compiler_params=params_of(16),
    )(shift, sums)


def adam(clip, grad, first, second, share):
    return kernel_call(
        functools.partial(adam_kernel, share),
        in_specs=[IN_SMEM] + [IN_VMEM] * 3,
        out_specs=[IN_VMEM] * 3,
        out_shape=[shape_of((1, share), F32)] * 3,
        compiler_params=params_of(24),
    )(clip, grad, first, second)


def split_weights(pieces, n, share):
    shapes = [(rows, cols) for rows, cols, _, _ in MATS.values()] + [(32, 128)]
    rows = 16 * (-(-share * n // TILE) + 2)
    return kernel_call(
        functools.partial(weights_kernel, n, share),
        in_specs=[IN_VMEM],
        out_specs=[IN_VMEM] * 6,
        out_shape=[shape_of(s, BF) for s in shapes],
        scratch_shapes=[pltpu.VMEM((rows, 128), BF)],
        compiler_params=params_of(48),
    )(pieces)


def row_shapes(*cols):
    return [shape_of((ROW, abs(c)), F32 if c < 0 else BF) for c in cols]


def self_fwd(causal, row, x, w, fq, fk):
    names = ("qkv", "ctx", "lse", "r1")
    vm = pltpu.VMEM
    got = kernel_call(
        self_fwd_kernel,
        micros=5,
        grid=(1,),
        in_specs=[IN_SMEM, at_row(row, D), whole_spec((D, 3 * D)), whole_spec((D, D)), at_row(row, 128), at_row(row, 128)],
        out_specs=[at_row(0, 3 * D), at_row(0, D), at_row(0, ROW, HEADS), at_row(0, D)],
        out_shape=row_shapes(3 * D, D) + [shape_of((HEADS, ROW), F32)] + row_shapes(-D),
        scratch_shapes=[vm((ROW, 128), F32), vm((ROW, ROW), F32)],
        compiler_params=params_of(32),
    )(causal, x, w["qkv"], w["out"], fq, fk)
    return dict(zip(names, got))


def enc_ffn(r1, w, vec):
    names = ("mem", "kv", "act", "slope", "r2")
    got = kernel_call(
        enc_ffn_kernel,
        micros=10,
        grid=(1,),
        in_specs=[
            at_row(0, D), whole_spec((6, D)), whole_spec((D, FF)), whole_spec((FF, D)), whole_spec((D, 2 * D)),
        ],
        out_specs=[at_row(0, 2 * D), at_row(0, 2 * D), at_row(0, FF), at_row(0, FF), at_row(0, D)],
        out_shape=row_shapes(2 * D, 2 * D, FF, FF, -D),
        scratch_shapes=[pltpu.VMEM((ROW, D), BF), pltpu.VMEM((ROW, D), F32)],
        compiler_params=params_of(48),
    )(r1, vec, w["up"], w["down"], w["cross"])
    return dict(zip(names, got))


def dec_call(row, r1, kv, go, w, vec, fq, fk):
    vm = pltpu.VMEM
    names = ("out", "gkv", "dr1", "dctx", "act", "dz", "hid", "branch", "left", "right", "gvec")
    got = kernel_call(
        functools.partial(dec_kernel, row),
        micros=23,
        grid=(1,),
        in_specs=[
            at_row(0, D), at_row(0, 2 * D), ANYWHERE, whole_spec((6, D)), whole_spec((D, 2 * D)),
            ANYWHERE, ANYWHERE, ANYWHERE, at_row(row, 128), at_row(row, 128),
        ],
        out_specs=[ANYWHERE, at_row(0, 2 * D), at_row(0, D), at_row(0, D)] + [ANYWHERE] * 5
        + [at_row(0, 2 * D), whole_spec((8, D))],
        out_shape=row_shapes(D, 2 * D, -D, D, FF, FF, D, D, 2 * D, 2 * D) + [shape_of((8, D), F32)],
        scratch_shapes=[
            vm((ROW, D), BF), vm((HEADS, ROW), F32), vm((ROW, 128), F32), vm((ROW, D), BF), vm((ROW, D), BF),
            vm((D, ROW), F32), vm((D, ROW), BF), vm((ROW, FF), BF), vm((ROW, FF), BF), vm((ROW, FF), BF), vm((ROW, D), BF),
            vm((ROW, D), BF), vm((ROW, 2 * D), BF), vm((ROW, D), BF), vm((ROW, D), BF), vm((D, D), BF), vm((D, FF), BF),
            vm((FF, D), BF), vm((ROW, D), F32), vm((ROW, D), F32), pltpu.SemaphoreType.DMA((4,)), pltpu.SemaphoreType.DMA((6,)),
        ],
        compiler_params=params_of(56),
    )(r1, kv, go, vec, w["cross"], w["out"], w["up"], w["down"], fq, fk)
    return dict(zip(names, got))


def enc_back(gkv, r1, fwd, w, vec):
    names = ("dr1", "dctx", "dz", "hid", "branch", "gvec")
    got = kernel_call(
        enc_back_kernel,
        micros=10,
        grid=(1,),
        in_specs=[
            at_row(0, 2 * D), at_row(0, D), at_row(0, D), at_row(0, FF), whole_spec((6, D)), whole_spec((D, 2 * D)),
            whole_spec((D, D)), whole_spec((D, FF)), whole_spec((FF, D)),
        ],
        out_specs=[at_row(0, c) for c in (D, D, FF, D, D)] + [whole_spec((8, D))],
        out_shape=row_shapes(-D, D, FF, D, D) + [shape_of((8, D), F32)],
        scratch_shapes=[pltpu.VMEM((ROW, D), F32)] * 2,
        compiler_params=params_of(56),
    )(gkv, r1, fwd["r2"], fwd["slope"], vec, w["cross"], w["out"], w["up"], w["down"])
    return dict(zip(names, got))


def rest_grads(is_dec, enc_rows, dec_rows):
    rows = len(dec_rows)
    ins = [row[kind] for some in (enc_rows, dec_rows) for kind in KINDS for row in some]
    vm = pltpu.VMEM
    kept = [vm((rows * ROW, dec_rows[0][kind].shape[1]), dec_rows[0][kind].dtype) for kind in KINDS]
    return kernel_call(
        functools.partial(rest_kernel, rows),
        micros=18,
        in_specs=[IN_SMEM] + [ANYWHERE] * len(ins),
        out_specs=[IN_VMEM],
        out_shape=[shape_of((VEC_AT - REST_AT, 128), BF)],
        scratch_shapes=kept
        + [vm((D, rows * ROW), BF), vm((D, FF), F32), vm((D, 2 * D), F32), vm((D, D), F32)]
        + [pltpu.SemaphoreType.DMA((len(KINDS) * rows,))],
        compiler_params=params_of(60),
    )(is_dec, *ins)[0]


def self_back(causal, row, grads, fwd, w, fq, fk):
    vm = pltpu.VMEM
    shapes = row_shapes(D, 3 * D)
    return kernel_call(
        self_back_kernel,
        micros=8,
        grid=(1,),
        in_specs=[
            IN_SMEM, at_row(0, D), at_row(0, D), at_row(0, 3 * D), at_row(0, ROW, HEADS), whole_spec((D, 3 * D)),
            at_row(row, 128), at_row(row, 128),
        ],
        out_specs=[whole_spec(s.shape) for s in shapes],
        out_shape=shapes,
        scratch_shapes=[vm((D, ROW), F32), vm((D, ROW), BF), vm((ROW, ROW), F32)],
        compiler_params=params_of(40),
    )(causal, grads["dr1"], grads["dctx"], fwd["qkv"], fwd["lse"], w["qkv"], fq, fk)


def qkv_grad(x, dqkvs):
    vm = pltpu.VMEM
    t, rows = x.shape[0], len(dqkvs)
    return kernel_call(
        functools.partial(qkv_kernel, rows),
        micros=5,
        in_specs=[IN_VMEM] + [ANYWHERE] * rows,
        out_specs=[IN_VMEM],
        out_shape=[shape_of((REST_AT, 128), BF)],
        scratch_shapes=[vm((t, 3 * D), BF), vm((D, t), BF), vm((D, 3 * D), F32), pltpu.SemaphoreType.DMA((rows,))],
        compiler_params=params_of(40),
    )(x, *dqkvs)[0]


def pack(place, parts, planes, base, share, rows):
    half = rows // 2
    total = sum(p.shape[0] for p in parts)
    need = piece_row(share, 4 * planes[-1] + 3) - base + rows
    return kernel_call(
        functools.partial(pack_kernel, share, planes, base),
        in_specs=[IN_SMEM] + [IN_VMEM] * len(parts),
        out_specs=[IN_VMEM] * 4,
        out_shape=[shape_of((len(planes), 2, half, 128), BF)] * 4,
        scratch_shapes=[pltpu.VMEM((max(total, need), 128), BF)],
        compiler_params=params_of(40),
    )(place, *parts)


def mask_features(segments, live):
    t = segments.shape[0]
    lane = (jnp.arange(128, dtype=jnp.int32) % HD)[None, :]
    pair = lane // 2
    odd = lane % 2 == 1
    is_seg = pair < SEG_BITS
    is_pos = (pair >= SEG_BITS) & (pair < SEG_BITS + POS_BITS)
    place = (jnp.arange(t, dtype=jnp.int32) % ROW)[:, None]
    bit = jnp.where(
        is_seg,
        (segments[:, None] >> jnp.minimum(pair, SEG_BITS)) & 1,
        (place >> jnp.clip(pair - SEG_BITS, 0, POS_BITS)) & 1,
    )
    query = jnp.where(odd, 1 - bit, bit) * (is_seg | is_pos)
    key = jnp.where(odd, bit, 1 - bit)
    keys = [jnp.where(is_seg | (is_pos & (live[i][:, None] != 1)), key.astype(F32) * -BIG, 0.0).astype(BF) for i in range(2)]
    return query.astype(BF), keys[0], keys[1]


def passed_along(value, axis, steps):
    count = lax.axis_size(axis)
    first, last = (max(0, -steps), min(count, count - steps))
    return lax.ppermute(value, axis, [(source, source + steps) for source in range(first, last)])


def ghosts(shapes):
    if not shapes:
        return ()
    return kernel_call(lambda *refs: None, out_specs=[ANYWHERE] * len(shapes), out_shape=list(shapes))()


def either(is_decoder, dec, enc):
    thunks = (enc, dec)
    made = [jax.eval_shape(t) for t in thunks]
    slots, where = [], []
    for tree in made:
        free = list(range(len(slots)))
        taken = []
        for leaf in jax.tree.leaves(tree):
            key = (leaf.shape, leaf.dtype)
            match = next((i for i in free if slots[i] == key), None)
            if match is None:
                slots.append(key)
                match = len(slots) - 1
            else:
                free.remove(match)
            taken.append(match)
        where.append(taken)

    def branch(which):
        def run():
            leaves = jax.tree.leaves(thunks[which]())
            filled = dict(zip(where[which], leaves))
            missing = [i for i in range(len(slots)) if i not in filled]
            filled.update(zip(missing, ghosts([shape_of(*slots[i]) for i in missing])))
            return tuple(filled[i] for i in range(len(slots)))

        return run

    got = lax.cond(is_decoder, branch(1), branch(0))
    back = [jax.tree.unflatten(jax.tree.structure(made[i]), [got[s] for s in where[i]]) for i in range(2)]
    return back[1], back[0]


def plane_permute(value, step):
    return lax.ppermute(value, "batch", [(i, i ^ step) for i in range(16)])


def line_permute(value, step, sources):
    pairs = [(4 * z + k, 4 * (z + step) + k) for z in sources for k in range(4)]
    return lax.ppermute(value, "batch", pairs)


def added(*values):
    total = values[0].astype(F32)
    for value in values[1:]:
        total = total + value.astype(F32)
    return total


def plane_sums(packed, y, x):
    send_a, keep_a, send_b, keep_b = packed
    got_a, got_b = plane_permute(send_a, 2), plane_permute(send_b, 1)

    def part(keep, got, index):
        return added(lax.dynamic_index_in_dim(keep, index, 1, False), lax.dynamic_index_in_dim(got, index, 1, False))

    far_a, far_b = part(keep_a, got_a, 1 - x).astype(BF), part(keep_b, got_b, 1 - y).astype(BF)
    in_a, in_b = plane_permute(far_a, 1), plane_permute(far_b, 2)
    sum_a, sum_b = added(part(keep_a, got_a, x), in_a), added(part(keep_b, got_b, y), in_b)
    return jnp.stack([sum_a.astype(BF), sum_b.astype(BF)], axis=1)


def line_sums(early, late, z):
    one, two, three = early[0], early[1], early[2]

    def low(value):
        return value.astype(BF)

    up = line_permute(three, 1, (0,))
    down = line_permute(one, -1, (3,))
    up = line_permute(low(jnp.where(z == 0, two.astype(F32), added(three, up))), 1, (0, 1))
    down = line_permute(low(jnp.where(z == 3, two.astype(F32), added(one, down))), -1, (2, 3))
    third = jnp.where(z == 0, one.astype(F32), added(jnp.where(z == 1, two, three), up))
    up = line_permute(low(third), 1, (0, 1, 2))
    zero = late[0]
    near = line_permute(zero, -1, (1, 3))
    pair = added(zero, near)
    far = line_permute(low(pair), -2, (2,))
    own = jnp.where(z == 1, one, jnp.where(z == 2, two, three))
    return jnp.where(z == 0, added(pair, far), added(own, up, down))


def shards(params, first_moment, second_moment, inputs, segments, live_mask, out_grad):
    is_decoder = lax.axis_index("section") == 1
    me = lax.axis_index("batch")
    n = lax.axis_size("batch")
    share = params.shape[1]
    rows = 16 * (share // TILE + 2)
    shift = lax.rem(me * (share % TILE), TILE)[None]
    x = inputs[0]
    t = x.shape[0]
    count = t // ROW

    own = shifted(shift, params, share, rows)
    pieces = lax.all_gather(own, "batch", axis=0, tiled=False)
    fq, fk_src, fk_tgt = mask_features(segments, live_mask)
    fk_self = jnp.where(is_decoder, fk_tgt, fk_src)
    pieces, fq, fk_src, fk_self = lax.optimization_barrier((pieces, fq, fk_src, fk_self))
    *mats, vec_rows = split_weights(pieces, n, share)
    w = dict(zip(MATS, mats))
    vec = vec_rows[:24].astype(F32).reshape(6, D)

    def nothing():
        return {}

    flag = is_decoder.astype(jnp.int32)[None]
    fwd = [self_fwd(flag, 0, x, w, fq, fk_self)]
    _, first = either(is_decoder, nothing, lambda: enc_ffn(fwd[0]["r1"], w, vec))
    kv_in = passed_along(first["kv"], "section", 1)
    fwd += [self_fwd(flag, r, x, w, fq, fk_self) for r in range(1, count)]
    kept = [first]

    def dec_row(row, kv):
        return dec_call(row, fwd[row]["r1"], kv, out_grad, w, vec, fq, fk_src)

    def enc_row(row, grad_kv):
        return enc_back(grad_kv, fwd[row]["r1"], kept[row], w, vec)

    dec_rows, enc_rows = [], []
    kvs, back = [kv_in], []
    for row in range(count):

        def enc_make():
            done = [enc_row(row - 1, back[row - 1])] if row else []
            ahead = [enc_ffn(fwd[row + 1]["r1"], w, vec)] if row + 1 < count else []
            return ahead, done

        got, (ahead, done) = either(is_decoder, lambda: dec_row(row, kvs[row]), enc_make)
        dec_rows.append(got)
        enc_rows += done
        kept += ahead
        kvs += [passed_along(k["kv"], "section", 1) for k in ahead]
        back.append(passed_along(got["gkv"], "section", -1))
    _, done = either(is_decoder, nothing, lambda: enc_row(count - 1, back[count - 1]))
    enc_rows.append(done)

    def grads_of(rows):
        return [{**made, "ctx": fwd[r]["ctx"]} for r, made in enumerate(rows)]

    enc_all = [
        {**made, "act": kept[r]["act"], "left": kept[r]["mem"], "right": back[r]} for r, made in enumerate(enc_rows)
    ]
    rest = rest_grads(flag, grads_of(enc_all), grads_of(dec_rows))
    gvec = jnp.where(is_decoder, sum(r["gvec"] for r in dec_rows), sum(r["gvec"] for r in enc_rows))
    fl_vec = jnp.pad(gvec[:6].reshape(24, 128).astype(BF), ((0, 24), (0, 0)))

    y, x_at, z = lax.rem(me // 2, 2), lax.rem(me, 2), me // 4
    place = jnp.stack([y, x_at])
    custom = n == 16
    if custom:
        early = plane_sums(pack(place, [rest, fl_vec], (1, 2, 3), REST_AT, share, rows), y, x_at)

    dxs, dqkvs = [], []
    for row in range(count):
        mine = {k: jnp.where(is_decoder, dec_rows[row][k], enc_rows[row][k]) for k in ("dr1", "dctx")}
        dx, dqkv = self_back(flag, row, mine, fwd[row], w, fq, fk_self)
        dxs.append(dx)
        dqkvs.append(dqkv)
    fl_qkv = qkv_grad(x, dqkvs)
    dx = jnp.concatenate(dxs, axis=0)
    layer_out = jnp.where(
        is_decoder,
        jnp.concatenate([r["out"] for r in dec_rows], axis=0),
        jnp.concatenate([k["mem"][:, :D] for k in kept], axis=0),
    )

    if custom:
        need = piece_row(share, 3) + rows
        late = plane_sums(pack(place, [fl_qkv, rest[: need - REST_AT]], (0,), 0, share, rows), y, x_at)
        mine = line_sums(early, late, z).reshape(rows, 128)
    else:
        spare = jnp.zeros((piece_row(share, n - 1) + rows - FLAT_ROWS, 128), BF)
        flat = jnp.concatenate([fl_qkv, rest, fl_vec[:24], spare], axis=0)
        stacked = jnp.concatenate([flat[piece_row(share, b) :][:rows] for b in range(n)], axis=0)
        mine = lax.psum_scatter(stacked, "batch", scatter_dimension=0, tiled=True).astype(F32)
    grad_share, squares = unshifted(shift, jnp.pad(mine, ((0, 8), (0, 0))), share)

    square_sum = jnp.sum(squares)
    if custom:
        square_sum = square_sum.reshape(1, 1)
        square_sum = square_sum + lax.ppermute(square_sum, "section", [(0, 1), (1, 0)])
        for step in (1, 2, 4, 8):
            square_sum = square_sum + plane_permute(square_sum, step)
        square_sum = square_sum[0, 0]
    else:
        square_sum = lax.psum(square_sum, ("section", "batch"))
    grad_norm = jnp.sqrt(square_sum)
    clip_factor = MAXNORM / jnp.maximum(grad_norm, MAXNORM)
    param_step, new_first, new_second = adam(clip_factor[None], grad_share, first_moment, second_moment, share)
    return (param_step, new_first, new_second, grad_share, layer_out[None], dx[None], grad_norm)


def solution(mesh):
    in_specs = (
        P("section", "batch"),
        P("section", "batch"),
        P("section", "batch"),
        P("section", "batch", None),
        P("batch"),
        P(None, "batch"),
        P("batch", None),
    )
    out_specs = (
        P("section", "batch"),
        P("section", "batch"),
        P("section", "batch"),
        P("section", "batch"),
        P("section", "batch", None),
        P("section", "batch", None),
        P(),
    )
    return jax.shard_map(shards, mesh=mesh, in_specs=in_specs, out_specs=out_specs, check_vma=False)
```

time: 611 us -> 428 us (0.70)
  waiting for transfers between devices: 314 us -> 155 us
  starting transfers between devices: 4.31 us -> 49.9 us
  blocking collectives: 39.9 us -> 0 us
  local copies, waits for them, and re-layouts: 56 us -> 17.7 us
  Pallas kernels: 118 us -> 148 us
  other arithmetic: 41.5 us -> 13.9 us
    reduce_scatter x1 -> x0, waiting for transfers between devices: 139 us -> none  [shards(): mine = lax.psum_scatter(stacked, 'batch', scatter_dimension=0, tiled=True)]
    ppermute x2 -> x6, waiting for transfers between devices: 71.2 us -> 15.2 us  [passed_along(): lax.ppermute(value, axis, [(source, source + steps) for source in range(f...]
    psum x1 -> x0, blocking collectives: 39.9 us -> none  [shards(): lax.psum(jnp.sum(grad_share * grad_share), ('section', 'batch'))]
    ppermute x0 -> x20, waiting for transfers between devices: none -> 37.8 us  [the longest x12 18.9 us: plane_permute(): return lax.ppermute(value, 'batch', [(i, i ^ step) for i in range(16)])]
    ppermute x0 -> x20, starting transfers between devices: none -> 36.3 us  [the longest x12 23.9 us: plane_permute(): return lax.ppermute(value, 'batch', [(i, i ^ step) for i in range(16)])]
    pallas_call x5 -> x23, Pallas kernels: 118 us -> 148 us  [kernel_call(): return lambda *operands: tuple(call(*operands))]
    broadcast_in_dim x6 -> x0, local copies, waits for them, and re-layouts: 20.1 us -> none  [the longest x1 5.05 us: shards(): param_step[None]]
    unnamed x5 -> x0, other arithmetic: 15.7 us -> none
  transfers between devices with their start and end apart: 4 -> 27, of which waited for: 4 -> 16; matrix products, arithmetic and copies ran while one was open for 3% -> 3% of each run, Pallas kernels for 0% -> 9%
where the time goes in v2:
time: 428 us; the launch traced here: 420 us
  waiting for transfers between devices  155 us (36%)
  Pallas kernels  148 us (35%)
  starting transfers between devices  49.9 us (12%)
  between operations  20.5 us (5%)
  local copies, waits for them, and re-layouts  17.7 us (4%)
  loops' own time  14.6 us (3%)
  other arithmetic  13.9 us (3%)
    pallas_call x23, Pallas kernels, kernel_call(): return lambda *operands: tuple(call(*operands))  148 us
    all_gather x1, waiting for transfers between devices, shards(): pieces = lax.all_gather(own, 'batch', axis=0, tiled=False)  102 us
    ppermute x12, starting transfers between devices, plane_permute(): return lax.ppermute(value, 'batch', [(i, i ^ step) for i in range(16)])  23.9 us
    ppermute x12, waiting for transfers between devices, plane_permute(): return lax.ppermute(value, 'batch', [(i, i ^ step) for i in range(16)])  18.9 us
    ppermute x7, waiting for transfers between devices, line_permute(): return lax.ppermute(value, 'batch', pairs)  17.7 us
    ppermute x6, waiting for transfers between devices, passed_along(): lax.ppermute(value, axis, [(source, source + steps) for source in range(f...  15.2 us
    unnamed x114, local copies, waits for them, and re-layouts  14.8 us
    another operation x5, loops' own time, either(): got = lax.cond(is_decoder, branch(1), branch(0))  14.6 us
  transfers between devices with their start and end apart: 27, of which 16 were waited for; matrix products, arithmetic and copies ran while one was open for 3% of the time, Pallas kernels for 9%

profile of v2, /device:TPU:0, one launch (start us, length us, event | category | flops | bytes accessed | tf_op | source)
XLA Modules:
  0.0 420.1 jit_solution(17354471720735511035)
XLA Ops:
  8.4 2.7 shard_map.126
  11.3 1.6 fusion.8.fq
  12.8 2.3 select_convert_fusion.1
  16.6 102.1 %all-gather.3.cloned.1.call-done = bf16[29184,128]{1,0:T(8,128)(2,1)} async-done(((bf16[1824,128]{1,0:T(8,128)(2,1)}), bf16[29184,128]{1,0:T(8,128)(2,1)}) %all-gather.3.cloned.1.call-update) | async-done | bytes 7471120 | tf_op jit(solution)/shard_map/all_gather | solution.py:923
  118.7 8.6 %shard_map.127 = (bf16[512,1536]{1,0:T(8,128)(2,1)S(1)}, bf16[512,512]{1,0:T(8,128)(2,1)}, bf16[512,1024]{1,0:T(8,128)(2,1)}, bf16[512,2048]{1,0:T(8,128)(2,1)},...) custom-call(bf16[16,1824,128]{2,1,0:T(8,128)(2,1)} %bitcast.86), custom_call_target="tpu_custom_call" | custom-call | flops 1000000000 | tf_op jit(solution)/shard_map/pallas_call | solution.py:598
  128.0 6.4 %shard_map.129 = (bf16[512,1536]{1,0:T(8,128)(2,1)S(1)}, bf16[512,512]{1,0:T(8,128)(2,1)S(1)}, f32[8,512]{1,0:T(8,128)S(1)}, f32[512,512]{1,0:T(8,128)}) custom-call(s32[1]{0:T(128)} %bitcast.4.causal_ref.dec_ref, bf16[1536,512]{1,0:T(8,128)(2,1)S(1)} %bitcast.82, bf16[512,1536]{1,0:T(8,128)(2,1)S(1)} %get-tuple-element.380.wqkv, ...), custom_call_target="tpu_custom_call" | custom-call | flops 5000000000 | tf_op jit(solution)/shard_map/pallas_call | solution.py:598
  137.0 10.8 %conditional.5 = ((bf16[512,2048]{1,0:T(8,128)(2,1)}, bf16[512,1024]{1,0:T(8,128)(2,1)}, bf16[512,1024]{1,0:T(8,128)(2,1)}, f32[512,512]{1,0:T(8,128)}, bf16[512,2048]{1,0:T(8,128)(2,1)})) conditional(s32[]{:T(128)} %convert_element_type.283, (f32[512,512]{1,0:T(8,128)}, f32[6,512]{1,0:T(8,128)S(1)}, bf16[512,2048]{1,0:T(8,128)(2,1)S(1)}, ...), branch_computations={%region_0.1_spmd, %region_1.2_spmd} | conditional | flops 10000000000 | bytes 48 | solution.py:857
  137.2 10.5 %branch_0_fun.9 = (bf16[512,1024]{1,0:T(8,128)(2,1)}, bf16[512,1024]{1,0:T(8,128)(2,1)}, bf16[512,2048]{1,0:T(8,128)(2,1)}, bf16[512,2048]{1,0:T(8,128)(2,1)}, f32[512,512]{1,0:T(8,128)}) custom-call(f32[512,512]{1,0:T(8,128)} %get-tuple-element.136.r1_ref, f32[6,512]{1,0:T(8,128)S(1)} %get-tuple-element.137.vec, ...), custom_call_target="tpu_custom_call" | custom-call | flops 10000000000 | tf_op jit(solution)/shard_map/cond/branch_0_fun/pallas_call | solution.py:598
  147.7 2.3 collective-permute-start
  150.0 6.3 %shard_map.128 = (bf16[512,1536]{1,0:T(8,128)(2,1)S(1)}, bf16[512,512]{1,0:T(8,128)(2,1)S(1)}, f32[8,512]{1,0:T(8,128)S(1)}, f32[512,512]{1,0:T(8,128)}) custom-call(s32[1]{0:T(128)} %bitcast.4.causal_ref.dec_ref, bf16[1536,512]{1,0:T(8,128)(2,1)S(1)} %bitcast.83, bf16[512,1536]{1,0:T(8,128)(2,1)S(1)} %get-tuple-element.380.wqkv, ...), custom_call_target="tpu_custom_call" | custom-call | flops 5000000000 | tf_op jit(solution)/shard_map/pallas_call | solution.py:598
  158.9 19.4 %conditional.6 = (bf16[512,2048]{1,0:T(8,128)(2,1)}, bf16[512,1024]{1,0:T(8,128)(2,1)}, bf16[512,1024]{1,0:T(8,128)(2,1)}, f32[512,512]{1,0:T(8,128)}, bf16[512,...) conditional(s32[]{:T(128)} %convert_element_type.283, ...), branch_computations={%region_2.3_spmd, %region_3.4_spmd} | conditional | flops 23000000512 | bytes 88 | solution.py:857
  158.9 12.1 %branch_0_fun.10 = (bf16[512,1024]{1,0:T(8,128)(2,1)}, bf16[512,1024]{1,0:T(8,128)(2,1)}, bf16[512,2048]{1,0:T(8,128)(2,1)}, bf16[512,2048]{1,0:T(8,128)(2,1)}, f32[512,512]{1,0:T(8,128)}) custom-call(f32[512,512]{1,0:T(8,128)} %get-tuple-element.146.r1_ref, f32[6,512]{1,0:T(8,128)S(1)} %get-tuple-element.147.vec, ...), custom_call_target="tpu_custom_call" | custom-call | flops 10000000000 | tf_op jit(solution)/shard_map/cond/branch_0_fun/pallas_call | solution.py:598
  178.3 2.6 collective-permute-start.2
  182.2 6.3 %shard_map.130 = (bf16[512,1536]{1,0:T(8,128)(2,1)S(1)}, bf16[512,512]{1,0:T(8,128)(2,1)S(1)}, f32[8,512]{1,0:T(8,128)S(1)}, f32[512,512]{1,0:T(8,128)}) custom-call(s32[1]{0:T(128)} %bitcast.4.causal_ref.dec_ref, bf16[1536,512]{1,0:T(8,128)(2,1)S(1)} %bitcast.84, bf16[512,1536]{1,0:T(8,128)(2,1)S(1)} %get-tuple-element.380.wqkv, ...), custom_call_target="tpu_custom_call" | custom-call | flops 5000000000 | tf_op jit(solution)/shard_map/pallas_call | solution.py:598
  191.0 23.5 %conditional.7 = (bf16[512,2048]{1,0:T(8,128)(2,1)}, bf16[512,1024]{1,0:T(8,128)(2,1)}, bf16[512,1024]{1,0:T(8,128)(2,1)}, f32[512,512]{1,0:T(8,128)}, bf16[512,...) conditional(s32[]{:T(128)} %convert_element_type.283, ...), branch_computations={%region_4.5_spmd, %region_5.6_spmd} | conditional | flops 24000000000 | bytes 4194436 | solution.py:857
  191.1 9.9 %branch_0_fun.13 = (f32[512,512]{1,0:T(8,128)S(1)}, bf16[512,512]{1,0:T(8,128)(2,1)}, bf16[512,2048]{1,0:T(8,128)(2,1)}, bf16[512,512]{1,0:T(8,128)(2,1)}, bf16[512,512]{1,0:T(8,128)(2,1)}, /*index=5*/f32[8,512]{1,0:T(8,128)}) custom-call(bf16[512,1024]{1,0:T(8,128)(2,1)} %get-tuple-element.193.gkv_ref, f32[512,512]{1,0:T(8,128)} %get-tuple-element.194.r1_ref, ...), custom_call_target="tpu_custom_call" | custom-call | flops 10000000000 | tf_op jit(solution)/shard_map/cond/branch_0_fun/pallas_call | solution.py:598
  200.9 10.5 %branch_0_fun.12 = (bf16[512,1024]{1,0:T(8,128)(2,1)}, bf16[512,1024]{1,0:T(8,128)(2,1)}, bf16[512,2048]{1,0:T(8,128)(2,1)}, bf16[512,2048]{1,0:T(8,128)(2,1)}, f32[512,512]{1,0:T(8,128)}) custom-call(f32[512,512]{1,0:T(8,128)} %get-tuple-element.183.r1_ref, f32[6,512]{1,0:T(8,128)S(1)} %get-tuple-element.184.vec, ...), custom_call_target="tpu_custom_call" | custom-call | flops 10000000000 | tf_op jit(solution)/shard_map/cond/branch_0_fun/pallas_call | solution.py:598
  214.5 4.9 %collective-permute-start.4 = (bf16[512,1024]{1,0:T(8,128)(2,1)}, bf16[512,1024]{1,0:T(8,128)(2,1)S(1)}, u32[]{:S(2)}, u32[]{:S(2)}) collective-permute-start(bf16[512,1024]{1,0:T(8,128)(2,1)} %get-tuple-element.404), channel_id=1, source_target_pairs={{0,16},{1,17},{2,18},{3,19},{4,20},{5,21},{6,22},{7,23},{8,24},{9,... | collective-permute-start | bytes 3145736 | tf_op jit(solution)/shard_map/ppermute | solution.py:820
  221.8 2.5 collective-permute-done.3.refs_16_
  224.3 14.9 %conditional.8 = (bf16[512,512]{1,0:T(8,128)(2,1)}, bf16[512,512]{1,0:T(8,128)(2,1)}, f32[512,512]{1,0:T(8,128)}, bf16[512,2048]{1,0:T(8,128)(2,1)}, f32[8,512]{...) conditional(s32[]{:T(128)} %convert_element_type.283, ...), branch_computations={%region_6.7_spmd, %region_7.8_spmd} | conditional | flops 23000000512 | bytes 88 | solution.py:857
  224.3 10.9 %branch_0_fun.15 = (f32[512,512]{1,0:T(8,128)}, bf16[512,512]{1,0:T(8,128)(2,1)}, bf16[512,2048]{1,0:T(8,128)(2,1)}, bf16[512,512]{1,0:T(8,128)(2,1)}, bf16[512,512]{1,0:T(8,128)(2,1)}, /*index=5*/f32[8,512]{1,0:T(8,128)}) custom-call(bf16[512,1024]{1,0:T(8,128)(2,1)} %get-tuple-element.229.gkv_ref, f32[512,512]{1,0:T(8,128)} %get-tuple-element.230.r1_ref, ...), custom_call_target="tpu_custom_call" | custom-call | flops 10000000000 | tf_op jit(solution)/shard_map/cond/branch_0_fun/pallas_call | solution.py:598
  241.7 11.6 %collective-permute-done.5.refs_17_ = bf16[512,1024]{1,0:T(8,128)(2,1)} collective-permute-done((bf16[512,1024]{1,0:T(8,128)(2,1)}, bf16[512,1024]{1,0:T(8,128)(2,1)}, u32[]{:S(2)}, u32[]{:S(2)}) %collective-permute-start.5) | collective-permute-done | bytes 1048608 | tf_op jit(solution)/shard_map/ppermute | solution.py:820
  253.3 10.4 %conditional.9 = ((bf16[512,512]{1,0:T(8,128)(2,1)}, bf16[512,512]{1,0:T(8,128)(2,1)}, f32[512,512]{1,0:T(8,128)}, bf16[512,2048]{1,0:T(8,128)(2,1)}, f32[8,512]{1,0:T(8,128)S(1)}, /*index=5*/bf16[512,512]{1,0:T(8,128)(2,1)})) conditional(s32[]{:T(128)} %convert_element_type.283, (bf16[512,1024]{1,0:T(8,128)(2,1)}, f32[512,512]{1,0:T(8,128)}, ...), branch_computations={%region_8.9_spmd, %region_9.10_spmd} | conditional | flops 10000000000 | bytes 56 | solution.py:857
  253.3 10.4 %branch_0_fun.17 = (f32[512,512]{1,0:T(8,128)}, bf16[512,512]{1,0:T(8,128)(2,1)}, bf16[512,2048]{1,0:T(8,128)(2,1)}, bf16[512,512]{1,0:T(8,128)(2,1)}, bf16[512,512]{1,0:T(8,128)(2,1)}, /*index=5*/f32[8,512]{1,0:T(8,128)S(1)}) custom-call(bf16[512,1024]{1,0:T(8,128)(2,1)} %get-tuple-element.270.gkv_ref, f32[512,512]{1,0:T(8,128)} %get-tuple-element.271.r1_ref, ...), custom_call_target="tpu_custom_call" | custom-call | flops 10000000000 | tf_op jit(solution)/shard_map/cond/branch_0_fun/pallas_call | solution.py:598
  263.8 2.0 broadcast_select_fusion.1
  265.8 20.4 %shard_map.135.refs_0_ = bf16[22528,128]{1,0:T(8,128)(2,1)} custom-call(s32[1]{0:T(128)} %bitcast.4.causal_ref.dec_ref, bf16[512,512]{1,0:T(8,128)(2,1)S(1)} %copy-done.57, bf16[512,512]{1,0:T(8,128)(2,1)} %get-tuple-element.419.refs_1_.refs_26_, bf16[512,512]{1,0:T(8,128)(2,1)} %get-tuple-element.420.refs_2_, bf16[512,2048]{1,0:T(8,128)(2,1)} %get-tuple-element.421.refs_3_, ...), custom_call_target="tpu_custom_call" | custom-call | flops 17999998976 | tf_op jit(solution)/shard_map/pallas_call | solution.py:598
  286.1 2.6 copy-done
  294.4 6.8 %shard_map.133 = (bf16[512,512]{1,0:T(8,128)(2,1)S(1)}, bf16[512,1536]{1,0:T(8,128)(2,1)S(1)}) custom-call(s32[1]{0:T(128)} %bitcast.4.causal_ref.dec_ref, f32[512,512]{1,0:T(8,128)S(1)} %get-tuple-element.472.dr1_ref, bf16[512,512]{1,0:T(8,128)(2,1)S(1)} %get-tuple-element.474.dctx_ref, bf16[512,1536]{1,0:T(8,128)(2,1)S(1)} %copy-done.17, ...), custom_call_target="tpu_custom_call" | custom-call | flops 8000000000 | tf_op jit(solution)/shard_map/pallas_call | solution.py:598
  301.2 6.6 %shard_map.132 = (bf16[512,512]{1,0:T(8,128)(2,1)S(1)}, bf16[512,1536]{1,0:T(8,128)(2,1)S(1)}) custom-call(s32[1]{0:T(128)} %bitcast.4.causal_ref.dec_ref, f32[512,512]{1,0:T(8,128)S(1)} %get-tuple-element.473.dr1_ref, bf16[512,512]{1,0:T(8,128)(2,1)S(1)} %get-tuple-element.475.dctx_ref, bf16[512,1536]{1,0:T(8,128)(2,1)S(1)} %copy-done.15, ...), custom_call_target="tpu_custom_call" | custom-call | flops 8000000000 | tf_op jit(solution)/shard_map/pallas_call | solution.py:598
  307.9 6.0 %collective-permute-done.12 = bf16[3,2,912,128]{3,2,0,1:T(8,128)(2,1)S(1)} collective-permute-done((bf16[3,2,912,128]{3,2,0,1:T(8,128)(2,1)S(1)}, bf16[3,2,912,128]{3,2,0,1:T(8,128)(2,1)S(1)}, u32[]{:S(2)}, u32[]{:S(2)}) %collective-permute-start.12) | collective-permute-done | bytes 1400864 | tf_op jit(solution)/shard_map/ppermute | solution.py:863
  315.6 6.8 %shard_map.131 = (bf16[512,512]{1,0:T(8,128)(2,1)S(1)}, bf16[512,1536]{1,0:T(8,128)(2,1)S(1)}) custom-call(s32[1]{0:T(128)} %bitcast.4.causal_ref.dec_ref, f32[512,512]{1,0:T(8,128)S(1)} %broadcast_select_fusion.5.dr1_ref, bf16[512,512]{1,0:T(8,128)(2,1)S(1)} %get-tuple-element.476.dctx_ref, bf16[512,1536]{1,0:T(8,128)(2,1)S(1)} %copy-done.13, ...), custom_call_target="tpu_custom_call" | custom-call | flops 8000000000 | tf_op jit(solution)/shard_map/pallas_call | solution.py:598
  324.4 4.7 %shard_map.134.refs_0_ = bf16[6144,128]{1,0:T(8,128)(2,1)S(1)} custom-call(bf16[1536,512]{1,0:T(8,128)(2,1)S(1)} %bitcast.85, bf16[512,1536]{1,0:T(8,128)(2,1)S(1)} %get-tuple-element.402.refs_0_, bf16[512,1536]{1,0:T(8,128)(2,1)S(1)} %get-tuple-element.410.refs_1_, bf16[512,1536]{1,0:T(8,128)(2,1)S(1)} %get-tuple-element.417.refs_2_), custom_call_target="tpu_custom_call" | custom-call | flops 5000000000 | tf_op jit(solution)/shard_map/pallas_call | solution.py:598
  332.0 5.2 %collective-permute-done.13 = bf16[3,912,128]{2,1,0:T(8,128)(2,1)S(1)} collective-permute-done((bf16[3,912,128]{2,1,0:T(8,128)(2,1)S(1)}, bf16[3,912,128]{2,1,0:T(8,128)(2,1)S(1)}, u32[]{:S(2)}, u32[]{:S(2)}) %collective-permute-start.13) | collective-permute-done | bytes 700448 | tf_op jit(solution)/shard_map/ppermute | solution.py:863
  337.8 2.6 collective-permute-start.16
  340.5 3.3 collective-permute-done.6
  344.5 1.6 collective-permute-start.9
  346.9 4.4 %collective-permute-start.17 = (bf16[2,912,128]{2,1,0:T(8,128)(2,1)S(1)}, bf16[2,912,128]{2,1,0:T(8,128)(2,1)S(1)}, u32[]{:S(2)}, u32[]{:S(2)}) collective-permute-start(bf16[2,912,128]{2,1,0:T(8,128)(2,1)S(1)} %get-tuple-element.470), channel_id=1, source_target_pairs={{0,4},{1,5},{2,6},{3,7},{4,8},{5,9},{6,10},{7,11},{16,20},{17,21},... | collective-permute-start | bytes 1400840 | tf_op jit(solution)/shard_map/ppermute | solution.py:868
  352.9 7.8 %collective-permute-done.17 = bf16[2,912,128]{2,1,0:T(8,128)(2,1)S(1)} collective-permute-done((bf16[2,912,128]{2,1,0:T(8,128)(2,1)S(1)}, bf16[2,912,128]{2,1,0:T(8,128)(2,1)S(1)}, u32[]{:S(2)}, u32[]{:S(2)}) %collective-permute-start.17) | collective-permute-done | bytes 466976 | tf_op jit(solution)/shard_map/ppermute | solution.py:868
  362.0 4.3 %collective-permute-done.10 = bf16[2,912,128]{2,1,0:T(8,128)(2,1)S(1)} collective-permute-done((bf16[2,912,128]{2,1,0:T(8,128)(2,1)S(1)}, bf16[2,912,128]{2,1,0:T(8,128)(2,1)S(1)}, u32[]{:S(2)}, u32[]{:S(2)}) %collective-permute-start.10) | collective-permute-done | bytes 466976 | tf_op jit(solution)/shard_map/ppermute | solution.py:868
  370.0 1.6 maximum_select_fusion
  372.9 5.0 %collective-permute-done.11 = bf16[2,912,128]{2,1,0:T(8,128)(2,1)S(1)} collective-permute-done((bf16[2,912,128]{2,1,0:T(8,128)(2,1)S(1)}, bf16[2,912,128]{2,1,0:T(8,128)(2,1)S(1)}, u32[]{:S(2)}, u32[]{:S(2)}) %collective-permute-start.11) | collective-permute-done | bytes 466976 | tf_op jit(solution)/shard_map/ppermute | solution.py:868
  378.4 3.4 shard_map.138
  384.9 2.2 collective-permute-start.22
  389.2 2.3 collective-permute-start.23
  393.4 8.0 %collective-permute-start.24 = (f32[1,1]{1,0:T(1,128)}, f32[1,1]{1,0:T(1,128)}, u32[]{:S(2)}, u32[]{:S(2)}) collective-permute-start(f32[1,1]{1,0:T(1,128)} %add.292), channel_id=1, source_target_pairs={{0,4},{1,5},{2,6},{3,7},{4,0},{5,1},{6,2},{7,3},{8,12},{9,13},{10,... | collective-permute-start | bytes 20 | tf_op jit(solution)/shard_map/ppermute | solution.py:863
  402.3 2.8 collective-permute-start.25
  405.2 1.6 collective-permute-done.25
  408.8 3.1 shard_map.139
  (193 shorter events, 45.9 us)
Async XLA Ops:
  7.2 111.6 %all-gather.3.cloned.1.call-start = ((), (), s32[]{:S(2)}) async-start(), calls=%async_computation | async-start | bytes 7938048 | tf_op jit(solution)/shard_map/all_gather | solution.py:923
  118.7 9.2 %copy-start.1 = (bf16[1,1536,512]{2,1,0:T(8,128)(2,1)S(1)}, bf16[1,1536,512]{2,1,0:T(8,128)(2,1)}, u32[]{:S(2)}) copy-start(bf16[1,1536,512]{2,1,0:T(8,128)(2,1)} %param.20) | copy-start | bytes 4718596
  127.3 54.9 %copy-start.3 = (bf16[512,1536]{1,0:T(8,128)(2,1)}, bf16[512,1536]{1,0:T(8,128)(2,1)S(1)}, u32[]{:S(2)}) copy-start(bf16[512,1536]{1,0:T(8,128)(2,1)S(1)} %get-tuple-element.380.wqkv) | copy-start | bytes 4718596
  128.0 9.0 %copy-start.47 = (bf16[512,2048]{1,0:T(8,128)(2,1)S(1)}, bf16[512,2048]{1,0:T(8,128)(2,1)}, u32[]{:S(2)}) copy-start(bf16[512,2048]{1,0:T(8,128)(2,1)} %get-tuple-element.386) | copy-start | bytes 6291460
  128.0 9.0 %copy-start.50 = (bf16[2048,512]{1,0:T(8,128)(2,1)S(1)}, bf16[2048,512]{1,0:T(8,128)(2,1)}, u32[]{:S(2)}) copy-start(bf16[2048,512]{1,0:T(8,128)(2,1)} %get-tuple-element.387) | copy-start | bytes 6291460
  147.7 11.2 %collective-permute-start = (bf16[512,1024]{1,0:T(8,128)(2,1)}, bf16[512,1024]{1,0:T(8,128)(2,1)}, u32[]{:S(2)}, u32[]{:S(2)}) collective-permute-start(bf16[512,1024]{1,0:T(8,128)(2,1)} %get-tuple-element.390), channel_id=1, source_target_pairs={{0,16},{1,17},{2,18},{3,19},{4,20},{5,21},{6,22},{7,23},{8,24},{9,... | collective-permute-start | bytes 3145736 | tf_op jit(solution)/shard_map/ppermute | solution.py:820
  178.3 12.7 %copy-start.41 = (f32[6,512]{1,0:T(8,128)S(1)}, f32[6,512]{1,0:T(8,128)}, u32[]{:S(2)}) copy-start(f32[6,512]{1,0:T(8,128)} %reshape.380) | copy-start | bytes 36868
  178.3 12.7 %copy-start.48 = (bf16[512,2048]{1,0:T(8,128)(2,1)S(1)}, bf16[512,2048]{1,0:T(8,128)(2,1)}, u32[]{:S(2)}) copy-start(bf16[512,2048]{1,0:T(8,128)(2,1)} %get-tuple-element.386) | copy-start | bytes 6291460
  178.3 12.7 %copy-start.51 = (bf16[2048,512]{1,0:T(8,128)(2,1)S(1)}, bf16[2048,512]{1,0:T(8,128)(2,1)}, u32[]{:S(2)}) copy-start(bf16[2048,512]{1,0:T(8,128)(2,1)} %get-tuple-element.387) | copy-start | bytes 6291460
  178.3 12.7 %copy-start.55 = (bf16[512,512]{1,0:T(8,128)(2,1)S(1)}, bf16[512,512]{1,0:T(8,128)(2,1)}, u32[]{:S(2)}) copy-start(bf16[512,512]{1,0:T(8,128)(2,1)} %get-tuple-element.381.wout) | copy-start | bytes 1572868
  178.3 12.7 %collective-permute-start.2 = (bf16[512,1024]{1,0:T(8,128)(2,1)}, bf16[512,1024]{1,0:T(8,128)(2,1)}, u32[]{:S(2)}, u32[]{:S(2)}) collective-permute-start(bf16[512,1024]{1,0:T(8,128)(2,1)} %get-tuple-element.394), channel_id=1, source_target_pairs={{0,16},{1,17},{2,18},{3,19},{4,20},{5,21},{6,22},{7,23},{8,24},{9,... | collective-permute-start | bytes 3145736 | tf_op jit(solution)/shard_map/ppermute | solution.py:820
  180.9 10.1 %collective-permute-start.1 = (bf16[512,1024]{1,0:T(8,128)(2,1)}, bf16[512,1024]{1,0:T(8,128)(2,1)}, u32[]{:S(2)}, u32[]{:S(2)}) collective-permute-start(bf16[512,1024]{1,0:T(8,128)(2,1)} %get-tuple-element.394), channel_id=1, source_target_pairs={{16,0},{17,1},{18,2},{19,3},{20,4},{21,5},{22,6},{23,7},{24,8},{25... | collective-permute-start | bytes 3145736 | tf_op jit(solution)/shard_map/ppermute | solution.py:820
  191.0 33.3 %copy-start.26 = (f32[512,512]{1,0:T(8,128)S(1)}, f32[512,512]{1,0:T(8,128)}, u32[]{:S(2)}) copy-start(f32[512,512]{1,0:T(8,128)} %get-tuple-element.392.refs_33_) | copy-start | bytes 3145732
  191.0 9.9 %copy-start.53 = (bf16[512,1024]{1,0:T(8,128)(2,1)S(1)}, bf16[512,1024]{1,0:T(8,128)(2,1)}, u32[]{:S(2)}) copy-start(bf16[512,1024]{1,0:T(8,128)(2,1)} %get-tuple-element.187.w_cross) | copy-start | bytes 3145732 | tf_op jit(solution)/shard_map/cond
  214.5 27.0 %copy-start.25 = (f32[512,512]{1,0:T(8,128)}, f32[512,512]{1,0:T(8,128)S(1)}, u32[]{:S(2)}) copy-start(f32[512,512]{1,0:T(8,128)S(1)} %get-tuple-element.397.refs_9_) | copy-start | bytes 3145732
  214.5 7.3 %collective-permute-start.4 = (bf16[512,1024]{1,0:T(8,128)(2,1)}, bf16[512,1024]{1,0:T(8,128)(2,1)S(1)}, u32[]{:S(2)}, u32[]{:S(2)}) collective-permute-start(bf16[512,1024]{1,0:T(8,128)(2,1)} %get-tuple-element.404), channel_id=1, source_target_pairs={{0,16},{1,17},{2,18},{3,19},{4,20},{5,21},{6,22},{7,23},{8,24},{9,... | collective-permute-start | bytes 3145736 | tf_op jit(solution)/shard_map/ppermute | solution.py:820
  219.4 4.9 %collective-permute-start.3 = (bf16[512,1024]{1,0:T(8,128)(2,1)}, bf16[512,1024]{1,0:T(8,128)(2,1)}, u32[]{:S(2)}, u32[]{:S(2)}) collective-permute-start(bf16[512,1024]{1,0:T(8,128)(2,1)} %get-tuple-element.404), channel_id=1, source_target_pairs={{16,0},{17,1},{18,2},{19,3},{20,4},{21,5},{22,6},{23,7},{24,8},{25... | collective-permute-start | bytes 3145736 | tf_op jit(solution)/shard_map/ppermute | solution.py:820
  224.3 16.3 %copy-start.38 = (bf16[512,1024]{1,0:T(8,128)(2,1)S(1)}, bf16[512,1024]{1,0:T(8,128)(2,1)}, u32[]{:S(2)}) copy-start(bf16[512,1024]{1,0:T(8,128)(2,1)} %get-tuple-element.427.refs_12_) | copy-start | bytes 3145732
  239.2 14.1 %collective-permute-start.5 = (bf16[512,1024]{1,0:T(8,128)(2,1)}, bf16[512,1024]{1,0:T(8,128)(2,1)}, u32[]{:S(2)}, u32[]{:S(2)}) collective-permute-start(bf16[512,1024]{1,0:T(8,128)(2,1)} %get-tuple-element.411), channel_id=1, source_target_pairs={{16,0},{17,1},{18,2},{19,3},{20,4},{21,5},{22,6},{23,7},{24,8},{25... | collective-permute-start | bytes 3145736 | tf_op jit(solution)/shard_map/ppermute | solution.py:820
  240.6 12.7 %copy-start.49 = (bf16[512,2048]{1,0:T(8,128)(2,1)S(1)}, bf16[512,2048]{1,0:T(8,128)(2,1)}, u32[]{:S(2)}) copy-start(bf16[512,2048]{1,0:T(8,128)(2,1)} %get-tuple-element.386) | copy-start | bytes 6291460
  241.5 11.8 %copy-start.27 = (f32[512,512]{1,0:T(8,128)S(1)}, f32[512,512]{1,0:T(8,128)}, u32[]{:S(2)}) copy-start(f32[512,512]{1,0:T(8,128)} %get-tuple-element.403.refs_34_) | copy-start | bytes 3145732
  241.5 11.8 %copy-start.42 = (f32[6,512]{1,0:T(8,128)S(1)}, f32[6,512]{1,0:T(8,128)}, u32[]{:S(2)}) copy-start(f32[6,512]{1,0:T(8,128)} %reshape.380) | copy-start | bytes 36868
  241.5 11.8 %copy-start.56 = (bf16[512,512]{1,0:T(8,128)(2,1)S(1)}, bf16[512,512]{1,0:T(8,128)(2,1)}, u32[]{:S(2)}) copy-start(bf16[512,512]{1,0:T(8,128)(2,1)} %get-tuple-element.381.wout) | copy-start | bytes 1572868
  253.3 10.4 %copy-start.43 = (f32[8,512]{1,0:T(8,128)S(1)}, f32[8,512]{1,0:T(8,128)}, u32[]{:S(2)}) copy-start(f32[8,512]{1,0:T(8,128)} %get-tuple-element.448) | copy-start | bytes 49156
  253.3 10.4 %copy-start.44 = (f32[8,512]{1,0:T(8,128)S(1)}, f32[8,512]{1,0:T(8,128)}, u32[]{:S(2)}) copy-start(f32[8,512]{1,0:T(8,128)} %get-tuple-element.447) | copy-start | bytes 49156
  253.3 10.4 %copy-start.45 = (f32[8,512]{1,0:T(8,128)S(1)}, f32[8,512]{1,0:T(8,128)}, u32[]{:S(2)}) copy-start(f32[8,512]{1,0:T(8,128)} %get-tuple-element.449) | copy-start | bytes 49156
  290.2 23.7 %collective-permute-start.12 = (bf16[3,2,912,128]{3,2,0,1:T(8,128)(2,1)S(1)}, bf16[3,2,912,128]{3,2,0,1:T(8,128)(2,1)S(1)}, u32[]{:S(2)}, u32[]{:S(2)}) collective-permute-start(bf16[3,2,912,128]{3,2,0,1:T(8,128)(2,1)S(1)} %copy.15), channel_id=1, source_target_pairs={{0,2},{1,3},{2,0},{3,1},{4,6},{5,7},{6,4},{7,5},{8,10},{9,11},{10,... | collective-permute-start | bytes 4202504 | tf_op jit(solution)/shard_map/ppermute | solution.py:863
  291.8 31.7 %collective-permute-start.14 = (bf16[3,2,912,128]{3,2,0,1:T(8,128)(2,1)S(1)}, bf16[3,2,912,128]{3,2,0,1:T(8,128)(2,1)S(1)}, u32[]{:S(2)}, u32[]{:S(2)}) collective-permute-start(bf16[3,2,912,128]{3,2,0,1:T(8,128)(2,1)S(1)} %copy.18), channel_id=1, source_target_pairs={{0,1},{1,0},{2,3},{3,2},{4,5},{5,4},{6,7},{7,6},{8,9},{9,8},{10,11... | collective-permute-start | bytes 4202504 | tf_op jit(solution)/shard_map/ppermute | solution.py:863
  314.0 23.1 %collective-permute-start.13 = (bf16[3,912,128]{2,1,0:T(8,128)(2,1)S(1)}, bf16[3,912,128]{2,1,0:T(8,128)(2,1)S(1)}, u32[]{:S(2)}, u32[]{:S(2)}) collective-permute-start(bf16[3,912,128]{2,1,0:T(8,128)(2,1)S(1)} %fusion.11), channel_id=1, source_target_pairs={{0,1},{1,0},{2,3},{3,2},{4,5},{5,4},{6,7},{7,6},{8,9},{9,8},{10,11... | collective-permute-start | bytes 2101256 | tf_op jit(solution)/shard_map/ppermute | solution.py:863
  323.7 13.7 %collective-permute-start.15 = (bf16[3,912,128]{2,1,0:T(8,128)(2,1)S(1)}, bf16[3,912,128]{2,1,0:T(8,128)(2,1)S(1)}, u32[]{:S(2)}, u32[]{:S(2)}) collective-permute-start(bf16[3,912,128]{2,1,0:T(8,128)(2,1)S(1)} %fusion.14), channel_id=1, source_target_pairs={{0,2},{1,3},{2,0},{3,1},{4,6},{5,7},{6,4},{7,5},{8,10},{9,11},{10,... | collective-permute-start | bytes 2101256 | tf_op jit(solution)/shard_map/ppermute | solution.py:863
  329.9 13.8 %collective-permute-start.6 = (bf16[1,2,912,128]{3,2,1,0:T(8,128)(2,1)S(1)}, bf16[1,2,912,128]{3,2,1,0:T(8,128)(2,1)S(1)}, u32[]{:S(2)}, u32[]{:S(2)}) collective-permute-start(bf16[1,2,912,128]{3,2,1,0:T(8,128)(2,1)S(1)} %get-tuple-element.444), channel_id=1, source_target_pairs={{0,2},{1,3},{2,0},{3,1},{4,6},{5,7},{6,4},{7,5},{8,10},{9,11},{10,... | collective-permute-start | bytes 1400840 | tf_op jit(solution)/shard_map/ppermute | solution.py:863
  331.4 13.0 %collective-permute-start.8 = (bf16[1,2,912,128]{3,2,1,0:T(8,128)(2,1)S(1)}, bf16[1,2,912,128]{3,2,1,0:T(8,128)(2,1)S(1)}, u32[]{:S(2)}, u32[]{:S(2)}) collective-permute-start(bf16[1,2,912,128]{3,2,1,0:T(8,128)(2,1)S(1)} %get-tuple-element.446), channel_id=1, source_target_pairs={{0,1},{1,0},{2,3},{3,2},{4,5},{5,4},{6,7},{7,6},{8,9},{9,8},{10,11... | collective-permute-start | bytes 1400840 | tf_op jit(solution)/shard_map/ppermute | solution.py:863
  337.8 8.8 %collective-permute-start.16 = (bf16[2,912,128]{2,1,0:T(8,128)(2,1)S(1)}, bf16[2,912,128]{2,1,0:T(8,128)(2,1)S(1)}, u32[]{:S(2)}, u32[]{:S(2)}) collective-permute-start(bf16[2,912,128]{2,1,0:T(8,128)(2,1)S(1)} %fusion.19), channel_id=1, source_target_pairs={{0,4},{1,5},{2,6},{3,7},{16,20},{17,21},{18,22},{19,23}} | collective-permute-start | bytes 1400840 | tf_op jit(solution)/shard_map/ppermute | solution.py:868
  343.8 7.5 %collective-permute-start.7 = (bf16[1,912,128]{2,1,0:T(8,128)(2,1)S(1)}, bf16[1,912,128]{2,1,0:T(8,128)(2,1)S(1)}, u32[]{:S(2)}, u32[]{:S(2)}) collective-permute-start(bf16[1,912,128]{2,1,0:T(8,128)(2,1)S(1)} %fusion.23), channel_id=1, source_target_pairs={{0,1},{1,0},{2,3},{3,2},{4,5},{5,4},{6,7},{7,6},{8,9},{9,8},{10,11... | collective-permute-start | bytes 700424 | tf_op jit(solution)/shard_map/ppermute | solution.py:863
  344.5 7.0 %collective-permute-start.9 = (bf16[1,912,128]{2,1,0:T(8,128)(2,1)S(1)}, bf16[1,912,128]{2,1,0:T(8,128)(2,1)S(1)}, u32[]{:S(2)}, u32[]{:S(2)}) collective-permute-start(bf16[1,912,128]{2,1,0:T(8,128)(2,1)S(1)} %fusion.24), channel_id=1, source_target_pairs={{0,2},{1,3},{2,0},{3,1},{4,6},{5,7},{6,4},{7,5},{8,10},{9,11},{10,... | collective-permute-start | bytes 700424 | tf_op jit(solution)/shard_map/ppermute | solution.py:863
  346.9 13.8 %collective-permute-start.17 = (bf16[2,912,128]{2,1,0:T(8,128)(2,1)S(1)}, bf16[2,912,128]{2,1,0:T(8,128)(2,1)S(1)}, u32[]{:S(2)}, u32[]{:S(2)}) collective-permute-start(bf16[2,912,128]{2,1,0:T(8,128)(2,1)S(1)} %get-tuple-element.470), channel_id=1, source_target_pairs={{0,4},{1,5},{2,6},{3,7},{4,8},{5,9},{6,10},{7,11},{16,20},{17,21},... | collective-permute-start | bytes 1400840 | tf_op jit(solution)/shard_map/ppermute | solution.py:868
  351.6 14.7 %collective-permute-start.10 = (bf16[2,912,128]{2,1,0:T(8,128)(2,1)S(1)}, bf16[2,912,128]{2,1,0:T(8,128)(2,1)S(1)}, u32[]{:S(2)}, u32[]{:S(2)}) collective-permute-start(bf16[2,912,128]{2,1,0:T(8,128)(2,1)S(1)} %maximum_bitcast_fusion.1), channel_id=1, source_target_pairs={{4,0},{5,1},{6,2},{7,3},{12,8},{13,9},{14,10},{15,11},{20,16},{21,... | collective-permute-start | bytes 1400840 | tf_op jit(solution)/shard_map/ppermute | solution.py:868
  361.0 8.1 %collective-permute-start.19 = (bf16[2,912,128]{2,1,0:T(8,128)(2,1)S(1)}, bf16[2,912,128]{2,1,0:T(8,128)(2,1)S(1)}, u32[]{:S(2)}, u32[]{:S(2)}) collective-permute-start(bf16[2,912,128]{2,1,0:T(8,128)(2,1)S(1)} %get-tuple-element.469), channel_id=1, source_target_pairs={{12,8},{13,9},{14,10},{15,11},{28,24},{29,25},{30,26},{31,27}} | collective-permute-start | bytes 1400840 | tf_op jit(solution)/shard_map/ppermute | solution.py:868
  366.5 11.4 %collective-permute-start.11 = (bf16[2,912,128]{2,1,0:T(8,128)(2,1)S(1)}, bf16[2,912,128]{2,1,0:T(8,128)(2,1)S(1)}, u32[]{:S(2)}, u32[]{:S(2)}) collective-permute-start(bf16[2,912,128]{2,1,0:T(8,128)(2,1)S(1)} %fusion.6), channel_id=1, source_target_pairs={{8,0},{9,1},{10,2},{11,3},{24,16},{25,17},{26,18},{27,19}} | collective-permute-start | bytes 1400840 | tf_op jit(solution)/shard_map/ppermute | solution.py:868
  367.8 10.1 %collective-permute-start.18 = (bf16[2,912,128]{2,1,0:T(8,128)(2,1)S(1)}, bf16[2,912,128]{2,1,0:T(8,128)(2,1)S(1)}, u32[]{:S(2)}, u32[]{:S(2)}) collective-permute-start(bf16[2,912,128]{2,1,0:T(8,128)(2,1)S(1)} %get-tuple-element.468), channel_id=1, source_target_pairs={{0,4},{1,5},{2,6},{3,7},{4,8},{5,9},{6,10},{7,11},{8,12},{9,13},{1... | collective-permute-start | bytes 1400840 | tf_op jit(solution)/shard_map/ppermute | solution.py:868
  369.3 8.5 %collective-permute-start.20 = (bf16[2,912,128]{2,1,0:T(8,128)(2,1)S(1)}, bf16[2,912,128]{2,1,0:T(8,128)(2,1)S(1)}, u32[]{:S(2)}, u32[]{:S(2)}) collective-permute-start(bf16[2,912,128]{2,1,0:T(8,128)(2,1)S(1)} %fusion.5), channel_id=1, source_target_pairs={{8,4},{9,5},{10,6},{11,7},{12,8},{13,9},{14,10},{15,11},{24,20},{2... | collective-permute-start | bytes 1400840 | tf_op jit(solution)/shard_map/ppermute | solution.py:868
  378.4 29.2 %copy-start.6 = (f32[1,229568]{1,0:T(1,128)S(1)}, f32[1,229568]{1,0:T(1,128)}, u32[]{:S(2)}) copy-start(f32[1,229568]{1,0:T(1,128)} %first_ref.1) | copy-start | bytes 2754820
  378.4 29.2 %copy-start.7 = (f32[1,229568]{1,0:T(1,128)S(1)}, f32[1,229568]{1,0:T(1,128)}, u32[]{:S(2)}) copy-start(f32[1,229568]{1,0:T(1,128)} %second_ref.1) | copy-start | bytes 2754820
  382.4 1.2 collective-permute-start.21
  384.9 3.6 collective-permute-start.22
  389.2 3.6 collective-permute-start.23
  393.4 8.2 %collective-permute-start.24 = (f32[1,1]{1,0:T(1,128)}, f32[1,1]{1,0:T(1,128)}, u32[]{:S(2)}, u32[]{:S(2)}) collective-permute-start(f32[1,1]{1,0:T(1,128)} %add.292), channel_id=1, source_target_pairs={{0,4},{1,5},{2,6},{3,7},{4,0},{5,1},{6,2},{7,3},{8,12},{9,13},{10,... | collective-permute-start | bytes 20 | tf_op jit(solution)/shard_map/ppermute | solution.py:863
  402.3 4.5 %collective-permute-start.25 = (f32[1,1]{1,0:T(1,128)}, f32[1,1]{1,0:T(1,128)}, u32[]{:S(2)}, u32[]{:S(2)}) collective-permute-start(f32[1,1]{1,0:T(1,128)} %add.293), channel_id=1, source_target_pairs={{0,8},{1,9},{2,10},{3,11},{4,12},{5,13},{6,14},{7,15},{8,0},{9,1},... | collective-permute-start | bytes 20 | tf_op jit(solution)/shard_map/ppermute | solution.py:863
  (37 other events, 124.2 us)
Sparse Core Ops, SparseCore 0:
  11.4 107.2 all-gather.2

commit v3 on v2

--- a/solution.py
+++ b/solution.py
@@ -388,45 +388,125 @@
     outs[5][...] = flat[VEC_AT : VEC_AT + 32, :]
 
 
-def self_fwd_kernel(causal_ref, x_ref, wqkv, wout, fq, fk, qkv_ref, ctx_ref, lse_ref, r1_ref, lse_s, tri_s):
-    x = x_ref[...]
-    qkv_ref[...] = dot_nn(x, wqkv[...]).astype(BF)
+SLOTS = ((0, 1, 2, 3), (1, 0, 3, 2), (2, 2, 0, 1), (3, 3, 1, 0))
+
+
+def place_pieces(share, z_of, y, x, halves, flat):
+    half = halves[0].shape[0]
+    for which in range(2):
+        for dy in range(2):
+            for dx in range(2):
+                piece = halves[4 * which + 2 * dy + dx]
+                b = 4 * z_of + 2 * lax.rem(y + dy, 2) + lax.rem(x + dx, 2)
+                row = pl.multiple_of(16 * ((share * b) // TILE), 16)
+                if which == 0:
+                    flat[pl.ds(row, 16), :] += piece[0:16, :]
+                    flat[pl.ds(row + 16, half - 16), :] = piece[16:half, :]
+                else:
+                    kept = 16 * (share // TILE) - half
+                    flat[pl.ds(row + half, kept), :] = piece[0:kept, :]
+                    flat[pl.ds(row + half + kept, half - kept), :] += piece[kept:half, :]
+
+
+def clear_edges(share, pieces, flat):
+    for b in pieces:
+        row = 16 * (share * b // TILE)
+        last = row + 16 * (share // TILE)
+        flat[row : row + 16, :] = jnp.zeros((16, 128), BF)
+        flat[last : last + 32, :] = jnp.zeros((32, 128), BF)
+
+
+def slot_copies(refs, kept, sems):
+    a, ax, ay, b, by, bx = refs
+    order = (a, ax, ay.at[0], ay.at[1], b, bx.at[0], by, bx.at[1])
+    return [pltpu.make_async_copy(ref, kept.at[i], sems.at[i]) for i, ref in enumerate(order)]
+
+
+def place_kernel(share, place_ref, *refs):
+    slots, outs, refs = [refs[6 * i : 6 * i + 6] for i in range(4)], refs[24:30], refs[30:]
+    mats, (vec_s, kept, flat, sems, out_sems) = refs[:5], refs[5:]
+    sent, emit = emitter(out_sems)
+    y, x = place_ref[1], place_ref[2]
+    made = [slot_copies(slot, kept.at[i], sems.at[i]) for i, slot in enumerate(slots)]
+    for some in made:
+        for one in some:
+            one.start()
+    clear_edges(share, range(16), flat)
+    for i, some in enumerate(made):
+        z_of = place_ref[3 + i]
+        for one in some:
+            one.wait()
+        place_pieces(share, z_of, y, x, [kept.at[i, j] for j in range(8)], flat)
+    for name, mat, out in zip(MATS, mats, outs):
+        to_matrix(name, flat, MATS[name][2], mat)
+        emit(mat, out)
+    vec_s[...] = flat[VEC_AT : VEC_AT + 32, :]
+    emit(vec_s, outs[5])
+    for one in sent:
+        one.wait()
+
+
+def self_fwd_kernel(causal_ref, x_ref, wqkv, fq, fk, qkv_ref, ctx_ref, lse_ref, lse_s, tri_s):
+    qkv_ref[...] = dot_nn(x_ref[...], wqkv[...]).astype(BF)
     attend_fwd(
         causal_ref[0], qkv_ref, 0, qkv_ref, D, qkv_ref, 2 * D, fq[...], fk[...], ctx_ref, lse_ref, lse_s, tri_s
     )
-    r1_ref[...] = x.astype(F32) + dot_nn(ctx_ref[...], wout[...])
-
-
-def enc_ffn_kernel(r1_ref, vec, w_up, w_down, w_cross, mem_ref, kv_ref, act_ref, slope_ref, r2_ref, hid_s, total_s):
-    hat, _ = ln_parts(r1_ref[...])
+
+
+def emitter(sems):
+    sent = []
+
+    def emit(source, target):
+        sent.append(pltpu.make_async_copy(source, target, sems.at[len(sent)]))
+        sent[-1].start()
+
+    return sent, emit
+
+
+def enc_ffn_kernel(
+    loop, x_ref, ctx_ref, vec, w_out, w_up_any, w_down_any, w_cross_any,
+    mem_ref, kv_ref, act_any, slope_any, r1_any, r2_any,
+    hid_s, total_s, act_s, slope_s, r1_s, r2_s, w_up, w_down, w_cross, in_sems, out_sems,
+):
+    made = copies((w_up_any, w_down_any, w_cross_any), (w_up, w_down, w_cross), in_sems)
+    sent, emit = emitter(out_sems)
+    r1 = x_ref[...].astype(F32) + dot_nn(ctx_ref[...], w_out[...])
+    r1_s[...] = r1
+    emit(r1_s, r1_any)
+    hat, _ = ln_parts(r1)
     y1 = hat * vec[0:1, :] + vec[1:2, :]
     hid_s[...] = y1.astype(BF)
-    r2_ref[...] = y1
-    r2 = r2_ref[...] + ffn_fwd(hid_s, w_up, w_down, act_ref, slope_ref, total_s, True)
-    r2_ref[...] = r2
+    r2_s[...] = y1
+    made[0].wait()
+    made[1].wait()
+    r2 = r2_s[...] + ffn_fwd(hid_s, w_up, w_down, act_s, slope_s, total_s, loop)
+    emit(act_s, act_any)
+    emit(slope_s, slope_any)
+    r2_s[...] = r2
+    emit(r2_s, r2_any)
     hat, _ = ln_parts(r2)
     mem = (hat * vec[2:3, :] + vec[3:4, :]).astype(BF)
     mem_ref[:, :D] = mem
     mem_ref[:, D:] = mem
+    made[2].wait()
     kv_ref[...] = dot_nn(mem, w_cross[...]).astype(BF)
+    for one in sent:
+        one.wait()
 
 
 def dec_kernel(
-    row, r1_ref, kv_ref, go_any, vec, w_cross, w_out_any, w_up_any, w_down_any, fq, fk,
+    row, x_ref, ctx1_ref, kv_ref, go_any, vec, w_cross, w_out, w_up_any, w_down_any, fq, fk,
     out_any, gkv_ref, dr1_ref, dctx1_ref, act_any, dz_any, hid_any, br_any, left_any, right_ref, gvec,
     cq_s, lse_s, wide_s, dctx_s, dcq_s, dqt_s, kt_s, slope_s, act_s, dz_s, hid_s, br_s, left_s, out_s,
-    go_ref, w_out, w_up, w_down, keep_s, total_s, in_sems, out_sems,
+    go_ref, w_up, w_down, keep_s, r1_s, in_sems, out_sems,
 ):
-    up_copy, down_copy, go_copy, out_copy = copies(
-        (w_up_any, w_down_any, go_any.at[pl.ds(row * ROW, ROW)], w_out_any), (w_up, w_down, go_ref, w_out), in_sems
-    )
-    sent = []
-
-    def emit(source, target):
-        sent.append(pltpu.make_async_copy(source, target, out_sems.at[len(sent)]))
-        sent[-1].start()
-
-    hat1, _ = ln_parts(r1_ref[...])
+    up_copy, down_copy, go_copy = copies(
+        (w_up_any, w_down_any, go_any.at[pl.ds(row * ROW, ROW)]), (w_up, w_down, go_ref), in_sems
+    )
+    sent, emit = emitter(out_sems)
+    r1 = x_ref[...].astype(F32) + dot_nn(ctx1_ref[...], w_out[...])
+    r1_s[...] = r1
+    hat1, _ = ln_parts(r1)
     y1 = hat1 * vec[0:1, :] + vec[1:2, :]
     y1_b = y1.astype(BF)
     left_s[:, :D] = y1_b
@@ -442,7 +522,7 @@
     emit(hid_s, hid_any)
     up_copy.wait()
     down_copy.wait()
-    r3 = keep_s[...] + ffn_fwd(hid_s, w_up, w_down, act_s, slope_s, total_s, False)
+    r3 = keep_s[...] + ffn_fwd(hid_s, w_up, w_down, act_s, slope_s, None, False)
     emit(act_s, act_any)
     hat3, rstd3 = ln_parts(r3)
     out_s[...] = (hat3 * vec[4:5, :] + vec[5:6, :]).astype(BF)
@@ -453,7 +533,7 @@
     br_s[...] = dr3.astype(BF)
     emit(br_s, br_any)
     keep_s[...] = dr3
-    dy2 = keep_s[...] + ffn_bwd(br_s, w_up, w_down, slope_s, dz_s, total_s, False)
+    dy2 = keep_s[...] + ffn_bwd(br_s, w_up, w_down, slope_s, dz_s, None, False)
     emit(dz_s, dz_any)
     dr2, gain2, shift2 = ln_back(dy2, hat2, rstd2, vec[2:3, :])
     dr2_b = dr2.astype(BF)
@@ -465,8 +545,7 @@
     )
     dcq = dcq_s[...]
     right_ref[:, :D] = dcq
-    out_copy.wait()
-    self_head(dr2 + dot_nt(dcq, w_cross[:, :D]), r1_ref, vec, w_out, dr1_ref, dctx1_ref, gvec)
+    self_head(dr2 + dot_nt(dcq, w_cross[:, :D]), r1_s, vec, w_out, dr1_ref, dctx1_ref, gvec)
     gvec[2:3, :] = gain2
     gvec[3:4, :] = shift2
     gvec[4:5, :] = gain3
@@ -476,100 +555,135 @@
 
 
 def enc_back_kernel(
-    gkv_ref, r1_ref, r2_ref, slope_ref, vec, w_cross, w_out, w_up, w_down,
-    dr1_ref, dctx1_ref, dz_ref, hid_ref, br_ref, gvec, keep_s, total_s,
+    gkv_ref, r1_any, r2_ref, slope_any, vec, w_cross, w_out_any, w_up_any, w_down_any,
+    dr1_ref, dctx1_ref, dz_any, hid_any, br_any, gvec,
+    keep_s, total_s, r1_ref, slope_s, w_out, w_up, w_down, dz_s, hid_s, br_s, in_sems, out_sems,
 ):
+    made = copies(
+        (r1_any, slope_any, w_down_any, w_up_any, w_out_any), (r1_ref, slope_s, w_down, w_up, w_out), in_sems
+    )
+    sent, emit = emitter(out_sems)
     dmem = dot_nt(gkv_ref[...], w_cross[...])
     hat2, rstd2 = ln_parts(r2_ref[...])
     dr2, gain2, shift2 = ln_back(dmem, hat2, rstd2, vec[2:3, :])
+    br_s[...] = dr2.astype(BF)
+    emit(br_s, br_any)
+    keep_s[...] = dr2
+    made[0].wait()
     hat1, _ = ln_parts(r1_ref[...])
-    hid_ref[...] = (hat1 * vec[0:1, :] + vec[1:2, :]).astype(BF)
-    br_ref[...] = dr2.astype(BF)
-    keep_s[...] = dr2
-    dy1 = keep_s[...] + ffn_bwd(br_ref, w_up, w_down, slope_ref, dz_ref, total_s, True)
+    hid_s[...] = (hat1 * vec[0:1, :] + vec[1:2, :]).astype(BF)
+    emit(hid_s, hid_any)
+    for one in made[1:4]:
+        one.wait()
+    dy1 = keep_s[...] + ffn_bwd(br_s, w_up, w_down, slope_s, dz_s, total_s, True)
+    emit(dz_s, dz_any)
+    made[4].wait()
     self_head(dy1, r1_ref, vec, w_out, dr1_ref, dctx1_ref, gvec)
     gvec[2:3, :] = gain2
     gvec[3:4, :] = shift2
     gvec[4:8, :] = jnp.zeros((4, D), F32)
-
-
-KINDS = ("hid", "dz", "ctx", "dr1", "left", "right", "act", "branch")
-
-
-def rest_kernel(rows, dec_ref, *refs):
-    count = len(KINDS) * rows
-    sources, flat, refs = (refs[:count], refs[count : 2 * count]), refs[2 * count], refs[2 * count + 1 :]
-    kept, (hid_t, g_big, g_cross, g_out, sems) = dict(zip(KINDS, refs)), refs[len(KINDS) :]
-
-    def fetch(ins, i):
-        target = kept[KINDS[i // rows]].at[pl.ds((i % rows) * ROW, ROW)]
-        return pltpu.make_async_copy(ins[i], target, sems.at[i])
-
-    for which, ins in enumerate(sources):
-
-        @pl.when(dec_ref[0] == which)
-        def _(ins=ins):
-            for i in range(count):
-                fetch(ins, i).start()
-
-    def ready(*kinds):
-        for kind in kinds:
+    for one in sent:
+        one.wait()
+
+
+def row_fetcher(kinds, rows, dec_ref, refs):
+    count = len(kinds) * rows
+    buffers, sems = refs[-len(kinds) - 1 : -1], refs[-1]
+    ins = refs[: -len(kinds) - 1]
+    sources = [ins[i : i + count] for i in range(0, len(ins), count)]
+    kept = dict(zip(kinds, buffers))
+
+    def fetch(some, i):
+        size = some[i].shape[0]
+        target = kept[kinds[i // rows]].at[pl.ds((i % rows) * size, size)]
+        return pltpu.make_async_copy(some[i], target, sems.at[i])
+
+    def begin(some):
+        for i in range(count):
+            fetch(some, i).start()
+
+    if len(sources) == 1:
+        begin(sources[0])
+    else:
+        for which, some in enumerate(sources):
+            pl.when(dec_ref[0] == which)(functools.partial(begin, some))
+
+    def ready(*some):
+        for kind in some:
             for r in range(rows):
-                fetch(sources[0], KINDS.index(kind) * rows + r).wait()
-
-    base = {name: MATS[name][2] - REST_AT for name in MATS}
+                fetch(sources[0], kinds.index(kind) * rows + r).wait()
+
+    return kept, ready
+
+
+def fetched(kinds, sources):
+    ins = [row[kind] for some in sources for kind in kinds for row in some]
+    rows = len(sources[0])
+    kept = []
+    for kind in kinds:
+        size, cols = sources[0][0][kind].shape
+        kept.append(pltpu.VMEM((rows * size, cols), sources[0][0][kind].dtype))
+    return ins, kept + [pltpu.SemaphoreType.DMA((len(kinds) * rows,))]
+
+
+FFN_KINDS = ("hid", "dz", "act", "branch")
+ATTEND_KINDS = ("ctx", "dr1", "left", "right")
+
+
+def ffn_grads_kernel(rows, dec_ref, *refs):
+    count = 2 * len(FFN_KINDS) * rows
+    ins, flat, (hid_t, g_up, g_down), rest = refs[:count], refs[count], refs[count + 1 : count + 4], refs[count + 4 :]
+    kept, ready = row_fetcher(FFN_KINDS, rows, dec_ref, (*ins, *rest))
     ready("hid", "dz")
     hid_t[...] = kept["hid"][...].T
-
-    def up(c, _):
-        cols = pl.ds(pl.multiple_of(c * CHUNK, CHUNK), CHUNK)
-        g_big[:, cols] = dot_nn(hid_t[...], kept["dz"][:, cols])
-        return 0
-
-    lax.fori_loop(0, FF // CHUNK, up, 0)
-    to_flat("up", g_big, flat, base["up"])
+    for c in range(FF // CHUNK):
+        cols = slice(c * CHUNK, (c + 1) * CHUNK)
+        g_up[:, cols] = dot_nn(hid_t[...], kept["dz"][:, cols])
+    to_flat("up", g_up, flat, 0)
+    ready("act", "branch")
+    for c in range(FF // D):
+        part = slice(c * D, (c + 1) * D)
+        g_down[part, :] = dot_tn(kept["act"][:, part], kept["branch"][...])
+    to_flat("down", g_down, flat, MATS["down"][2] - MATS["up"][2])
+
+
+def attend_grads_kernel(rows, dec_ref, *refs):
+    count = 2 * len(ATTEND_KINDS) * rows
+    ins, flat, (g_cross, g_out), rest = refs[:count], refs[count], refs[count + 1 : count + 3], refs[count + 3 :]
+    kept, ready = row_fetcher(ATTEND_KINDS, rows, dec_ref, (*ins, *rest))
     ready("ctx", "dr1")
     g_out[...] = dot_tn(kept["ctx"][...], kept["dr1"][...].astype(BF))
-    to_flat("out", g_out, flat, base["out"])
+    to_flat("out", g_out, flat, 0)
     ready("left", "right")
     for at in (0, D):
         g_cross[:, at : at + D] = dot_tn(kept["left"][:, at : at + D], kept["right"][:, at : at + D])
-    to_flat("cross", g_cross, flat, base["cross"])
-    ready("act", "branch")
-    rows_n, _, _, group = MATS["down"]
-    perm = group_perm("down", True)
-
-    for c in range(rows_n // D):
+    to_flat("cross", g_cross, flat, MATS["cross"][2] - REST_AT)
+
+
+BACK_KINDS = ("qkv", "lse", "dctx", "dr1")
+
+
+def self_back_kernel(ins, causal_ref, wqkv, fq, fk, *refs):
+    (dx_ref, dqkv, dqt_s, kt_s, tri_s), rest = refs[ins : ins + 5], refs[ins + 5 :]
+    kept, ready = row_fetcher(BACK_KINDS, 1, causal_ref, (*refs[:ins], *rest))
+    ready("qkv", "lse", "dctx")
+    qkv = kept["qkv"]
+    attend_bwd(
+        causal_ref[0], qkv, 0, qkv, D, qkv, 2 * D, fq[...], fk[...], kept["lse"], kept["dctx"],
+        ((dqkv, 0), (dqkv, D), (dqkv, 2 * D)), dqt_s, kt_s, tri_s,
+    )
+    ready("dr1")
+    dx_ref[...] = (kept["dr1"][...] + dot_nt(dqkv[...], wqkv[...])).astype(BF)
+
+
+def qkv_kernel(ins, rows, dec_ref, x_ref, *refs):
+    (fl_qkv, x_t, g_qkv), rest = refs[ins : ins + 3], refs[ins + 3 :]
+    kept, ready = row_fetcher(("dqkv",), rows, dec_ref, (*refs[:ins], *rest))
+    x_t[...] = x_ref[...].T
+    ready("dqkv")
+    for c in range(3):
         cols = slice(c * D, (c + 1) * D)
-        g_out[...] = dot_tn(kept["act"][:, cols], kept["branch"][...])
-        for g in range(D // group):
-            block = g_out[g * group : (g + 1) * group, :].astype(BF)
-            blocked = jnp.concatenate([block[:, 128 * j : 128 * j + 128] for j in range(4)], axis=0)
-            at = base["down"] + (c * (D // group) + g) * 4 * group
-            flat[at : at + 4 * group, :] = dot_nn(perm, blocked).astype(BF)
-
-
-def self_back_kernel(causal_ref, dr1_ref, dctx_ref, qkv_ref, lse_ref, wqkv, fq, fk, dx_ref, dqkv, dqt_s, kt_s, tri_s):
-    attend_bwd(
-        causal_ref[0], qkv_ref, 0, qkv_ref, D, qkv_ref, 2 * D, fq[...], fk[...], lse_ref, dctx_ref,
-        ((dqkv, 0), (dqkv, D), (dqkv, 2 * D)), dqt_s, kt_s, tri_s,
-    )
-    dx_ref[...] = (dr1_ref[...] + dot_nt(dqkv[...], wqkv[...])).astype(BF)
-
-
-def qkv_kernel(rows, x_ref, *refs):
-    ins, fl_qkv, dqkv, x_t, g_qkv, sems = refs[:rows], *refs[rows:]
-    made = copies(ins, [dqkv.at[pl.ds(r * ROW, ROW)] for r in range(rows)], sems)
-    x_t[...] = x_ref[...].T
-    for one in made:
-        one.wait()
-
-    def step(c, _):
-        cols = pl.ds(pl.multiple_of(c * D, D), D)
-        g_qkv[:, cols] = dot_nn(x_t[...], dqkv[:, cols])
-        return 0
-
-    lax.fori_loop(0, 3, step, 0)
+        g_qkv[:, cols] = dot_nn(x_t[...], kept["dqkv"][:, cols])
     to_flat("qkv", g_qkv, fl_qkv, 0)
 
 
@@ -614,7 +728,7 @@
         out_specs=[IN_VMEM],
         out_shape=[shape_of((rows, 128), BF)],
         scratch_shapes=[pltpu.VMEM((rows + 32, 128), F32)],
-        compiler_params=params_of(16),
+        compiler_params=params_of(8),
     )(shift, params)[0]
 
 
@@ -624,7 +738,7 @@
         in_specs=[IN_SMEM, IN_VMEM],
         out_specs=[IN_VMEM] * 2,
         out_shape=[shape_of((1, share), F32), shape_of((8, 128), F32)],
-        compiler_params=params_of(16),
+        compiler_params=params_of(8),
     )(shift, sums)
 
 
@@ -634,61 +748,81 @@
         in_specs=[IN_SMEM] + [IN_VMEM] * 3,
         out_specs=[IN_VMEM] * 3,
         out_shape=[shape_of((1, share), F32)] * 3,
-        compiler_params=params_of(24),
+        compiler_params=params_of(16),
     )(clip, grad, first, second)
 
 
 def split_weights(pieces, n, share):
     shapes = [(rows, cols) for rows, cols, _, _ in MATS.values()] + [(32, 128)]
     rows = 16 * (-(-share * n // TILE) + 2)
-    return kernel_call(
+    got = kernel_call(
         functools.partial(weights_kernel, n, share),
         in_specs=[IN_VMEM],
         out_specs=[IN_VMEM] * 6,
         out_shape=[shape_of(s, BF) for s in shapes],
         scratch_shapes=[pltpu.VMEM((rows, 128), BF)],
-        compiler_params=params_of(48),
+        compiler_params=params_of(60),
     )(pieces)
+    return dict(zip((*MATS, "vec"), got))
+
+
+def placed_weights(place, slots, share, rows):
+    vm = pltpu.VMEM
+    shapes = [(rows, cols) for rows, cols, _, _ in MATS.values()] + [(32, 128)]
+    got = kernel_call(
+        functools.partial(place_kernel, share),
+        micros=9,
+        in_specs=[IN_SMEM] + [ANYWHERE] * 24,
+        out_specs=[ANYWHERE] * 6,
+        out_shape=[shape_of(s, BF) for s in shapes],
+        scratch_shapes=[vm(s, BF) for s in shapes]
+        + [vm((4, 8, rows // 2, 128), BF), vm((piece_row(share, 15) + rows + 16, 128), BF)]
+        + [pltpu.SemaphoreType.DMA((4, 8)), pltpu.SemaphoreType.DMA((6,))],
+        compiler_params=params_of(60),
+    )(place, *(one for slot in slots for one in slot))
+    return dict(zip((*MATS, "vec"), got))
 
 
 def row_shapes(*cols):
     return [shape_of((ROW, abs(c)), F32 if c < 0 else BF) for c in cols]
 
 
-def self_fwd(causal, row, x, w, fq, fk):
-    names = ("qkv", "ctx", "lse", "r1")
+def self_fwd(causal, row, x, w_qkv, fq, fk):
+    names = ("qkv", "ctx", "lse")
     vm = pltpu.VMEM
     got = kernel_call(
         self_fwd_kernel,
         micros=5,
         grid=(1,),
-        in_specs=[IN_SMEM, at_row(row, D), whole_spec((D, 3 * D)), whole_spec((D, D)), at_row(row, 128), at_row(row, 128)],
-        out_specs=[at_row(0, 3 * D), at_row(0, D), at_row(0, ROW, HEADS), at_row(0, D)],
-        out_shape=row_shapes(3 * D, D) + [shape_of((HEADS, ROW), F32)] + row_shapes(-D),
+        in_specs=[IN_SMEM, at_row(row, D), whole_spec((D, 3 * D)), at_row(row, 128), at_row(row, 128)],
+        out_specs=[at_row(0, 3 * D), at_row(0, D), at_row(0, ROW, HEADS)],
+        out_shape=row_shapes(3 * D, D) + [shape_of((HEADS, ROW), F32)],
         scratch_shapes=[vm((ROW, 128), F32), vm((ROW, ROW), F32)],
+        compiler_params=params_of(24),
+    )(causal, x, w_qkv, fq, fk)
+    return dict(zip(names, got))
+
+
+def enc_ffn(row, x, fwd, w, vec):
+    names = ("mem", "kv", "act", "slope", "r1", "r2")
+    vm = pltpu.VMEM
+    got = kernel_call(
+        functools.partial(enc_ffn_kernel, row > 0),
+        micros=8,
+        grid=(1,),
+        in_specs=[at_row(row, D), at_row(0, D), whole_spec((6, D)), whole_spec((D, D))] + [ANYWHERE] * 3,
+        out_specs=[at_row(0, 2 * D), at_row(0, 2 * D)] + [ANYWHERE] * 4,
+        out_shape=row_shapes(2 * D, 2 * D, FF, FF, -D, -D),
+        scratch_shapes=[
+            vm((ROW, D), BF), vm((ROW, D), F32), vm((ROW, FF), BF), vm((ROW, FF), BF), vm((ROW, D), F32), vm((ROW, D), F32),
+            vm((D, FF), BF), vm((FF, D), BF), vm((D, 2 * D), BF), pltpu.SemaphoreType.DMA((3,)), pltpu.SemaphoreType.DMA((4,)),
+        ],
         compiler_params=params_of(32),
-    )(causal, x, w["qkv"], w["out"], fq, fk)
+    )(x, fwd["ctx"], vec, w["out"], w["up"], w["down"], w["cross"])
     return dict(zip(names, got))
 
 
-def enc_ffn(r1, w, vec):
-    names = ("mem", "kv", "act", "slope", "r2")
-    got = kernel_call(
-        enc_ffn_kernel,
-        micros=10,
-        grid=(1,),
-        in_specs=[
-            at_row(0, D), whole_spec((6, D)), whole_spec((D, FF)), whole_spec((FF, D)), whole_spec((D, 2 * D)),
-        ],
-        out_specs=[at_row(0, 2 * D), at_row(0, 2 * D), at_row(0, FF), at_row(0, FF), at_row(0, D)],
-        out_shape=row_shapes(2 * D, 2 * D, FF, FF, -D),
-        scratch_shapes=[pltpu.VMEM((ROW, D), BF), pltpu.VMEM((ROW, D), F32)],
-        compiler_params=params_of(48),
-    )(r1, vec, w["up"], w["down"], w["cross"])
-    return dict(zip(names, got))
-
-
-def dec_call(row, r1, kv, go, w, vec, fq, fk):
+def dec_call(row, x, fwd, kv, go, w, vec, fq, fk):
     vm = pltpu.VMEM
     names = ("out", "gkv", "dr1", "dctx", "act", "dz", "hid", "branch", "left", "right", "gvec")
     got = kernel_call(
@@ -696,8 +830,8 @@
         micros=23,
         grid=(1,),
         in_specs=[
-            at_row(0, D), at_row(0, 2 * D), ANYWHERE, whole_spec((6, D)), whole_spec((D, 2 * D)),
-            ANYWHERE, ANYWHERE, ANYWHERE, at_row(row, 128), at_row(row, 128),
+            at_row(row, D), at_row(0, D), at_row(0, 2 * D), ANYWHERE, whole_spec((6, D)), whole_spec((D, 2 * D)),
+            whole_spec((D, D)), ANYWHERE, ANYWHERE, at_row(row, 128), at_row(row, 128),
         ],
         out_specs=[ANYWHERE, at_row(0, 2 * D), at_row(0, D), at_row(0, D)] + [ANYWHERE] * 5
         + [at_row(0, 2 * D), whole_spec((8, D))],
@@ -705,94 +839,98 @@
         scratch_shapes=[
             vm((ROW, D), BF), vm((HEADS, ROW), F32), vm((ROW, 128), F32), vm((ROW, D), BF), vm((ROW, D), BF),
             vm((D, ROW), F32), vm((D, ROW), BF), vm((ROW, FF), BF), vm((ROW, FF), BF), vm((ROW, FF), BF), vm((ROW, D), BF),
-            vm((ROW, D), BF), vm((ROW, 2 * D), BF), vm((ROW, D), BF), vm((ROW, D), BF), vm((D, D), BF), vm((D, FF), BF),
-            vm((FF, D), BF), vm((ROW, D), F32), vm((ROW, D), F32), pltpu.SemaphoreType.DMA((4,)), pltpu.SemaphoreType.DMA((6,)),
+            vm((ROW, D), BF), vm((ROW, 2 * D), BF), vm((ROW, D), BF), vm((ROW, D), BF), vm((D, FF), BF),
+            vm((FF, D), BF), vm((ROW, D), F32), vm((ROW, D), F32), pltpu.SemaphoreType.DMA((3,)),
+            pltpu.SemaphoreType.DMA((6,)),
         ],
-        compiler_params=params_of(56),
-    )(r1, kv, go, vec, w["cross"], w["out"], w["up"], w["down"], fq, fk)
+        compiler_params=params_of(60),
+    )(x, fwd["ctx"], kv, go, vec, w["cross"], w["out"], w["up"], w["down"], fq, fk)
     return dict(zip(names, got))
 
 
-def enc_back(gkv, r1, fwd, w, vec):
+def enc_back(gkv, fwd, w, vec):
     names = ("dr1", "dctx", "dz", "hid", "branch", "gvec")
+    vm = pltpu.VMEM
     got = kernel_call(
         enc_back_kernel,
-        micros=10,
-        grid=(1,),
-        in_specs=[
-            at_row(0, 2 * D), at_row(0, D), at_row(0, D), at_row(0, FF), whole_spec((6, D)), whole_spec((D, 2 * D)),
-            whole_spec((D, D)), whole_spec((D, FF)), whole_spec((FF, D)),
-        ],
-        out_specs=[at_row(0, c) for c in (D, D, FF, D, D)] + [whole_spec((8, D))],
-        out_shape=row_shapes(-D, D, FF, D, D) + [shape_of((8, D), F32)],
-        scratch_shapes=[pltpu.VMEM((ROW, D), F32)] * 2,
-        compiler_params=params_of(56),
-    )(gkv, r1, fwd["r2"], fwd["slope"], vec, w["cross"], w["out"], w["up"], w["down"])
-    return dict(zip(names, got))
-
-
-def rest_grads(is_dec, enc_rows, dec_rows):
-    rows = len(dec_rows)
-    ins = [row[kind] for some in (enc_rows, dec_rows) for kind in KINDS for row in some]
-    vm = pltpu.VMEM
-    kept = [vm((rows * ROW, dec_rows[0][kind].shape[1]), dec_rows[0][kind].dtype) for kind in KINDS]
-    return kernel_call(
-        functools.partial(rest_kernel, rows),
-        micros=18,
-        in_specs=[IN_SMEM] + [ANYWHERE] * len(ins),
-        out_specs=[IN_VMEM],
-        out_shape=[shape_of((VEC_AT - REST_AT, 128), BF)],
-        scratch_shapes=kept
-        + [vm((D, rows * ROW), BF), vm((D, FF), F32), vm((D, 2 * D), F32), vm((D, D), F32)]
-        + [pltpu.SemaphoreType.DMA((len(KINDS) * rows,))],
-        compiler_params=params_of(60),
-    )(is_dec, *ins)[0]
-
-
-def self_back(causal, row, grads, fwd, w, fq, fk):
-    vm = pltpu.VMEM
-    shapes = row_shapes(D, 3 * D)
-    return kernel_call(
-        self_back_kernel,
         micros=8,
         grid=(1,),
         in_specs=[
-            IN_SMEM, at_row(0, D), at_row(0, D), at_row(0, 3 * D), at_row(0, ROW, HEADS), whole_spec((D, 3 * D)),
-            at_row(row, 128), at_row(row, 128),
+            at_row(0, 2 * D), ANYWHERE, at_row(0, D), ANYWHERE, whole_spec((6, D)), whole_spec((D, 2 * D)),
+            ANYWHERE, ANYWHERE, ANYWHERE,
         ],
+        out_specs=[at_row(0, D), at_row(0, D)] + [ANYWHERE] * 3 + [whole_spec((8, D))],
+        out_shape=row_shapes(-D, D, FF, D, D) + [shape_of((8, D), F32)],
+        scratch_shapes=[
+            vm((ROW, D), F32), vm((ROW, D), F32), vm((ROW, D), F32), vm((ROW, FF), BF), vm((D, D), BF), vm((D, FF), BF),
+            vm((FF, D), BF), vm((ROW, FF), BF), vm((ROW, D), BF), vm((ROW, D), BF), pltpu.SemaphoreType.DMA((5,)),
+            pltpu.SemaphoreType.DMA((3,)),
+        ],
+        compiler_params=params_of(32),
+    )(gkv, fwd["r1"], fwd["r2"], fwd["slope"], vec, w["cross"], w["out"], w["up"], w["down"])
+    return dict(zip(names, got))
+
+
+def row_grads(body, kinds, flat_rows, scratch, is_dec, sources):
+    ins, kept = fetched(kinds, sources)
+    return kernel_call(
+        functools.partial(body, len(sources[0])),
+        micros=1,
+        in_specs=[IN_SMEM] + [ANYWHERE] * len(ins),
+        out_specs=[IN_VMEM],
+        out_shape=[shape_of((flat_rows, 128), BF)],
+        scratch_shapes=scratch + kept,
+        compiler_params=params_of(48),
+    )(is_dec, *ins)[0]
+
+
+def self_back(causal, row, sources, w, fq, fk):
+    vm = pltpu.VMEM
+    shapes = row_shapes(D, 3 * D)
+    ins, kept = fetched(BACK_KINDS, [[one] for one in sources])
+    got = kernel_call(
+        functools.partial(self_back_kernel, len(ins)),
+        micros=1,
+        grid=(1,),
+        in_specs=[IN_SMEM, whole_spec((D, 3 * D)), at_row(row, 128), at_row(row, 128)] + [ANYWHERE] * len(ins),
         out_specs=[whole_spec(s.shape) for s in shapes],
         out_shape=shapes,
-        scratch_shapes=[vm((D, ROW), F32), vm((D, ROW), BF), vm((ROW, ROW), F32)],
-        compiler_params=params_of(40),
-    )(causal, grads["dr1"], grads["dctx"], fwd["qkv"], fwd["lse"], w["qkv"], fq, fk)
-
-
-def qkv_grad(x, dqkvs):
+        scratch_shapes=[vm((D, ROW), F32), vm((D, ROW), BF), vm((ROW, ROW), F32)] + kept,
+        compiler_params=params_of(28),
+    )(causal, w["qkv"], fq, fk, *ins)
+    return dict(zip(("dx", "dqkv"), got))
+
+
+def qkv_grad(is_dec, x, sources):
     vm = pltpu.VMEM
-    t, rows = x.shape[0], len(dqkvs)
+    t, rows = x.shape[0], len(sources[0])
+    ins, kept = fetched(("dqkv",), sources)
     return kernel_call(
-        functools.partial(qkv_kernel, rows),
-        micros=5,
-        in_specs=[IN_VMEM] + [ANYWHERE] * rows,
+        functools.partial(qkv_kernel, len(ins), rows),
+        micros=1,
+        in_specs=[IN_SMEM, IN_VMEM] + [ANYWHERE] * len(ins),
         out_specs=[IN_VMEM],
         out_shape=[shape_of((REST_AT, 128), BF)],
-        scratch_shapes=[vm((t, 3 * D), BF), vm((D, t), BF), vm((D, 3 * D), F32), pltpu.SemaphoreType.DMA((rows,))],
-        compiler_params=params_of(40),
-    )(x, *dqkvs)[0]
+        scratch_shapes=[vm((D, t), BF), vm((D, 3 * D), F32)] + kept,
+        compiler_params=params_of(28),
+    )(is_dec, x, *ins)[0]
 
 
 def pack(place, parts, planes, base, share, rows):
     half = rows // 2
-    total = sum(p.shape[0] for p in parts)
+    parts = [p if isinstance(p, tuple) else (p, p.shape[0]) for p in parts]
+    total = sum(count for _, count in parts)
     need = piece_row(share, 4 * planes[-1] + 3) - base + rows
     return kernel_call(
         functools.partial(pack_kernel, share, planes, base),
-        in_specs=[IN_SMEM] + [IN_VMEM] * len(parts),
-        out_specs=[IN_VMEM] * 4,
+        micros=1,
+        grid=(1,),
+        in_specs=[IN_SMEM] + [pl.BlockSpec((count, 128), lambda i: (0, 0), pipeline_mode=pl.Buffered(1)) for _, count in parts],
+        out_specs=[whole_spec((len(planes), 2, half, 128))] * 4,
         out_shape=[shape_of((len(planes), 2, half, 128), BF)] * 4,
         scratch_shapes=[pltpu.VMEM((max(total, need), 128), BF)],
-        compiler_params=params_of(40),
-    )(place, *parts)
+        compiler_params=params_of(32),
+    )(place, *(p for p, _ in parts))
 
 
 def mask_features(segments, live):
@@ -812,12 +950,6 @@
     key = jnp.where(odd, bit, 1 - bit)
     keys = [jnp.where(is_seg | (is_pos & (live[i][:, None] != 1)), key.astype(F32) * -BIG, 0.0).astype(BF) for i in range(2)]
     return query.astype(BF), keys[0], keys[1]
-
-
-def passed_along(value, axis, steps):
-    count = lax.axis_size(axis)
-    first, last = (max(0, -steps), min(count, count - steps))
-    return lax.ppermute(value, axis, [(source, source + steps) for source in range(first, last)])
 
 
 def ghosts(shapes):
@@ -868,6 +1000,60 @@
     return lax.ppermute(value, "batch", pairs)
 
 
+def over_all(value):
+    axes = ("section", "batch")
+    places = [(core, i) for core in range(2) for i in range(16)]
+
+    def flat(core, i):
+        return core * 16 + i
+
+    total = value
+    for core_step in range(2):
+        for step in range(4):
+            if core_step or step:
+                pairs = [(flat(c, i), flat(c ^ core_step, i ^ step)) for c, i in places]
+                total = total + lax.ppermute(value, axes, pairs)
+    value = total
+    for step in (4, 8, 12):
+        total = total + plane_permute(value, step)
+    return total
+
+
+def tied(*values):
+    return lax.optimization_barrier(values)
+
+
+def gathered(own, z):
+    half = own.shape[0] // 2
+
+    def first(block):
+        a, b = block[:half], block[half:]
+        return a, b, plane_permute(a, 1), plane_permute(b, 2)
+
+    def second(parts):
+        a, b, ax, by = parts
+        return (a, ax, plane_permute(jnp.stack([a, ax]), 2), b, by, plane_permute(jnp.stack([b, by]), 1))
+
+    up, down = line_permute(own, 1, (0, 1, 2)), line_permute(own, -1, (1, 2, 3))
+    begun = first(own)
+    zero = second(begun)
+    up, down, _ = tied(up, down, begun)
+    up_two, down_two = line_permute(up, 1, (1, 2)), line_permute(down, -1, (1, 2))
+    begun = first(jnp.where((z == 0) | (z == 2), down, up))
+    zero, begun = tied(zero, begun)
+    one = second(begun)
+    up_two, down_two, _ = tied(up_two, down_two, zero)
+    up_three, down_three = line_permute(up_two, 1, (2,)), line_permute(down_two, -1, (1,))
+    begun = first(jnp.where(z == 0, down_two, jnp.where(z == 1, down, up_two)))
+    one, begun = tied(one, begun)
+    two = second(begun)
+    up_three, down_three, _ = tied(up_three, down_three, one)
+    begun = first(jnp.where(z == 0, down_three, jnp.where(z == 1, down_two, jnp.where(z == 2, up, up_three))))
+    two, begun = tied(two, begun)
+    three = second(begun)
+    return zero, one, two, three
+
+
 def added(*values):
     total = values[0].astype(F32)
     for value in values[1:]:
@@ -875,9 +1061,13 @@
     return total
 
 
-def plane_sums(packed, y, x):
+def plane_start(packed):
     send_a, keep_a, send_b, keep_b = packed
-    got_a, got_b = plane_permute(send_a, 2), plane_permute(send_b, 1)
+    return keep_a, plane_permute(send_a, 2), keep_b, plane_permute(send_b, 1)
+
+
+def plane_end(begun, y, x):
+    keep_a, got_a, keep_b, got_b = begun
 
     def part(keep, got, index):
         return added(lax.dynamic_index_in_dim(keep, index, 1, False), lax.dynamic_index_in_dim(got, index, 1, False))
@@ -888,8 +1078,8 @@
     return jnp.stack([sum_a.astype(BF), sum_b.astype(BF)], axis=1)
 
 
-def line_sums(early, late, z):
-    one, two, three = early[0], early[1], early[2]
+def line_sums(early, mid, late, z):
+    one, two, three = mid[0], early[0], early[1]
 
     def low(value):
         return value.astype(BF)
@@ -919,73 +1109,111 @@
     t = x.shape[0]
     count = t // ROW
 
+    y, x_at, z = lax.rem(me // 2, 2), lax.rem(me, 2), me // 4
+    custom = n == 16
+    flag = is_decoder.astype(jnp.int32)[None]
     own = shifted(shift, params, share, rows)
-    pieces = lax.all_gather(own, "batch", axis=0, tiled=False)
     fq, fk_src, fk_tgt = mask_features(segments, live_mask)
     fk_self = jnp.where(is_decoder, fk_tgt, fk_src)
-    pieces, fq, fk_src, fk_self = lax.optimization_barrier((pieces, fq, fk_src, fk_self))
-    *mats, vec_rows = split_weights(pieces, n, share)
-    w = dict(zip(MATS, mats))
-    vec = vec_rows[:24].astype(F32).reshape(6, D)
+    if custom:
+        spot = jnp.concatenate([jnp.stack([z, y, x_at]), jnp.asarray(SLOTS, jnp.int32)[:, z]])
+        slots, fq, fk_src, fk_self = tied(gathered(own, z), fq, fk_src, fk_self)
+        w = placed_weights(spot, slots, share, rows)
+    else:
+        pieces = lax.all_gather(own, "batch", axis=0, tiled=False)
+        pieces, fq, fk_src, fk_self = tied(pieces, fq, fk_src, fk_self)
+        w = split_weights(pieces, n, share)
+    def forward(row):
+        return self_fwd(flag, row, x, w["qkv"], fq, fk_self)
+
+    first_fwd = forward(0)
+    vec = w["vec"][:24].astype(F32).reshape(6, D)
 
     def nothing():
         return {}
 
-    flag = is_decoder.astype(jnp.int32)[None]
-    fwd = [self_fwd(flag, 0, x, w, fq, fk_self)]
-    _, first = either(is_decoder, nothing, lambda: enc_ffn(fwd[0]["r1"], w, vec))
-    kv_in = passed_along(first["kv"], "section", 1)
-    fwd += [self_fwd(flag, r, x, w, fq, fk_self) for r in range(1, count)]
-    kept = [first]
-
-    def dec_row(row, kv):
-        return dec_call(row, fwd[row]["r1"], kv, out_grad, w, vec, fq, fk_src)
-
-    def enc_row(row, grad_kv):
-        return enc_back(grad_kv, fwd[row]["r1"], kept[row], w, vec)
-
-    dec_rows, enc_rows = [], []
-    kvs, back = [kv_in], []
+    def swapped(value):
+        return lax.ppermute(value, "section", [(0, 1), (1, 0)])
+
+    fwd, first = either(
+        is_decoder, lambda: [forward(r) for r in range(1, count)], lambda: enc_ffn(0, x, first_fwd, w, vec)
+    )
+    dec_fwd, enc_fwd = [first_fwd, *fwd], [first_fwd]
+    kept, dec_rows, enc_rows, back, enc_self = [first], [], [], [], []
+    kv_in = swapped(first["kv"])
     for row in range(count):
 
+        def dec_make():
+            got = dec_call(row, x, dec_fwd[row], kv_in, out_grad, w, vec, fq, fk_src)
+            return got.pop("gkv"), got
+
         def enc_make():
-            done = [enc_row(row - 1, back[row - 1])] if row else []
-            ahead = [enc_ffn(fwd[row + 1]["r1"], w, vec)] if row + 1 < count else []
-            return ahead, done
-
-        got, (ahead, done) = either(is_decoder, lambda: dec_row(row, kvs[row]), enc_make)
+            fwd, ahead, done, far = [], [], [], []
+            if row + 1 < count:
+                fwd = [forward(r) for r in range(1, count)] if row == 0 else []
+                ahead = [enc_ffn(row + 1, x, fwd[0] if row == 0 else enc_fwd[row + 1], w, vec)]
+            if row:
+                done = [enc_back(back[row - 1], kept[row - 1], w, vec)]
+            if row and row == count - 1:
+                far = [self_back(flag, 0, [{**enc_rows[0], **enc_fwd[0]} if enc_rows else {**done[0], **enc_fwd[0]}], w, fq, fk_self)]
+            return [k.pop("kv") for k in ahead], (fwd, ahead, done, far)
+
+        (sent, got), (_, (fwd, ahead, done, far)) = either(is_decoder, dec_make, enc_make)
         dec_rows.append(got)
+        enc_fwd += fwd
         enc_rows += done
         kept += ahead
-        kvs += [passed_along(k["kv"], "section", 1) for k in ahead]
-        back.append(passed_along(got["gkv"], "section", -1))
-    _, done = either(is_decoder, nothing, lambda: enc_row(count - 1, back[count - 1]))
+        enc_self += far
+        kv_in = swapped(sent)
+        back.append(kv_in)
+
+    last = count - 1
+    dec_self, done = either(
+        is_decoder,
+        lambda: [self_back(flag, 0, [{**dec_rows[0], **dec_fwd[0]}], w, fq, fk_self)] if last else [],
+        lambda: enc_back(back[last], kept[last], w, vec),
+    )
     enc_rows.append(done)
-
-    def grads_of(rows):
-        return [{**made, "ctx": fwd[r]["ctx"]} for r, made in enumerate(rows)]
-
+    dec_all = [{**made, **fwd} for made, fwd in zip(dec_rows, dec_fwd)]
     enc_all = [
-        {**made, "act": kept[r]["act"], "left": kept[r]["mem"], "right": back[r]} for r, made in enumerate(enc_rows)
+        {**made, **fwd, "act": k["act"], "left": k["mem"], "right": g}
+        for made, fwd, k, g in zip(enc_rows, enc_fwd, kept, back)
     ]
-    rest = rest_grads(flag, grads_of(enc_all), grads_of(dec_rows))
+    both = [enc_all, dec_all]
+
     gvec = jnp.where(is_decoder, sum(r["gvec"] for r in dec_rows), sum(r["gvec"] for r in enc_rows))
     fl_vec = jnp.pad(gvec[:6].reshape(24, 128).astype(BF), ((0, 24), (0, 0)))
 
-    y, x_at, z = lax.rem(me // 2, 2), lax.rem(me, 2), me // 4
+    vm = pltpu.VMEM
+    flat_ffn = row_grads(
+        ffn_grads_kernel, FFN_KINDS, VEC_AT - MATS["up"][2],
+        [vm((D, t), BF), vm((D, FF), F32), vm((FF, D), F32)], flag, both,
+    )
     place = jnp.stack([y, x_at])
-    custom = n == 16
     if custom:
-        early = plane_sums(pack(place, [rest, fl_vec], (1, 2, 3), REST_AT, share, rows), y, x_at)
-
-    dxs, dqkvs = [], []
-    for row in range(count):
-        mine = {k: jnp.where(is_decoder, dec_rows[row][k], enc_rows[row][k]) for k in ("dr1", "dctx")}
-        dx, dqkv = self_back(flag, row, mine, fwd[row], w, fq, fk_self)
-        dxs.append(dx)
-        dqkvs.append(dqkv)
-    fl_qkv = qkv_grad(x, dqkvs)
-    dx = jnp.concatenate(dxs, axis=0)
+        packed = pack(place, [flat_ffn, fl_vec], (2, 3), MATS["up"][2], share, rows)
+        early = plane_start(packed)
+        flag, _ = tied(flag, packed[0])
+    flat_attend = row_grads(
+        attend_grads_kernel, ATTEND_KINDS, MATS["up"][2] - REST_AT,
+        [vm((D, 2 * D), F32), vm((D, D), F32)], flag, both,
+    )
+    if custom:
+        need = piece_row(share, 7) + rows - MATS["up"][2]
+        packed = pack(place, [flat_attend, (flat_ffn, need)], (1,), REST_AT, share, rows)
+        mid = plane_start(packed)
+        flag, _ = tied(flag, packed[0])
+
+    common = []
+    for row in range(len(dec_self), count):
+        common.append(self_back(flag, row, [enc_all[row], dec_all[row]], w, fq, fk_self))
+    if custom:
+        early, common[-1] = tied(early, common[-1])
+        early = plane_end(early, y, x_at)
+    fl_qkv = qkv_grad(flag, x, [[*enc_self, *common], [*dec_self, *common]])
+    dx = jnp.concatenate(
+        [jnp.where(is_decoder, d["dx"], e["dx"]) for d, e in zip(dec_self, enc_self)] + [r["dx"] for r in common], axis=0
+    )
     layer_out = jnp.where(
         is_decoder,
         jnp.concatenate([r["out"] for r in dec_rows], axis=0),
@@ -993,23 +1221,22 @@
     )
 
     if custom:
+        mid, fl_qkv = tied(mid, fl_qkv)
+        mid = plane_end(mid, y, x_at)
         need = piece_row(share, 3) + rows
-        late = plane_sums(pack(place, [fl_qkv, rest[: need - REST_AT]], (0,), 0, share, rows), y, x_at)
-        mine = line_sums(early, late, z).reshape(rows, 128)
+        late = plane_start(pack(place, [fl_qkv, (flat_attend, need - REST_AT)], (0,), 0, share, rows))
+        late = plane_end(late, y, x_at)
+        mine = line_sums(early, mid, late, z).reshape(rows, 128)
     else:
         spare = jnp.zeros((piece_row(share, n - 1) + rows - FLAT_ROWS, 128), BF)
-        flat = jnp.concatenate([fl_qkv, rest, fl_vec[:24], spare], axis=0)
+        flat = jnp.concatenate([fl_qkv, flat_attend, flat_ffn, fl_vec[:24], spare], axis=0)
         stacked = jnp.concatenate([flat[piece_row(share, b) :][:rows] for b in range(n)], axis=0)
         mine = lax.psum_scatter(stacked, "batch", scatter_dimension=0, tiled=True).astype(F32)
     grad_share, squares = unshifted(shift, jnp.pad(mine, ((0, 8), (0, 0))), share)
 
     square_sum = jnp.sum(squares)
     if custom:
-        square_sum = square_sum.reshape(1, 1)
-        square_sum = square_sum + lax.ppermute(square_sum, "section", [(0, 1), (1, 0)])
-        for step in (1, 2, 4, 8):
-            square_sum = square_sum + plane_permute(square_sum, step)
-        square_sum = square_sum[0, 0]
+        square_sum = over_all(square_sum.reshape(1, 1))[0, 0]
     else:
         square_sum = lax.psum(square_sum, ("section", "batch"))
     grad_norm = jnp.sqrt(square_sum)

time: 428 us -> 397 us (0.928); the launches traced: 420 us -> 394 us
  waiting for transfers between devices: 155 us -> 85.4 us
  starting transfers between devices: 49.9 us -> 92.4 us
  loops' own time: 14.6 us -> 25.2 us
  between operations: 20.5 us -> 10.1 us
  local copies, waits for them, and re-layouts: 17.7 us -> 8.24 us
  other arithmetic: 13.9 us -> 22.6 us
    all_gather x1 -> x0, waiting for transfers between devices: 102 us -> none  [shards(): pieces = lax.all_gather(own, 'batch', axis=0, tiled=False)]
    ppermute x12 -> x31, waiting for transfers between devices: 18.9 us -> 57.6 us  [plane_permute(): return lax.ppermute(value, 'batch', [(i, i ^ step) for i in range(16)])]
    ppermute x12 -> x31, starting transfers between devices: 23.9 us -> 44.5 us  [plane_permute(): return lax.ppermute(value, 'batch', [(i, i ^ step) for i in range(16)])]
    ppermute x7 -> x13, starting transfers between devices: 12.4 us -> 27.7 us  [line_permute(): return lax.ppermute(value, 'batch', pairs)]
    unnamed x114 -> x112, local copies, waits for them, and re-layouts: 14.8 us -> 3.51 us
    another operation x5, loops' own time: 14.6 us -> 25.2 us  [either(): got = lax.cond(is_decoder, branch(1), branch(0))]
    ppermute x7 -> x11, starting transfers between devices: 13.6 us -> 20.3 us  [the longest x4 13.4 us: swapped(): return lax.ppermute(value, 'section', [(0, 1), (1, 0)])]
    ppermute x7 -> x11, waiting for transfers between devices: 16.4 us -> 10.5 us  [the longest x4 10.5 us: swapped(): return lax.ppermute(value, 'section', [(0, 1), (1, 0)])]
  transfers between devices with their start and end apart: 27 -> 55, of which waited for: 16 -> 21; matrix products, arithmetic and copies ran while one was open for 3% -> 6% of each run, Pallas kernels for 9% -> 7%
where the time goes in v3:
time: 397 us; the launch traced here: 394 us
  Pallas kernels  150 us (38%)
  starting transfers between devices  92.4 us (23%)
  waiting for transfers between devices  85.4 us (22%)
  loops' own time  25.2 us (6%)
  other arithmetic  22.6 us (6%)
  between operations  10.1 us (3%)
  local copies, waits for them, and re-layouts  8.24 us (2%)
    pallas_call x27, Pallas kernels, kernel_call(): return lambda *operands: tuple(call(*operands))  150 us
    ppermute x31, waiting for transfers between devices, plane_permute(): return lax.ppermute(value, 'batch', [(i, i ^ step) for i in range(16)])  57.6 us
    ppermute x31, starting transfers between devices, plane_permute(): return lax.ppermute(value, 'batch', [(i, i ^ step) for i in range(16)])  44.5 us
    ppermute x13, starting transfers between devices, line_permute(): return lax.ppermute(value, 'batch', pairs)  27.7 us
    another operation x5, loops' own time, either(): got = lax.cond(is_decoder, branch(1), branch(0))  25.2 us
    ppermute x13, waiting for transfers between devices, line_permute(): return lax.ppermute(value, 'batch', pairs)  17.3 us
    ppermute x4, starting transfers between devices, swapped(): return lax.ppermute(value, 'section', [(0, 1), (1, 0)])  13.4 us
    ppermute x4, waiting for transfers between devices, swapped(): return lax.ppermute(value, 'section', [(0, 1), (1, 0)])  10.5 us
  transfers between devices with their start and end apart: 55, of which 21 were waited for; matrix products, arithmetic and copies ran while one was open for 6% of the time, Pallas kernels for 7%

profile of v3, /device:TPU:0, one launch (start us, length us, event | category | flops | bytes accessed | tf_op | source)
XLA Modules:
  0.0 393.9 jit_solution(8304626855727848919)
XLA Ops:
  3.8 5.0 %collective-permute-start.4 = (bf16[1824,128]{1,0:T(8,128)(2,1)S(1)}, bf16[1824,128]{1,0:T(8,128)(2,1)S(1)}, u32[]{:S(2)}, u32[]{:S(2)}) collective-permute-start(bf16[1824,128]{1,0:T(8,128)(2,1)S(1)} %shard_map.135), channel_id=1, source_target_pairs={{0,4},{1,5},{2,6},{3,7},{4,8},{5,9},{6,10},{7,11},{8,12},{9,13},{1... | collective-permute-start | bytes 1400840 | tf_op jit(solution)/shard_map/ppermute | solution.py:1000
  13.3 4.1 %collective-permute-done.2.refs_4_ = bf16[912,128]{1,0:T(8,128)(2,1)S(1)} collective-permute-done((bf16[912,128]{1,0:T(8,128)(2,1)S(1)}, bf16[912,128]{1,0:T(8,128)(2,1)S(1)}, u32[]{:S(2)}, u32[]{:S(2)}) %collective-permute-start.2) | collective-permute-done | bytes 233504 | tf_op jit(solution)/shard_map/ppermute | solution.py:995
  19.0 3.8 collective-permute-done.5
  29.4 4.4 %collective-permute-done.6.refs_7_ = bf16[912,128]{1,0:T(8,128)(2,1)S(1)} collective-permute-done((bf16[912,128]{1,0:T(8,128)(2,1)S(1)}, bf16[912,128]{1,0:T(8,128)(2,1)S(1)}, u32[]{:S(2)}, u32[]{:S(2)}) %collective-permute-start.6) | collective-permute-done | bytes 233504 | tf_op jit(solution)/shard_map/ppermute | solution.py:995
  36.7 4.9 %collective-permute-done.7.refs_10_ = bf16[912,128]{1,0:T(8,128)(2,1)S(1)} collective-permute-done((bf16[912,128]{1,0:T(8,128)(2,1)S(1)}, bf16[912,128]{1,0:T(8,128)(2,1)S(1)}, u32[]{:S(2)}, u32[]{:S(2)}) %collective-permute-start.7) | collective-permute-done | bytes 233504 | tf_op jit(solution)/shard_map/ppermute | solution.py:995
  47.9 9.2 %collective-permute-done.12.refs_13_ = bf16[912,128]{1,0:T(8,128)(2,1)S(1)} collective-permute-done((bf16[912,128]{1,0:T(8,128)(2,1)S(1)}, bf16[912,128]{1,0:T(8,128)(2,1)S(1)}, u32[]{:S(2)}, u32[]{:S(2)}) %collective-permute-start.12) | collective-permute-done | bytes 233504 | tf_op jit(solution)/shard_map/ppermute | solution.py:995
  71.0 7.2 %collective-permute-done.18.refs_19_ = bf16[912,128]{1,0:T(8,128)(2,1)S(1)} collective-permute-done((bf16[912,128]{1,0:T(8,128)(2,1)S(1)}, bf16[912,128]{1,0:T(8,128)(2,1)S(1)}, u32[]{:S(2)}, u32[]{:S(2)}) %collective-permute-start.18) | collective-permute-done | bytes 233504 | tf_op jit(solution)/shard_map/ppermute | solution.py:995
  78.1 3.7 collective-permute-done.19.refs_22_
  85.8 4.8 %collective-permute-done.21.refs_23_ = bf16[2,912,128]{2,1,0:T(8,128)(2,1)S(1)} collective-permute-done((bf16[2,912,128]{2,1,0:T(8,128)(2,1)S(1)}, bf16[2,912,128]{2,1,0:T(8,128)(2,1)S(1)}, u32[]{:S(2)}, u32[]{:S(2)}) %collective-permute-start.21) | collective-permute-done | bytes 466976 | tf_op jit(solution)/shard_map/ppermute | solution.py:995
  91.3 10.1 %shard_map.136 = (bf16[512,1536]{1,0:T(8,128)(2,1)S(1)}, bf16[512,512]{1,0:T(8,128)(2,1)}, bf16[512,1024]{1,0:T(8,128)(2,1)}, bf16[512,2048]{1,0:T(8,128)(2,1)},...) custom-call(s32[7]{0:T(128)} %pad_add_fusion.1.place_ref, bf16[912,128]{1,0:T(8,128)(2,1)} %copy-done.43, ...), custom_call_target="tpu_custom_call" | custom-call | flops 8999999488 | tf_op jit(solution)/shard_map/pallas_call | solution.py:712
  101.4 5.1 %shard_map.137 = (bf16[512,1536]{1,0:T(8,128)(2,1)}, bf16[512,512]{1,0:T(8,128)(2,1)S(1)}, f32[8,512]{1,0:T(8,128)S(1)}) custom-call(s32[1]{0:T(128)} %bitcast.3.causal_ref.dec_ref, bf16[1536,512]{1,0:T(8,128)(2,1)} %bitcast.121, bf16[512,1536]{1,0:T(8,128)(2,1)S(1)} %get-tuple-element.651.wqkv, bf16[1536,128]{1,0:T(8,128)(2,1)S(1)} %fusion.7.fq, ...), custom_call_target="tpu_custom_call" | custom-call | flops 5000000000 | tf_op jit(solution)/shard_map/pallas_call | solution.py:712
  106.5 12.8 %conditional.5 = (bf16[512,2048]{1,0:T(8,128)(2,1)}, bf16[512,1024]{1,0:T(8,128)(2,1)}, bf16[512,1024]{1,0:T(8,128)(2,1)}, f32[512,512]{1,0:T(8,128)}, f32[512,5...) conditional(s32[]{:T(128)} %convert_element_type.419, ...), branch_computations={%region_0.1_spmd, %region_1.2_spmd} | conditional | flops 11000000512 | bytes 6291580 | solution.py:989
  106.8 12.1 %branch_0_fun.14 = (bf16[512,1024]{1,0:T(8,128)(2,1)}, bf16[512,1024]{1,0:T(8,128)(2,1)}, bf16[512,2048]{1,0:T(8,128)(2,1)}, bf16[512,2048]{1,0:T(8,128)(2,1)}, f32[512,512]{1,0:T(8,128)}, /*index=5*/f32[512,512]{1,0:T(8,128)}) custom-call(bf16[1536,512]{1,0:T(8,128)(2,1)} %get-tuple-element.200.x_ref, bf16[512,512]{1,0:T(8,128)(2,1)S(1)} %get-tuple-element.201.ctx_ref, ...), custom_call_target="tpu_custom_call" | custom-call | flops 8000000000 | tf_op jit(solution)/shard_map/cond/branch_0_fun/pallas_call | solution.py:712
  119.4 2.9 collective-permute-done.22
  122.3 30.8 %conditional.6 = (bf16[512,1024]{1,0:T(8,128)(2,1)}, bf16[512,512]{1,0:T(8,128)(2,1)}, f32[8,512]{1,0:T(8,128)S(1)}, bf16[512,1536]{1,0:T(8,128)(2,1)}, bf16[512...) conditional(s32[]{:T(128)} %convert_element_type.419, ...), branch_computations={%region_2.3_spmd, %region_3.4_spmd} | conditional | flops 24000000000 | bytes 31457568 | solution.py:989
  127.1 5.3 %branch_0_fun.16 = (bf16[512,1536]{1,0:T(8,128)(2,1)}, bf16[512,512]{1,0:T(8,128)(2,1)S(1)}, f32[8,512]{1,0:T(8,128)S(1)}) custom-call(s32[1]{0:T(128)} %get-tuple-element.237.causal_ref, bf16[1536,512]{1,0:T(8,128)(2,1)} %get-tuple-element.236.x_ref, bf16[512,1536]{1,0:T(8,128)(2,1)S(1)} %get-tuple-element.238.wqkv, ...), custom_call_target="tpu_custom_call" | custom-call | flops 5000000000 | tf_op jit(solution)/shard_map/cond/branch_0_fun/pallas_call | solution.py:712
  132.5 10.3 %branch_0_fun.17 = (bf16[512,1024]{1,0:T(8,128)(2,1)}, bf16[512,1024]{1,0:T(8,128)(2,1)}, bf16[512,2048]{1,0:T(8,128)(2,1)}, bf16[512,2048]{1,0:T(8,128)(2,1)}, f32[512,512]{1,0:T(8,128)}, /*index=5*/f32[512,512]{1,0:T(8,128)}) custom-call(bf16[1536,512]{1,0:T(8,128)(2,1)S(1)} %copy-done.19, bf16[512,512]{1,0:T(8,128)(2,1)S(1)} %get-tuple-element.804.ctx_ref, ...), custom_call_target="tpu_custom_call" | custom-call | flops 8000000000 | tf_op jit(solution)/shard_map/cond/branch_0_fun/pallas_call | solution.py:712
  142.8 5.3 %branch_0_fun.18 = (bf16[512,1536]{1,0:T(8,128)(2,1)}, bf16[512,512]{1,0:T(8,128)(2,1)}, f32[8,512]{1,0:T(8,128)S(1)}) custom-call(s32[1]{0:T(128)} %get-tuple-element.237.causal_ref, bf16[1536,512]{1,0:T(8,128)(2,1)S(1)} %copy-done.19, bf16[512,1536]{1,0:T(8,128)(2,1)S(1)} %get-tuple-element.238.wqkv, bf16[1536,128]{1,0:T(8,128)(2,1)S(1)} %get-tuple-element.239.fq, ...), custom_call_target="tpu_custom_call" | custom-call | flops 5000000000 | tf_op jit(solution)/shard_map/cond/branch_0_fun/pallas_call | solution.py:712
  153.0 4.0 %collective-permute-start.23 = (bf16[512,1024]{1,0:T(8,128)(2,1)}, bf16[512,1024]{1,0:T(8,128)(2,1)}, u32[]{:S(2)}, u32[]{:S(2)}) collective-permute-start(bf16[512,1024]{1,0:T(8,128)(2,1)} %get-tuple-element.663), channel_id=1, source_target_pairs={{0,16},{16,0},{1,17},{17,1},{2,18},{18,2},{3,19},{19,3},{4,20},{20... | collective-permute-start | bytes 3145736 | tf_op jit(solution)/shard_map/ppermute | solution.py:1136
  157.0 2.6 collective-permute-done.23.refs_9_
  159.7 29.2 %conditional.7 = (bf16[512,1024]{1,0:T(8,128)(2,1)S(1)}, bf16[512,2048]{1,0:T(8,128)(2,1)}, bf16[512,1024]{1,0:T(8,128)(2,1)}, f32[512,512]{1,0:T(8,128)}, f32[5...) conditional(s32[]{:T(128)} %convert_element_type.419, ...), branch_computations={%region_4.5_spmd, %region_5.6_spmd} | conditional | flops 24000000000 | bytes 39846196 | solution.py:989
  159.7 13.7 %branch_0_fun.20 = (bf16[512,1024]{1,0:T(8,128)(2,1)}, bf16[512,1024]{1,0:T(8,128)(2,1)S(1)}, bf16[512,2048]{1,0:T(8,128)(2,1)}, bf16[512,2048]{1,0:T(8,128)(2,1...) custom-call(bf16[1536,512]{1,0:T(8,128)(2,1)} %get-tuple-element.287.x_ref, bf16[512,512]{1,0:T(8,128)(2,1)} %get-tuple-element.288.ctx_ref, ...), custom_call_target="tpu_custom_call" | custom-call | flops 8000000000 | tf_op jit(solution)/shard_map/cond/branch_0_fun/pallas_call | solution.py:712
  173.5 8.5 %branch_0_fun.21 = (f32[512,512]{1,0:T(8,128)}, bf16[512,512]{1,0:T(8,128)(2,1)}, bf16[512,2048]{1,0:T(8,128)(2,1)}, bf16[512,512]{1,0:T(8,128)(2,1)}, bf16[512,512]{1,0:T(8,128)(2,1)}, /*index=5*/f32[8,512]{1,0:T(8,128)S(1)}) custom-call(bf16[512,1024]{1,0:T(8,128)(2,1)} %get-tuple-element.300.gkv_ref, f32[512,512]{1,0:T(8,128)S(1)} %copy-done.61, ...), custom_call_target="tpu_custom_call" | custom-call | flops 8000000000 | tf_op jit(solution)/shard_map/cond/branch_0_fun/pallas_call | solution.py:712
  188.9 3.2 collective-permute-start.24
  194.5 26.8 %conditional.8 = (bf16[512,512]{1,0:T(8,128)(2,1)}, bf16[512,512]{1,0:T(8,128)(2,1)}, f32[512,512]{1,0:T(8,128)S(1)}, bf16[512,2048]{1,0:T(8,128)(2,1)}, f32[8,5...) conditional(s32[]{:T(128)} %convert_element_type.419, ...), branch_computations={%region_6.7_spmd, %region_7.8_spmd} | conditional | flops 24000000000 | bytes 96 | solution.py:989
  194.5 10.3 %branch_0_fun.23 = (f32[512,512]{1,0:T(8,128)S(1)}, bf16[512,512]{1,0:T(8,128)(2,1)}, bf16[512,2048]{1,0:T(8,128)(2,1)}, bf16[512,512]{1,0:T(8,128)(2,1)}, bf16[...) custom-call(bf16[512,1024]{1,0:T(8,128)(2,1)} %get-tuple-element.337.gkv_ref, f32[512,512]{1,0:T(8,128)} %get-tuple-element.338.r1_any, ...), custom_call_target="tpu_custom_call" | custom-call | flops 8000000000 | tf_op jit(solution)/shard_map/cond/branch_0_fun/pallas_call | solution.py:712
  204.9 9.4 %branch_0_fun.24 = (bf16[512,512]{1,0:T(8,128)(2,1)}, bf16[512,1536]{1,0:T(8,128)(2,1)}) custom-call(s32[1]{0:T(128)} %get-tuple-element.352.causal_ref, bf16[512,1536]{1,0:T(8,128)(2,1)S(1)} %get-tuple-element.353.wqkv, bf16[1536,128]{1,0:T(8,128)(2,1)S(1)} %get-tuple-element.354.fq, bf16[1536,128]{1,0:T(8,128)(2,1)S(1)} %get-tuple-element.355.fk, ...), custom_call_target="tpu_custom_call" | custom-call | flops 1000000000 | tf_op jit(solution)/shard_map/cond/branch_0_fun/pallas_call | solution.py:712
  221.4 6.1 %collective-permute-start.25 = (bf16[512,1024]{1,0:T(8,128)(2,1)}, bf16[512,1024]{1,0:T(8,128)(2,1)}, u32[]{:S(2)}, u32[]{:S(2)}) collective-permute-start(bf16[512,1024]{1,0:T(8,128)(2,1)} %get-tuple-element.679), channel_id=1, source_target_pairs={{0,16},{16,0},{1,17},{17,1},{2,18},{18,2},{3,19},{19,3},{4,20},{20... | collective-permute-start | bytes 3145736 | tf_op jit(solution)/shard_map/ppermute | solution.py:1136
  227.6 2.6 collective-permute-done.25.refs_11_
  230.1 11.2 %conditional.9 = (bf16[512,512]{1,0:T(8,128)(2,1)}, bf16[512,512]{1,0:T(8,128)(2,1)}, f32[512,512]{1,0:T(8,128)}, bf16[512,2048]{1,0:T(8,128)(2,1)}, f32[8,512]{...) conditional(s32[]{:T(128)} %convert_element_type.419, (bf16[512,1024]{1,0:T(8,128)(2,1)}, ...), branch_computations={%region_8.9_spmd, %region_9.10_spmd} | conditional | flops 8999999488 | bytes 56 | solution.py:989
  230.1 10.8 %branch_0_fun.26 = (f32[512,512]{1,0:T(8,128)}, bf16[512,512]{1,0:T(8,128)(2,1)}, bf16[512,2048]{1,0:T(8,128)(2,1)}, bf16[512,512]{1,0:T(8,128)(2,1)}, bf16[512,512]{1,0:T(8,128)(2,1)}, /*index=5*/f32[8,512]{1,0:T(8,128)S(1)}) custom-call(bf16[512,1024]{1,0:T(8,128)(2,1)} %get-tuple-element.388.gkv_ref, f32[512,512]{1,0:T(8,128)} %get-tuple-element.389.r1_any, ...), custom_call_target="tpu_custom_call" | custom-call | flops 8000000000 | tf_op jit(solution)/shard_map/cond/branch_0_fun/pallas_call | solution.py:712
  241.4 12.6 %shard_map.138.refs_0_.refs_1_ = bf16[16384,128]{1,0:T(8,128)(2,1)S(1)} custom-call(s32[1]{0:T(128)} %bitcast.3.causal_ref.dec_ref, bf16[512,512]{1,0:T(8,128)(2,1)} %get-tuple-element.668.refs_0_.refs_13_, bf16[512,512]{1,0:T(8,128)(2,1)} %get-tuple-element.678.refs_1_.refs_14_, bf16[512,512]{1,0:T(8,128)(2,1)} %get-tuple-element.683.refs_2_, ...), custom_call_target="tpu_custom_call" | custom-call | flops 1000000000 | tf_op jit(solution)/shard_map/pallas_call | solution.py:712
  261.7 5.4 %shard_map.140.refs_0_.refs_1_ = bf16[6144,128]{1,0:T(8,128)(2,1)S(1)} custom-call(s32[1]{0:T(128)} %bitcast.3.causal_ref.dec_ref, bf16[512,512]{1,0:T(8,128)(2,1)} %copy-done.14, bf16[512,512]{1,0:T(8,128)(2,1)S(1)} %copy-done.12, bf16[512,512]{1,0:T(8,128)(2,1)} %get-tuple-element.662.refs_2_, f32[512,512]{1,0:T(8,128)} %get-tuple-element.676.refs_3_, ...), custom_call_target="tpu_custom_call" | custom-call | flops 1000000000 | tf_op jit(solution)/shard_map/pallas_call | solution.py:712
  269.4 8.3 %shard_map.142 = (bf16[512,512]{1,0:T(8,128)(2,1)S(1)}, bf16[512,1536]{1,0:T(8,128)(2,1)S(1)}) custom-call(s32[1]{0:T(128)} %bitcast.3.causal_ref.dec_ref, bf16[512,1536]{1,0:T(8,128)(2,1)S(1)} %get-tuple-element.651.wqkv, bf16[1536,128]{1,0:T(8,128)(2,1)S(1)} %fusion.7.fq, bf16[1536,128]{1,0:T(8,128)(2,1)S(1)} %fusion.21.fk, ...), custom_call_target="tpu_custom_call" | custom-call | flops 1000000000 | tf_op jit(solution)/shard_map/pallas_call | solution.py:712
  277.8 7.1 %shard_map.143 = (bf16[512,512]{1,0:T(8,128)(2,1)S(1)}, bf16[512,1536]{1,0:T(8,128)(2,1)S(1)}) custom-call(s32[1]{0:T(128)} %bitcast.3.causal_ref.dec_ref, bf16[512,1536]{1,0:T(8,128)(2,1)S(1)} %get-tuple-element.651.wqkv, bf16[1536,128]{1,0:T(8,128)(2,1)S(1)} %fusion.7.fq, bf16[1536,128]{1,0:T(8,128)(2,1)S(1)} %fusion.21.fk, ...), custom_call_target="tpu_custom_call" | custom-call | flops 1000000000 | tf_op jit(solution)/shard_map/pallas_call | solution.py:712
  284.9 4.9 %shard_map.144.refs_0_ = bf16[6144,128]{1,0:T(8,128)(2,1)S(1)} custom-call(s32[1]{0:T(128)} %bitcast.3.causal_ref.dec_ref, bf16[1536,512]{1,0:T(8,128)(2,1)S(1)} %bitcast.129, bf16[512,1536]{1,0:T(8,128)(2,1)} %get-tuple-element.716.refs_0_, bf16[512,1536]{1,0:T(8,128)(2,1)S(1)} %get-tuple-element.721.refs_1_.refs_4_, ...), custom_call_target="tpu_custom_call" | custom-call | flops 1000000000 | tf_op jit(solution)/shard_map/pallas_call | solution.py:712
  298.8 11.9 %collective-permute-done.36 = bf16[1,912,128]{2,1,0:T(8,128)(2,1)S(1)} collective-permute-done((bf16[1,912,128]{2,1,0:T(8,128)(2,1)S(1)}, bf16[1,912,128]{2,1,0:T(8,128)(2,1)S(1)}, u32[]{:S(2)}, u32[]{:S(2)}) %collective-permute-start.36) | collective-permute-done | bytes 233504 | tf_op jit(solution)/shard_map/ppermute | solution.py:995
  315.4 4.7 %collective-permute-done.38 = bf16[2,912,128]{2,1,0:T(8,128)(2,1)S(1)} collective-permute-done((bf16[2,912,128]{2,1,0:T(8,128)(2,1)S(1)}, bf16[2,912,128]{2,1,0:T(8,128)(2,1)S(1)}, u32[]{:S(2)}, u32[]{:S(2)}) %collective-permute-start.38) | collective-permute-done | bytes 466976 | tf_op jit(solution)/shard_map/ppermute | solution.py:995
  322.6 4.0 %collective-permute-start.40 = (bf16[2,912,128]{2,1,0:T(8,128)(2,1)S(1)}, bf16[2,912,128]{2,1,0:T(8,128)(2,1)S(1)}, u32[]{:S(2)}, u32[]{:S(2)}) collective-permute-start(bf16[2,912,128]{2,1,0:T(8,128)(2,1)S(1)} %fusion.16), channel_id=1, source_target_pairs={{0,4},{1,5},{2,6},{3,7},{16,20},{17,21},{18,22},{19,23}} | collective-permute-start | bytes 1400840 | tf_op jit(solution)/shard_map/ppermute | solution.py:1000
  328.4 5.9 %collective-permute-done.40 = bf16[2,912,128]{2,1,0:T(8,128)(2,1)S(1)} collective-permute-done((bf16[2,912,128]{2,1,0:T(8,128)(2,1)S(1)}, bf16[2,912,128]{2,1,0:T(8,128)(2,1)S(1)}, u32[]{:S(2)}, u32[]{:S(2)}) %collective-permute-start.40) | collective-permute-done | bytes 466976 | tf_op jit(solution)/shard_map/ppermute | solution.py:1000
  334.5 4.6 %collective-permute-start.41 = (bf16[2,912,128]{2,1,0:T(8,128)(2,1)S(1)}, bf16[2,912,128]{2,1,0:T(8,128)(2,1)S(1)}, u32[]{:S(2)}, u32[]{:S(2)}) collective-permute-start(bf16[2,912,128]{2,1,0:T(8,128)(2,1)S(1)} %get-tuple-element.759), channel_id=1, source_target_pairs={{0,4},{1,5},{2,6},{3,7},{4,8},{5,9},{6,10},{7,11},{16,20},{17,21},... | collective-permute-start | bytes 1400840 | tf_op jit(solution)/shard_map/ppermute | solution.py:1000
  339.2 2.6 maximum_select_fusion
  343.4 4.5 %collective-permute-done.41 = bf16[2,912,128]{2,1,0:T(8,128)(2,1)S(1)} collective-permute-done((bf16[2,912,128]{2,1,0:T(8,128)(2,1)S(1)}, bf16[2,912,128]{2,1,0:T(8,128)(2,1)S(1)}, u32[]{:S(2)}, u32[]{:S(2)}) %collective-permute-start.41) | collective-permute-done | bytes 466976 | tf_op jit(solution)/shard_map/ppermute | solution.py:1000
  348.3 4.4 %collective-permute-start.42 = (bf16[2,912,128]{2,1,0:T(8,128)(2,1)S(1)}, bf16[2,912,128]{2,1,0:T(8,128)(2,1)S(1)}, u32[]{:S(2)}, u32[]{:S(2)}) collective-permute-start(bf16[2,912,128]{2,1,0:T(8,128)(2,1)S(1)} %get-tuple-element.761), channel_id=1, source_target_pairs={{0,4},{1,5},{2,6},{3,7},{4,8},{5,9},{6,10},{7,11},{8,12},{9,13},{1... | collective-permute-start | bytes 1400840 | tf_op jit(solution)/shard_map/ppermute | solution.py:1000
  359.3 3.4 shard_map.146
  375.1 5.8 %collective-permute-start.52 = (f32[1,1]{1,0:T(1,128)}, f32[1,1]{1,0:T(1,128)}, u32[]{:S(2)}, u32[]{:S(2)}) collective-permute-start(f32[1,1]{1,0:T(1,128)} %add.389), channel_id=1, source_target_pairs={{0,4},{1,5},{2,6},{3,7},{4,0},{5,1},{6,2},{7,3},{8,12},{9,13},{10,... | collective-permute-start | bytes 20 | tf_op jit(solution)/shard_map/ppermute | solution.py:995
  382.2 3.7 collective-permute-start.54
  389.5 3.1 shard_map.147
  (292 shorter events, 92.8 us)
Async XLA Ops:
  3.8 15.2 %collective-permute-start.4 = (bf16[1824,128]{1,0:T(8,128)(2,1)S(1)}, bf16[1824,128]{1,0:T(8,128)(2,1)S(1)}, u32[]{:S(2)}, u32[]{:S(2)}) collective-permute-start(bf16[1824,128]{1,0:T(8,128)(2,1)S(1)} %shard_map.135), channel_id=1, source_target_pairs={{0,4},{1,5},{2,6},{3,7},{4,8},{5,9},{6,10},{7,11},{8,12},{9,13},{1... | collective-permute-start | bytes 1400840 | tf_op jit(solution)/shard_map/ppermute | solution.py:1000
  8.7 14.0 %collective-permute-start.5 = (bf16[1824,128]{1,0:T(8,128)(2,1)S(1)}, bf16[1824,128]{1,0:T(8,128)(2,1)S(1)}, u32[]{:S(2)}, u32[]{:S(2)}) collective-permute-start(bf16[1824,128]{1,0:T(8,128)(2,1)S(1)} %shard_map.135), channel_id=1, source_target_pairs={{4,0},{5,1},{6,2},{7,3},{8,4},{9,5},{10,6},{11,7},{12,8},{13,9},{1... | collective-permute-start | bytes 1400840 | tf_op jit(solution)/shard_map/ppermute | solution.py:1000
  10.2 7.2 %collective-permute-start.2 = (bf16[912,128]{1,0:T(8,128)(2,1)S(1)}, bf16[912,128]{1,0:T(8,128)(2,1)S(1)}, u32[]{:S(2)}, u32[]{:S(2)}) collective-permute-start(bf16[912,128]{1,0:T(8,128)(2,1)S(1)} %get-tuple-element.630.refs_3_), channel_id=1, source_target_pairs={{0,2},{1,3},{2,0},{3,1},{4,6},{5,7},{6,4},{7,5},{8,10},{9,11},{10,... | collective-permute-start | bytes 700424 | tf_op jit(solution)/shard_map/ppermute | solution.py:995
  11.8 7.2 %collective-permute-start = (bf16[912,128]{1,0:T(8,128)(2,1)S(1)}, bf16[912,128]{1,0:T(8,128)(2,1)S(1)}, u32[]{:S(2)}, u32[]{:S(2)}) collective-permute-start(bf16[912,128]{1,0:T(8,128)(2,1)S(1)} %get-tuple-element.627.refs_0_), channel_id=1, source_target_pairs={{0,1},{1,0},{2,3},{3,2},{4,5},{5,4},{6,7},{7,6},{8,9},{9,8},{10,11... | collective-permute-start | bytes 700424 | tf_op jit(solution)/shard_map/ppermute | solution.py:995
  17.5 24.2 %collective-permute-start.3 = (bf16[2,912,128]{2,1,0:T(8,128)(2,1)S(1)}, bf16[2,912,128]{2,1,0:T(8,128)(2,1)}, u32[]{:S(2)}, u32[]{:S(2)}) collective-permute-start(bf16[2,912,128]{2,1,0:T(8,128)(2,1)S(1)} %pad_maximum_fusion.2), channel_id=1, source_target_pairs={{0,1},{1,0},{2,3},{3,2},{4,5},{5,4},{6,7},{7,6},{8,9},{9,8},{10,11... | collective-permute-start | bytes 1400840 | tf_op jit(solution)/shard_map/ppermute | solution.py:995
  22.9 10.9 %collective-permute-start.6 = (bf16[912,128]{1,0:T(8,128)(2,1)S(1)}, bf16[912,128]{1,0:T(8,128)(2,1)S(1)}, u32[]{:S(2)}, u32[]{:S(2)}) collective-permute-start(bf16[912,128]{1,0:T(8,128)(2,1)S(1)} %get-tuple-element.633.refs_6_), channel_id=1, source_target_pairs={{0,1},{1,0},{2,3},{3,2},{4,5},{5,4},{6,7},{7,6},{8,9},{9,8},{10,11... | collective-permute-start | bytes 700424 | tf_op jit(solution)/shard_map/ppermute | solution.py:995
  25.3 16.4 %collective-permute-start.1 = (bf16[2,912,128]{2,1,0:T(8,128)(2,1)}, bf16[2,912,128]{2,1,0:T(8,128)(2,1)}, u32[]{:S(2)}, u32[]{:S(2)}) collective-permute-start(bf16[2,912,128]{2,1,0:T(8,128)(2,1)} %pad_maximum_fusion.1), channel_id=1, source_target_pairs={{0,2},{1,3},{2,0},{3,1},{4,6},{5,7},{6,4},{7,5},{8,10},{9,11},{10,... | collective-permute-start | bytes 1400840 | tf_op jit(solution)/shard_map/ppermute | solution.py:995
  26.9 15.5 %collective-permute-start.10 = (bf16[1824,128]{1,0:T(8,128)(2,1)S(1)}, bf16[1824,128]{1,0:T(8,128)(2,1)S(1)}, u32[]{:S(2)}, u32[]{:S(2)}) collective-permute-start(bf16[1824,128]{1,0:T(8,128)(2,1)S(1)} %collective-permute-done.4), channel_id=1, source_target_pairs={{4,8},{5,9},{6,10},{7,11},{8,12},{9,13},{10,14},{11,15},{20,24},{2... | collective-permute-start | bytes 1400840 | tf_op jit(solution)/shard_map/ppermute | solution.py:1000
  27.5 14.9 %collective-permute-start.11 = (bf16[1824,128]{1,0:T(8,128)(2,1)S(1)}, bf16[1824,128]{1,0:T(8,128)(2,1)S(1)}, u32[]{:S(2)}, u32[]{:S(2)}) collective-permute-start(bf16[1824,128]{1,0:T(8,128)(2,1)S(1)} %collective-permute-done.5), channel_id=1, source_target_pairs={{4,0},{5,1},{6,2},{7,3},{8,4},{9,5},{10,6},{11,7},{20,16},{21,17},... | collective-permute-start | bytes 1400840 | tf_op jit(solution)/shard_map/ppermute | solution.py:1000
  33.8 7.9 %collective-permute-start.7 = (bf16[912,128]{1,0:T(8,128)(2,1)S(1)}, bf16[912,128]{1,0:T(8,128)(2,1)S(1)}, u32[]{:S(2)}, u32[]{:S(2)}) collective-permute-start(bf16[912,128]{1,0:T(8,128)(2,1)S(1)} %get-tuple-element.636.refs_9_), channel_id=1, source_target_pairs={{0,2},{1,3},{2,0},{3,1},{4,6},{5,7},{6,4},{7,5},{8,10},{9,11},{10,... | collective-permute-start | bytes 700424 | tf_op jit(solution)/shard_map/ppermute | solution.py:995
  41.7 21.5 %collective-permute-start.9 = (bf16[2,912,128]{2,1,0:T(8,128)(2,1)S(1)}, bf16[2,912,128]{2,1,0:T(8,128)(2,1)S(1)}, u32[]{:S(2)}, u32[]{:S(2)}) collective-permute-start(bf16[2,912,128]{2,1,0:T(8,128)(2,1)S(1)} %pad_maximum_fusion.4), channel_id=1, source_target_pairs={{0,1},{1,0},{2,3},{3,2},{4,5},{5,4},{6,7},{7,6},{8,9},{9,8},{10,11... | collective-permute-start | bytes 1400840 | tf_op jit(solution)/shard_map/ppermute | solution.py:995
  42.6 14.5 %collective-permute-start.12 = (bf16[912,128]{1,0:T(8,128)(2,1)S(1)}, bf16[912,128]{1,0:T(8,128)(2,1)S(1)}, u32[]{:S(2)}, u32[]{:S(2)}) collective-permute-start(bf16[912,128]{1,0:T(8,128)(2,1)S(1)} %get-tuple-element.639.refs_12_), channel_id=1, source_target_pairs={{0,1},{1,0},{2,3},{3,2},{4,5},{5,4},{6,7},{7,6},{8,9},{9,8},{10,11... | collective-permute-start | bytes 700424 | tf_op jit(solution)/shard_map/ppermute | solution.py:995
  44.1 19.1 %collective-permute-start.8 = (bf16[2,912,128]{2,1,0:T(8,128)(2,1)S(1)}, bf16[2,912,128]{2,1,0:T(8,128)(2,1)S(1)}, u32[]{:S(2)}, u32[]{:S(2)}) collective-permute-start(bf16[2,912,128]{2,1,0:T(8,128)(2,1)S(1)} %pad_maximum_fusion.3), channel_id=1, source_target_pairs={{0,2},{1,3},{2,0},{3,1},{4,6},{5,7},{6,4},{7,5},{8,10},{9,11},{10,... | collective-permute-start | bytes 1400840 | tf_op jit(solution)/shard_map/ppermute | solution.py:995
  45.7 21.9 %collective-permute-start.16 = (bf16[1824,128]{1,0:T(8,128)(2,1)S(1)}, bf16[1824,128]{1,0:T(8,128)(2,1)S(1)}, u32[]{:S(2)}, u32[]{:S(2)}) collective-permute-start(bf16[1824,128]{1,0:T(8,128)(2,1)S(1)} %collective-permute-done.10), channel_id=1, source_target_pairs={{8,12},{9,13},{10,14},{11,15},{24,28},{25,29},{26,30},{27,31}} | collective-permute-start | bytes 1400840 | tf_op jit(solution)/shard_map/ppermute | solution.py:1000
  46.4 21.2 %collective-permute-start.17 = (bf16[1824,128]{1,0:T(8,128)(2,1)S(1)}, bf16[1824,128]{1,0:T(8,128)(2,1)S(1)}, u32[]{:S(2)}, u32[]{:S(2)}) collective-permute-start(bf16[1824,128]{1,0:T(8,128)(2,1)S(1)} %collective-permute-done.11), channel_id=1, source_target_pairs={{4,0},{5,1},{6,2},{7,3},{20,16},{21,17},{22,18},{23,19}} | collective-permute-start | bytes 1400840 | tf_op jit(solution)/shard_map/ppermute | solution.py:1000
  57.1 6.1 %collective-permute-start.13 = (bf16[912,128]{1,0:T(8,128)(2,1)S(1)}, bf16[912,128]{1,0:T(8,128)(2,1)S(1)}, u32[]{:S(2)}, u32[]{:S(2)}) collective-permute-start(bf16[912,128]{1,0:T(8,128)(2,1)S(1)} %get-tuple-element.642.refs_15_), channel_id=1, source_target_pairs={{0,2},{1,3},{2,0},{3,1},{4,6},{5,7},{6,4},{7,5},{8,10},{9,11},{10,... | collective-permute-start | bytes 700424 | tf_op jit(solution)/shard_map/ppermute | solution.py:995
  64.1 17.7 %collective-permute-start.15 = (bf16[2,912,128]{2,1,0:T(8,128)(2,1)}, bf16[2,912,128]{2,1,0:T(8,128)(2,1)}, u32[]{:S(2)}, u32[]{:S(2)}) collective-permute-start(bf16[2,912,128]{2,1,0:T(8,128)(2,1)} %pad_maximum_fusion.6), channel_id=1, source_target_pairs={{0,1},{1,0},{2,3},{3,2},{4,5},{5,4},{6,7},{7,6},{8,9},{9,8},{10,11... | collective-permute-start | bytes 1400840 | tf_op jit(solution)/shard_map/ppermute | solution.py:995
  66.1 15.7 %collective-permute-start.14 = (bf16[2,912,128]{2,1,0:T(8,128)(2,1)}, bf16[2,912,128]{2,1,0:T(8,128)(2,1)}, u32[]{:S(2)}, u32[]{:S(2)}) collective-permute-start(bf16[2,912,128]{2,1,0:T(8,128)(2,1)} %pad_maximum_fusion.5), channel_id=1, source_target_pairs={{0,2},{1,3},{2,0},{3,1},{4,6},{5,7},{6,4},{7,5},{8,10},{9,11},{10,... | collective-permute-start | bytes 1400840 | tf_op jit(solution)/shard_map/ppermute | solution.py:995
  67.9 10.2 %collective-permute-start.18 = (bf16[912,128]{1,0:T(8,128)(2,1)S(1)}, bf16[912,128]{1,0:T(8,128)(2,1)S(1)}, u32[]{:S(2)}, u32[]{:S(2)}) collective-permute-start(bf16[912,128]{1,0:T(8,128)(2,1)S(1)} %get-tuple-element.645.refs_18_), channel_id=1, source_target_pairs={{0,1},{1,0},{2,3},{3,2},{4,5},{5,4},{6,7},{7,6},{8,9},{9,8},{10,11... | collective-permute-start | bytes 700424 | tf_op jit(solution)/shard_map/ppermute | solution.py:995
  68.8 13.0 %collective-permute-start.19 = (bf16[912,128]{1,0:T(8,128)(2,1)S(1)}, bf16[912,128]{1,0:T(8,128)(2,1)S(1)}, u32[]{:S(2)}, u32[]{:S(2)}) collective-permute-start(bf16[912,128]{1,0:T(8,128)(2,1)S(1)} %get-tuple-element.648.refs_21_), channel_id=1, source_target_pairs={{0,2},{1,3},{2,0},{3,1},{4,6},{5,7},{6,4},{7,5},{8,10},{9,11},{10,... | collective-permute-start | bytes 700424 | tf_op jit(solution)/shard_map/ppermute | solution.py:995
  81.9 8.6 %collective-permute-start.21 = (bf16[2,912,128]{2,1,0:T(8,128)(2,1)S(1)}, bf16[2,912,128]{2,1,0:T(8,128)(2,1)S(1)}, u32[]{:S(2)}, u32[]{:S(2)}) collective-permute-start(bf16[2,912,128]{2,1,0:T(8,128)(2,1)S(1)} %pad_maximum_fusion.8), channel_id=1, source_target_pairs={{0,1},{1,0},{2,3},{3,2},{4,5},{5,4},{6,7},{7,6},{8,9},{9,8},{10,11... | collective-permute-start | bytes 1400840 | tf_op jit(solution)/shard_map/ppermute | solution.py:995
  82.0 9.3 %collective-permute-start.20 = (bf16[2,912,128]{2,1,0:T(8,128)(2,1)S(1)}, bf16[2,912,128]{2,1,0:T(8,128)(2,1)}, u32[]{:S(2)}, u32[]{:S(2)}) collective-permute-start(bf16[2,912,128]{2,1,0:T(8,128)(2,1)S(1)} %pad_maximum_fusion.7), channel_id=1, source_target_pairs={{0,2},{1,3},{2,0},{3,1},{4,6},{5,7},{6,4},{7,5},{8,10},{9,11},{10,... | collective-permute-start | bytes 1400840 | tf_op jit(solution)/shard_map/ppermute | solution.py:995
  153.0 6.6 %collective-permute-start.23 = (bf16[512,1024]{1,0:T(8,128)(2,1)}, bf16[512,1024]{1,0:T(8,128)(2,1)}, u32[]{:S(2)}, u32[]{:S(2)}) collective-permute-start(bf16[512,1024]{1,0:T(8,128)(2,1)} %get-tuple-element.663), channel_id=1, source_target_pairs={{0,16},{16,0},{1,17},{17,1},{2,18},{18,2},{3,19},{19,3},{4,20},{20... | collective-permute-start | bytes 3145736 | tf_op jit(solution)/shard_map/ppermute | solution.py:1136
  221.4 8.8 %collective-permute-start.25 = (bf16[512,1024]{1,0:T(8,128)(2,1)}, bf16[512,1024]{1,0:T(8,128)(2,1)}, u32[]{:S(2)}, u32[]{:S(2)}) collective-permute-start(bf16[512,1024]{1,0:T(8,128)(2,1)} %get-tuple-element.679), channel_id=1, source_target_pairs={{0,16},{16,0},{1,17},{17,1},{2,18},{18,2},{3,19},{19,3},{4,20},{20... | collective-permute-start | bytes 3145736 | tf_op jit(solution)/shard_map/ppermute | solution.py:1136
  256.0 28.8 %collective-permute-start.28 = (bf16[2,2,912,128]{3,2,0,1:T(8,128)(2,1)}, bf16[2,2,912,128]{3,2,0,1:T(8,128)(2,1)}, u32[]{:S(2)}, u32[]{:S(2)}) collective-permute-start(bf16[2,2,912,128]{3,2,0,1:T(8,128)(2,1)} %copy.15), channel_id=1, source_target_pairs={{0,2},{1,3},{2,0},{3,1},{4,6},{5,7},{6,4},{7,5},{8,10},{9,11},{10,... | collective-permute-start | bytes 2801672 | tf_op jit(solution)/shard_map/ppermute | solution.py:995
  258.6 26.3 %collective-permute-start.29 = (bf16[2,2,912,128]{3,2,0,1:T(8,128)(2,1)}, bf16[2,2,912,128]{3,2,0,1:T(8,128)(2,1)}, u32[]{:S(2)}, u32[]{:S(2)}) collective-permute-start(bf16[2,2,912,128]{3,2,0,1:T(8,128)(2,1)} %copy.16), channel_id=1, source_target_pairs={{0,1},{1,0},{2,3},{3,2},{4,5},{5,4},{6,7},{7,6},{8,9},{9,8},{10,11... | collective-permute-start | bytes 2801672 | tf_op jit(solution)/shard_map/ppermute | solution.py:995
  268.0 21.8 %collective-permute-start.26 = (bf16[1,2,912,128]{3,2,1,0:T(8,128)(2,1)S(1)}, bf16[1,2,912,128]{3,2,1,0:T(8,128)(2,1)S(1)}, u32[]{:S(2)}, u32[]{:S(2)}) collective-permute-start(bf16[1,2,912,128]{3,2,1,0:T(8,128)(2,1)S(1)} %get-tuple-element.712), channel_id=1, source_target_pairs={{0,2},{1,3},{2,0},{3,1},{4,6},{5,7},{6,4},{7,5},{8,10},{9,11},{10,... | collective-permute-start | bytes 1400840 | tf_op jit(solution)/shard_map/ppermute | solution.py:995
  268.5 21.3 %collective-permute-start.27 = (bf16[1,2,912,128]{3,2,1,0:T(8,128)(2,1)S(1)}, bf16[1,2,912,128]{3,2,1,0:T(8,128)(2,1)S(1)}, u32[]{:S(2)}, u32[]{:S(2)}) collective-permute-start(bf16[1,2,912,128]{3,2,1,0:T(8,128)(2,1)S(1)} %get-tuple-element.714), channel_id=1, source_target_pairs={{0,1},{1,0},{2,3},{3,2},{4,5},{5,4},{6,7},{7,6},{8,9},{9,8},{10,11... | collective-permute-start | bytes 1400840 | tf_op jit(solution)/shard_map/ppermute | solution.py:995
  290.6 21.7 %collective-permute-start.30 = (bf16[1,2,912,128]{3,2,1,0:T(8,128)(2,1)S(1)}, bf16[1,2,912,128]{3,2,1,0:T(8,128)(2,1)S(1)}, u32[]{:S(2)}, u32[]{:S(2)}) collective-permute-start(bf16[1,2,912,128]{3,2,1,0:T(8,128)(2,1)S(1)} %get-tuple-element.736), channel_id=1, source_target_pairs={{0,2},{1,3},{2,0},{3,1},{4,6},{5,7},{6,4},{7,5},{8,10},{9,11},{10,... | collective-permute-start | bytes 1400840 | tf_op jit(solution)/shard_map/ppermute | solution.py:995
  292.1 21.9 %collective-permute-start.32 = (bf16[1,2,912,128]{3,2,1,0:T(8,128)(2,1)S(1)}, bf16[1,2,912,128]{3,2,1,0:T(8,128)(2,1)S(1)}, u32[]{:S(2)}, u32[]{:S(2)}) collective-permute-start(bf16[1,2,912,128]{3,2,1,0:T(8,128)(2,1)S(1)} %get-tuple-element.738), channel_id=1, source_target_pairs={{0,1},{1,0},{2,3},{3,2},{4,5},{5,4},{6,7},{7,6},{8,9},{9,8},{10,11... | collective-permute-start | bytes 1400840 | tf_op jit(solution)/shard_map/ppermute | solution.py:995
  293.6 17.1 %collective-permute-start.36 = (bf16[1,912,128]{2,1,0:T(8,128)(2,1)S(1)}, bf16[1,912,128]{2,1,0:T(8,128)(2,1)S(1)}, u32[]{:S(2)}, u32[]{:S(2)}) collective-permute-start(bf16[1,912,128]{2,1,0:T(8,128)(2,1)S(1)} %fusion.24), channel_id=1, source_target_pairs={{0,1},{1,0},{2,3},{3,2},{4,5},{5,4},{6,7},{7,6},{8,9},{9,8},{10,11... | collective-permute-start | bytes 700424 | tf_op jit(solution)/shard_map/ppermute | solution.py:995
  294.3 17.1 %collective-permute-start.37 = (bf16[1,912,128]{2,1,0:T(8,128)(2,1)S(1)}, bf16[1,912,128]{2,1,0:T(8,128)(2,1)S(1)}, u32[]{:S(2)}, u32[]{:S(2)}) collective-permute-start(bf16[1,912,128]{2,1,0:T(8,128)(2,1)S(1)} %fusion.25), channel_id=1, source_target_pairs={{0,2},{1,3},{2,0},{3,1},{4,6},{5,7},{6,4},{7,5},{8,10},{9,11},{10,... | collective-permute-start | bytes 700424 | tf_op jit(solution)/shard_map/ppermute | solution.py:995
  296.1 24.0 %collective-permute-start.38 = (bf16[2,912,128]{2,1,0:T(8,128)(2,1)S(1)}, bf16[2,912,128]{2,1,0:T(8,128)(2,1)S(1)}, u32[]{:S(2)}, u32[]{:S(2)}) collective-permute-start(bf16[2,912,128]{2,1,0:T(8,128)(2,1)S(1)} %fusion.10), channel_id=1, source_target_pairs={{0,1},{1,0},{2,3},{3,2},{4,5},{5,4},{6,7},{7,6},{8,9},{9,8},{10,11... | collective-permute-start | bytes 1400840 | tf_op jit(solution)/shard_map/ppermute | solution.py:995
  310.7 10.7 %collective-permute-start.39 = (bf16[2,912,128]{2,1,0:T(8,128)(2,1)S(1)}, bf16[2,912,128]{2,1,0:T(8,128)(2,1)S(1)}, u32[]{:S(2)}, u32[]{:S(2)}) collective-permute-start(bf16[2,912,128]{2,1,0:T(8,128)(2,1)S(1)} %fusion.11), channel_id=1, source_target_pairs={{0,2},{1,3},{2,0},{3,1},{4,6},{5,7},{6,4},{7,5},{8,10},{9,11},{10,... | collective-permute-start | bytes 1400840 | tf_op jit(solution)/shard_map/ppermute | solution.py:995
  311.6 31.8 %collective-permute-start.43 = (bf16[2,912,128]{2,1,0:T(8,128)(2,1)S(1)}, bf16[2,912,128]{2,1,0:T(8,128)(2,1)S(1)}, u32[]{:S(2)}, u32[]{:S(2)}) collective-permute-start(bf16[2,912,128]{2,1,0:T(8,128)(2,1)S(1)} %maximum_bitcast_fusion.2), channel_id=1, source_target_pairs={{12,8},{13,9},{14,10},{15,11},{28,24},{29,25},{30,26},{31,27}} | collective-permute-start | bytes 1400840 | tf_op jit(solution)/shard_map/ppermute | solution.py:1000
  312.4 14.3 %collective-permute-start.31 = (bf16[1,912,128]{2,1,0:T(8,128)(2,1)S(1)}, bf16[1,912,128]{2,1,0:T(8,128)(2,1)S(1)}, u32[]{:S(2)}, u32[]{:S(2)}) collective-permute-start(bf16[1,912,128]{2,1,0:T(8,128)(2,1)S(1)} %fusion.22), channel_id=1, source_target_pairs={{0,1},{1,0},{2,3},{3,2},{4,5},{5,4},{6,7},{7,6},{8,9},{9,8},{10,11... | collective-permute-start | bytes 700424 | tf_op jit(solution)/shard_map/ppermute | solution.py:995
  314.0 12.8 %collective-permute-start.33 = (bf16[1,912,128]{2,1,0:T(8,128)(2,1)S(1)}, bf16[1,912,128]{2,1,0:T(8,128)(2,1)S(1)}, u32[]{:S(2)}, u32[]{:S(2)}) collective-permute-start(bf16[1,912,128]{2,1,0:T(8,128)(2,1)S(1)} %fusion.23), channel_id=1, source_target_pairs={{0,2},{1,3},{2,0},{3,1},{4,6},{5,7},{6,4},{7,5},{8,10},{9,11},{10,... | collective-permute-start | bytes 700424 | tf_op jit(solution)/shard_map/ppermute | solution.py:995
  322.6 11.7 %collective-permute-start.40 = (bf16[2,912,128]{2,1,0:T(8,128)(2,1)S(1)}, bf16[2,912,128]{2,1,0:T(8,128)(2,1)S(1)}, u32[]{:S(2)}, u32[]{:S(2)}) collective-permute-start(bf16[2,912,128]{2,1,0:T(8,128)(2,1)S(1)} %fusion.16), channel_id=1, source_target_pairs={{0,4},{1,5},{2,6},{3,7},{16,20},{17,21},{18,22},{19,23}} | collective-permute-start | bytes 1400840 | tf_op jit(solution)/shard_map/ppermute | solution.py:1000
  327.0 14.8 %collective-permute-start.34 = (bf16[2,912,128]{2,1,0:T(8,128)(2,1)S(1)}, bf16[2,912,128]{2,1,0:T(8,128)(2,1)S(1)}, u32[]{:S(2)}, u32[]{:S(2)}) collective-permute-start(bf16[2,912,128]{2,1,0:T(8,128)(2,1)S(1)} %maximum_bitcast_fusion.1), channel_id=1, source_target_pairs={{4,0},{5,1},{6,2},{7,3},{12,8},{13,9},{14,10},{15,11},{20,16},{21,... | collective-permute-start | bytes 1400840 | tf_op jit(solution)/shard_map/ppermute | solution.py:1000
  334.5 13.4 %collective-permute-start.41 = (bf16[2,912,128]{2,1,0:T(8,128)(2,1)S(1)}, bf16[2,912,128]{2,1,0:T(8,128)(2,1)S(1)}, u32[]{:S(2)}, u32[]{:S(2)}) collective-permute-start(bf16[2,912,128]{2,1,0:T(8,128)(2,1)S(1)} %get-tuple-element.759), channel_id=1, source_target_pairs={{0,4},{1,5},{2,6},{3,7},{4,8},{5,9},{6,10},{7,11},{16,20},{17,21},... | collective-permute-start | bytes 1400840 | tf_op jit(solution)/shard_map/ppermute | solution.py:1000
  341.9 14.3 %collective-permute-start.35 = (bf16[2,912,128]{2,1,0:T(8,128)(2,1)S(1)}, bf16[2,912,128]{2,1,0:T(8,128)(2,1)S(1)}, u32[]{:S(2)}, u32[]{:S(2)}) collective-permute-start(bf16[2,912,128]{2,1,0:T(8,128)(2,1)S(1)} %fusion.5), channel_id=1, source_target_pairs={{8,0},{9,1},{10,2},{11,3},{24,16},{25,17},{26,18},{27,19}} | collective-permute-start | bytes 1400840 | tf_op jit(solution)/shard_map/ppermute | solution.py:1000
  348.3 10.5 %collective-permute-start.42 = (bf16[2,912,128]{2,1,0:T(8,128)(2,1)S(1)}, bf16[2,912,128]{2,1,0:T(8,128)(2,1)S(1)}, u32[]{:S(2)}, u32[]{:S(2)}) collective-permute-start(bf16[2,912,128]{2,1,0:T(8,128)(2,1)S(1)} %get-tuple-element.761), channel_id=1, source_target_pairs={{0,4},{1,5},{2,6},{3,7},{4,8},{5,9},{6,10},{7,11},{8,12},{9,13},{1... | collective-permute-start | bytes 1400840 | tf_op jit(solution)/shard_map/ppermute | solution.py:1000
  352.7 6.0 %collective-permute-start.44 = (bf16[2,912,128]{2,1,0:T(8,128)(2,1)S(1)}, bf16[2,912,128]{2,1,0:T(8,128)(2,1)S(1)}, u32[]{:S(2)}, u32[]{:S(2)}) collective-permute-start(bf16[2,912,128]{2,1,0:T(8,128)(2,1)S(1)} %get-tuple-element.762), channel_id=1, source_target_pairs={{8,4},{9,5},{10,6},{11,7},{12,8},{13,9},{14,10},{15,11},{24,20},{2... | collective-permute-start | bytes 1400840 | tf_op jit(solution)/shard_map/ppermute | solution.py:1000
  364.3 7.7 %collective-permute-start.47 = (f32[1,1]{1,0:T(1,128)}, f32[1,1]{1,0:T(1,128)}, u32[]{:S(2)}, u32[]{:S(2)}) collective-permute-start(f32[1,1]{1,0:T(1,128)} %bitcast.46), channel_id=1, source_target_pairs={{0,3},{1,2},{2,1},{3,0},{4,7},{5,6},{6,5},{7,4},{8,11},{9,10},{10,... | collective-permute-start | bytes 20 | tf_op jit(solution)/shard_map/ppermute | solution.py:1015
  366.7 6.0 %collective-permute-start.48 = (f32[1,1]{1,0:T(1,128)}, f32[1,1]{1,0:T(1,128)}, u32[]{:S(2)}, u32[]{:S(2)}) collective-permute-start(f32[1,1]{1,0:T(1,128)} %bitcast.46), channel_id=1, source_target_pairs={{0,16},{1,17},{2,18},{3,19},{4,20},{5,21},{6,22},{7,23},{8,24},{9,... | collective-permute-start | bytes 20 | tf_op jit(solution)/shard_map/ppermute | solution.py:1015
  366.7 6.5 %collective-permute-start.49 = (f32[1,1]{1,0:T(1,128)}, f32[1,1]{1,0:T(1,128)}, u32[]{:S(2)}, u32[]{:S(2)}) collective-permute-start(f32[1,1]{1,0:T(1,128)} %bitcast.46), channel_id=1, source_target_pairs={{0,17},{1,16},{2,19},{3,18},{4,21},{5,20},{6,23},{7,22},{8,25},{9,... | collective-permute-start | bytes 20 | tf_op jit(solution)/shard_map/ppermute | solution.py:1015
  367.4 6.5 %collective-permute-start.50 = (f32[1,1]{1,0:T(1,128)}, f32[1,1]{1,0:T(1,128)}, u32[]{:S(2)}, u32[]{:S(2)}) collective-permute-start(f32[1,1]{1,0:T(1,128)} %bitcast.46), channel_id=1, source_target_pairs={{0,18},{1,19},{2,16},{3,17},{4,22},{5,23},{6,20},{7,21},{8,26},{9,... | collective-permute-start | bytes 20 | tf_op jit(solution)/shard_map/ppermute | solution.py:1015
  375.1 10.7 %collective-permute-start.52 = (f32[1,1]{1,0:T(1,128)}, f32[1,1]{1,0:T(1,128)}, u32[]{:S(2)}, u32[]{:S(2)}) collective-permute-start(f32[1,1]{1,0:T(1,128)} %add.389), channel_id=1, source_target_pairs={{0,4},{1,5},{2,6},{3,7},{4,0},{5,1},{6,2},{7,3},{8,12},{9,13},{10,... | collective-permute-start | bytes 20 | tf_op jit(solution)/shard_map/ppermute | solution.py:995
  (76 other events, 803.3 us)

commit v4 on v3

--- a/solution.py
+++ b/solution.py
@@ -26,8 +26,10 @@
 BF = jnp.bfloat16
 TILE = 16 * 128
 CHUNK = 512
+PART = 64
 SEG_BITS = 12
 POS_BITS = 9
+DEC_FIRST = True
 LOOP = False
 
 MATS = {}
@@ -75,12 +77,22 @@
     return center * rstd, rstd
 
 
-def ln_back(grad, hat, rstd, gain):
+def ln_back(grad, resid, gain):
+    hat, rstd = ln_parts(resid)
     scaled = grad * gain
     first = jnp.mean(scaled, axis=-1, keepdims=True)
     second = jnp.mean(scaled * hat, axis=-1, keepdims=True)
     grad_resid = rstd * (scaled - first - hat * second)
     return grad_resid, jnp.sum(grad * hat, axis=0, keepdims=True), jnp.sum(grad, axis=0, keepdims=True)
+
+
+def by_rows(body):
+    total = None
+    for c in range(ROW // PART):
+        got = body(slice(c * PART, (c + 1) * PART))
+        if got is not None:
+            total = got if total is None else tuple(a + b for a, b in zip(total, got))
+    return total
 
 
 def gelu_both(pre):
@@ -230,48 +242,32 @@
         move(g, 0)
 
 
-def chunks(body, total_s, loop):
-    if not loop:
-        parts = [body(slice(c * CHUNK, (c + 1) * CHUNK)) for c in range(FF // CHUNK)]
-        return sum(parts[1:], parts[0])
-
-    def step(c, _):
-        part = body(pl.ds(pl.multiple_of(c * CHUNK, CHUNK), CHUNK))
-        total_s[...] = jnp.where(c == 0, 0.0, total_s[...]) + part
-        return 0
-
-    lax.fori_loop(0, FF // CHUNK, step, 0)
-    return total_s[...]
-
-
-def ffn_fwd(hidden_ref, w_up, w_down, act_ref, slope_ref, total_s, loop):
-    def body(cols):
+def ffn_fwd(hidden_ref, w_up, w_down, act_ref, slope_ref, total_s):
+    for c in range(FF // CHUNK):
+        cols = slice(c * CHUNK, (c + 1) * CHUNK)
         act, slope = gelu_both(dot_nn(hidden_ref[...], w_up[:, cols]))
-        act_b = act.astype(BF)
-        act_ref[:, cols] = act_b
+        act_ref[:, cols] = act.astype(BF)
         slope_ref[:, cols] = slope.astype(slope_ref.dtype)
-        return dot_nn(act_b, w_down[cols, :])
-
-    return chunks(body, total_s, loop)
-
-
-def ffn_bwd(branch_ref, w_up, w_down, slope_ref, dz_ref, total_s, loop):
-    def body(cols):
+    total_s[...] = dot_nn(act_ref[...], w_down[...])
+
+
+def ffn_bwd(branch_ref, w_up, w_down, slope_ref, dz_ref, total_s):
+    for c in range(FF // CHUNK):
+        cols = slice(c * CHUNK, (c + 1) * CHUNK)
         grad_act = dot_nt(branch_ref[...], w_down[cols, :])
-        grad_pre = (grad_act * slope_ref[:, cols].astype(F32)).astype(BF)
-        dz_ref[:, cols] = grad_pre
-        return dot_nt(grad_pre, w_up[:, cols])
-
-    return chunks(body, total_s, loop)
-
-
-def self_head(dy1, r1_ref, vec, w_out, dr1_ref, dctx_ref, gvec):
-    hat1, rstd1 = ln_parts(r1_ref[...])
-    dr1, gain1, shift1 = ln_back(dy1, hat1, rstd1, vec[0:1, :])
-    dr1_ref[...] = dr1
-    dctx_ref[...] = dot_nt(dr1.astype(BF), w_out[...]).astype(BF)
-    gvec[0:1, :] = gain1
-    gvec[1:2, :] = shift1
+        dz_ref[:, cols] = (grad_act * slope_ref[:, cols].astype(F32)).astype(BF)
+    total_s[...] = dot_nt(dz_ref[...], w_up[...])
+
+
+def self_head(grad_s, more_s, r1_ref, vec, w_out, dr1_ref, half_s, dctx_ref, gvec):
+    def body(rows):
+        dr1, gain, shift = ln_back(grad_s[rows, :] + more_s[rows, :], r1_ref[rows, :], vec[0:1, :])
+        dr1_ref[rows, :] = dr1
+        half_s[rows, :] = dr1.astype(BF)
+        return gain, shift
+
+    gvec[0:1, :], gvec[1:2, :] = by_rows(body)
+    dctx_ref[...] = dot_nt(half_s[...], w_out[...]).astype(BF)
 
 
 def copies(sources, targets, sems):
@@ -464,32 +460,40 @@
 
 
 def enc_ffn_kernel(
-    loop, x_ref, ctx_ref, vec, w_out, w_up_any, w_down_any, w_cross_any,
+    x_ref, ctx_ref, vec, w_out, w_up_any, w_down_any, w_cross_any,
     mem_ref, kv_ref, act_any, slope_any, r1_any, r2_any,
     hid_s, total_s, act_s, slope_s, r1_s, r2_s, w_up, w_down, w_cross, in_sems, out_sems,
 ):
     made = copies((w_up_any, w_down_any, w_cross_any), (w_up, w_down, w_cross), in_sems)
     sent, emit = emitter(out_sems)
-    r1 = x_ref[...].astype(F32) + dot_nn(ctx_ref[...], w_out[...])
-    r1_s[...] = r1
+    total_s[...] = dot_nn(ctx_ref[...], w_out[...])
+
+    def first(rows):
+        r1 = x_ref[rows, :].astype(F32) + total_s[rows, :]
+        r1_s[rows, :] = r1
+        y1 = ln_parts(r1)[0] * vec[0:1, :] + vec[1:2, :]
+        r2_s[rows, :] = y1
+        hid_s[rows, :] = y1.astype(BF)
+
+    by_rows(first)
     emit(r1_s, r1_any)
-    hat, _ = ln_parts(r1)
-    y1 = hat * vec[0:1, :] + vec[1:2, :]
-    hid_s[...] = y1.astype(BF)
-    r2_s[...] = y1
     made[0].wait()
     made[1].wait()
-    r2 = r2_s[...] + ffn_fwd(hid_s, w_up, w_down, act_s, slope_s, total_s, loop)
+    ffn_fwd(hid_s, w_up, w_down, act_s, slope_s, total_s)
     emit(act_s, act_any)
     emit(slope_s, slope_any)
-    r2_s[...] = r2
+
+    def second(rows):
+        r2 = r2_s[rows, :] + total_s[rows, :]
+        r2_s[rows, :] = r2
+        mem = (ln_parts(r2)[0] * vec[2:3, :] + vec[3:4, :]).astype(BF)
+        mem_ref[rows, :D] = mem
+        mem_ref[rows, D:] = mem
+
+    by_rows(second)
     emit(r2_s, r2_any)
-    hat, _ = ln_parts(r2)
-    mem = (hat * vec[2:3, :] + vec[3:4, :]).astype(BF)
-    mem_ref[:, :D] = mem
-    mem_ref[:, D:] = mem
     made[2].wait()
-    kv_ref[...] = dot_nn(mem, w_cross[...]).astype(BF)
+    kv_ref[...] = dot_nn(mem_ref[:, :D], w_cross[...]).astype(BF)
     for one in sent:
         one.wait()
 
@@ -498,58 +502,72 @@
     row, x_ref, ctx1_ref, kv_ref, go_any, vec, w_cross, w_out, w_up_any, w_down_any, fq, fk,
     out_any, gkv_ref, dr1_ref, dctx1_ref, act_any, dz_any, hid_any, br_any, left_any, right_ref, gvec,
     cq_s, lse_s, wide_s, dctx_s, dcq_s, dqt_s, kt_s, slope_s, act_s, dz_s, hid_s, br_s, left_s, out_s,
-    go_ref, w_up, w_down, keep_s, r1_s, in_sems, out_sems,
+    go_ref, w_up, w_down, keep_s, r1_s, r2_s, total_s, in_sems, out_sems,
 ):
     up_copy, down_copy, go_copy = copies(
         (w_up_any, w_down_any, go_any.at[pl.ds(row * ROW, ROW)]), (w_up, w_down, go_ref), in_sems
     )
     sent, emit = emitter(out_sems)
-    r1 = x_ref[...].astype(F32) + dot_nn(ctx1_ref[...], w_out[...])
-    r1_s[...] = r1
-    hat1, _ = ln_parts(r1)
-    y1 = hat1 * vec[0:1, :] + vec[1:2, :]
-    y1_b = y1.astype(BF)
-    left_s[:, :D] = y1_b
-    cq_s[...] = dot_nn(y1_b, w_cross[:, :D]).astype(BF)
+    total_s[...] = dot_nn(ctx1_ref[...], w_out[...])
+
+    def first(rows):
+        r1 = x_ref[rows, :].astype(F32) + total_s[rows, :]
+        r1_s[rows, :] = r1
+        y1 = ln_parts(r1)[0] * vec[0:1, :] + vec[1:2, :]
+        keep_s[rows, :] = y1
+        left_s[rows, :D] = y1.astype(BF)
+
+    by_rows(first)
+    cq_s[...] = dot_nn(left_s[:, :D], w_cross[:, :D]).astype(BF)
     ctx_s = left_s.at[:, D:]
     attend_fwd(None, cq_s, 0, kv_ref, 0, kv_ref, D, fq[...], fk[...], ctx_s, lse_s, wide_s, None)
     emit(left_s, left_any)
-    r2 = y1 + dot_nn(ctx_s[...], w_cross[:, D:])
-    hat2, rstd2 = ln_parts(r2)
-    y2 = hat2 * vec[2:3, :] + vec[3:4, :]
-    hid_s[...] = y2.astype(BF)
-    keep_s[...] = y2
+    total_s[...] = dot_nn(ctx_s[...], w_cross[:, D:])
+
+    def second(rows):
+        r2 = keep_s[rows, :] + total_s[rows, :]
+        r2_s[rows, :] = r2
+        y2 = ln_parts(r2)[0] * vec[2:3, :] + vec[3:4, :]
+        keep_s[rows, :] = y2
+        hid_s[rows, :] = y2.astype(BF)
+
+    by_rows(second)
     emit(hid_s, hid_any)
     up_copy.wait()
     down_copy.wait()
-    r3 = keep_s[...] + ffn_fwd(hid_s, w_up, w_down, act_s, slope_s, None, False)
+    ffn_fwd(hid_s, w_up, w_down, act_s, slope_s, total_s)
     emit(act_s, act_any)
-    hat3, rstd3 = ln_parts(r3)
-    out_s[...] = (hat3 * vec[4:5, :] + vec[5:6, :]).astype(BF)
+    go_copy.wait()
+
+    def third(rows):
+        r3 = keep_s[rows, :] + total_s[rows, :]
+        out_s[rows, :] = (ln_parts(r3)[0] * vec[4:5, :] + vec[5:6, :]).astype(BF)
+        dr3, gain, shift = ln_back(go_ref[rows, :].astype(F32), r3, vec[4:5, :])
+        keep_s[rows, :] = dr3
+        br_s[rows, :] = dr3.astype(BF)
+        return gain, shift
+
+    gvec[4:5, :], gvec[5:6, :] = by_rows(third)
     emit(out_s, out_any)
-
-    go_copy.wait()
-    dr3, gain3, shift3 = ln_back(go_ref[...].astype(F32), hat3, rstd3, vec[4:5, :])
-    br_s[...] = dr3.astype(BF)
     emit(br_s, br_any)
-    keep_s[...] = dr3
-    dy2 = keep_s[...] + ffn_bwd(br_s, w_up, w_down, slope_s, dz_s, None, False)
+    ffn_bwd(br_s, w_up, w_down, slope_s, dz_s, total_s)
     emit(dz_s, dz_any)
-    dr2, gain2, shift2 = ln_back(dy2, hat2, rstd2, vec[2:3, :])
-    dr2_b = dr2.astype(BF)
-    right_ref[:, D:] = dr2_b
-    dctx_s[...] = dot_nt(dr2_b, w_cross[:, D:]).astype(BF)
+
+    def fourth(rows):
+        dr2, gain, shift = ln_back(keep_s[rows, :] + total_s[rows, :], r2_s[rows, :], vec[2:3, :])
+        keep_s[rows, :] = dr2
+        right_ref[rows, D:] = dr2.astype(BF)
+        return gain, shift
+
+    gvec[2:3, :], gvec[3:4, :] = by_rows(fourth)
+    dctx_s[...] = dot_nt(right_ref[:, D:], w_cross[:, D:]).astype(BF)
     attend_bwd(
         None, cq_s, 0, kv_ref, 0, kv_ref, D, fq[...], fk[...], lse_s, dctx_s,
         ((dcq_s, 0), (gkv_ref, 0), (gkv_ref, D)), dqt_s, kt_s, None,
     )
-    dcq = dcq_s[...]
-    right_ref[:, :D] = dcq
-    self_head(dr2 + dot_nt(dcq, w_cross[:, :D]), r1_s, vec, w_out, dr1_ref, dctx1_ref, gvec)
-    gvec[2:3, :] = gain2
-    gvec[3:4, :] = shift2
-    gvec[4:5, :] = gain3
-    gvec[5:6, :] = shift3
+    right_ref[:, :D] = dcq_s[...]
+    total_s[...] = dot_nt(dcq_s[...], w_cross[:, :D])
+    self_head(keep_s, total_s, r1_s, vec, w_out, dr1_ref, dctx_s, dctx1_ref, gvec)
     for one in sent:
         one.wait()
 
@@ -557,31 +575,32 @@
 def enc_back_kernel(
     gkv_ref, r1_any, r2_ref, slope_any, vec, w_cross, w_out_any, w_up_any, w_down_any,
     dr1_ref, dctx1_ref, dz_any, hid_any, br_any, gvec,
-    keep_s, total_s, r1_ref, slope_s, w_out, w_up, w_down, dz_s, hid_s, br_s, in_sems, out_sems,
+    keep_s, total_s, r1_ref, slope_s, w_out, w_up, w_down, dz_s, hid_s, br_s, half_s, in_sems, out_sems,
 ):
     made = copies(
         (r1_any, slope_any, w_down_any, w_up_any, w_out_any), (r1_ref, slope_s, w_down, w_up, w_out), in_sems
     )
     sent, emit = emitter(out_sems)
-    dmem = dot_nt(gkv_ref[...], w_cross[...])
-    hat2, rstd2 = ln_parts(r2_ref[...])
-    dr2, gain2, shift2 = ln_back(dmem, hat2, rstd2, vec[2:3, :])
-    br_s[...] = dr2.astype(BF)
+    total_s[...] = dot_nt(gkv_ref[...], w_cross[...])
+    made[0].wait()
+
+    def first(rows):
+        dr2, gain, shift = ln_back(total_s[rows, :], r2_ref[rows, :], vec[2:3, :])
+        keep_s[rows, :] = dr2
+        br_s[rows, :] = dr2.astype(BF)
+        hid_s[rows, :] = (ln_parts(r1_ref[rows, :])[0] * vec[0:1, :] + vec[1:2, :]).astype(BF)
+        return gain, shift
+
+    gvec[2:3, :], gvec[3:4, :] = by_rows(first)
+    gvec[4:8, :] = jnp.zeros((4, D), F32)
     emit(br_s, br_any)
-    keep_s[...] = dr2
-    made[0].wait()
-    hat1, _ = ln_parts(r1_ref[...])
-    hid_s[...] = (hat1 * vec[0:1, :] + vec[1:2, :]).astype(BF)
     emit(hid_s, hid_any)
     for one in made[1:4]:
         one.wait()
-    dy1 = keep_s[...] + ffn_bwd(br_s, w_up, w_down, slope_s, dz_s, total_s, True)
+    ffn_bwd(br_s, w_up, w_down, slope_s, dz_s, total_s)
     emit(dz_s, dz_any)
     made[4].wait()
-    self_head(dy1, r1_ref, vec, w_out, dr1_ref, dctx1_ref, gvec)
-    gvec[2:3, :] = gain2
-    gvec[3:4, :] = shift2
-    gvec[4:8, :] = jnp.zeros((4, D), F32)
+    self_head(keep_s, total_s, r1_ref, vec, w_out, dr1_ref, half_s, dctx1_ref, gvec)
     for one in sent:
         one.wait()
 
@@ -807,7 +826,7 @@
     names = ("mem", "kv", "act", "slope", "r1", "r2")
     vm = pltpu.VMEM
     got = kernel_call(
-        functools.partial(enc_ffn_kernel, row > 0),
+        enc_ffn_kernel,
         micros=8,
         grid=(1,),
         in_specs=[at_row(row, D), at_row(0, D), whole_spec((6, D)), whole_spec((D, D))] + [ANYWHERE] * 3,
@@ -840,8 +859,8 @@
             vm((ROW, D), BF), vm((HEADS, ROW), F32), vm((ROW, 128), F32), vm((ROW, D), BF), vm((ROW, D), BF),
             vm((D, ROW), F32), vm((D, ROW), BF), vm((ROW, FF), BF), vm((ROW, FF), BF), vm((ROW, FF), BF), vm((ROW, D), BF),
             vm((ROW, D), BF), vm((ROW, 2 * D), BF), vm((ROW, D), BF), vm((ROW, D), BF), vm((D, FF), BF),
-            vm((FF, D), BF), vm((ROW, D), F32), vm((ROW, D), F32), pltpu.SemaphoreType.DMA((3,)),
-            pltpu.SemaphoreType.DMA((6,)),
+            vm((FF, D), BF), vm((ROW, D), F32), vm((ROW, D), F32), vm((ROW, D), F32), vm((ROW, D), F32),
+            pltpu.SemaphoreType.DMA((3,)), pltpu.SemaphoreType.DMA((6,)),
         ],
         compiler_params=params_of(60),
     )(x, fwd["ctx"], kv, go, vec, w["cross"], w["out"], w["up"], w["down"], fq, fk)
@@ -863,7 +882,7 @@
         out_shape=row_shapes(-D, D, FF, D, D) + [shape_of((8, D), F32)],
         scratch_shapes=[
             vm((ROW, D), F32), vm((ROW, D), F32), vm((ROW, D), F32), vm((ROW, FF), BF), vm((D, D), BF), vm((D, FF), BF),
-            vm((FF, D), BF), vm((ROW, FF), BF), vm((ROW, D), BF), vm((ROW, D), BF), pltpu.SemaphoreType.DMA((5,)),
+            vm((FF, D), BF), vm((ROW, FF), BF), vm((ROW, D), BF), vm((ROW, D), BF), vm((ROW, D), BF), pltpu.SemaphoreType.DMA((5,)),
             pltpu.SemaphoreType.DMA((3,)),
         ],
         compiler_params=params_of(32),
@@ -958,7 +977,7 @@
     return kernel_call(lambda *refs: None, out_specs=[ANYWHERE] * len(shapes), out_shape=list(shapes))()
 
 
-def either(is_decoder, dec, enc):
+def either(is_decoder, dec, enc, dec_first=False):
     thunks = (enc, dec)
     made = [jax.eval_shape(t) for t in thunks]
     slots, where = [], []
@@ -986,7 +1005,10 @@
 
         return run
 
-    got = lax.cond(is_decoder, branch(1), branch(0))
+    if dec_first:
+        got = lax.cond(jnp.logical_not(is_decoder), branch(0), branch(1))
+    else:
+        got = lax.cond(is_decoder, branch(1), branch(0))
     back = [jax.tree.unflatten(jax.tree.structure(made[i]), [got[s] for s in where[i]]) for i in range(2)]
     return back[1], back[0]
 
@@ -1135,37 +1157,38 @@
     def swapped(value):
         return lax.ppermute(value, "section", [(0, 1), (1, 0)])
 
-    fwd, first = either(
-        is_decoder, lambda: [forward(r) for r in range(1, count)], lambda: enc_ffn(0, x, first_fwd, w, vec)
-    )
-    dec_fwd, enc_fwd = [first_fwd, *fwd], [first_fwd]
+    fwd = [first_fwd]
+    first = enc_ffn(0, x, first_fwd, w, vec)
     kept, dec_rows, enc_rows, back, enc_self = [first], [], [], [], []
     kv_in = swapped(first["kv"])
+    if count > 1:
+        fwd.append(forward(1))
+        kv_in, fwd[1] = tied(kv_in, fwd[1])
     for row in range(count):
 
         def dec_make():
-            got = dec_call(row, x, dec_fwd[row], kv_in, out_grad, w, vec, fq, fk_src)
+            got = dec_call(row, x, fwd[row], kv_in, out_grad, w, vec, fq, fk_src)
             return got.pop("gkv"), got
 
         def enc_make():
-            fwd, ahead, done, far = [], [], [], []
-            if row + 1 < count:
-                fwd = [forward(r) for r in range(1, count)] if row == 0 else []
-                ahead = [enc_ffn(row + 1, x, fwd[0] if row == 0 else enc_fwd[row + 1], w, vec)]
-            if row:
-                done = [enc_back(back[row - 1], kept[row - 1], w, vec)]
+            ahead = [enc_ffn(row + 1, x, fwd[row + 1], w, vec)] if row + 1 < count else []
+            done = [enc_back(back[row - 1], kept[row - 1], w, vec)] if row else []
+            far = []
             if row and row == count - 1:
-                far = [self_back(flag, 0, [{**enc_rows[0], **enc_fwd[0]} if enc_rows else {**done[0], **enc_fwd[0]}], w, fq, fk_self)]
-            return [k.pop("kv") for k in ahead], (fwd, ahead, done, far)
-
-        (sent, got), (_, (fwd, ahead, done, far)) = either(is_decoder, dec_make, enc_make)
+                far = [self_back(flag, 0, [{**(enc_rows or done)[0], **fwd[0]}], w, fq, fk_self)]
+            return [k.pop("kv") for k in ahead], (ahead, done, far)
+
+        (sent, got), (_, (ahead, done, far)) = either(is_decoder, dec_make, enc_make, DEC_FIRST)
         dec_rows.append(got)
-        enc_fwd += fwd
         enc_rows += done
         kept += ahead
         enc_self += far
         kv_in = swapped(sent)
+        if row + 2 < count:
+            fwd.append(forward(row + 2))
+            kv_in, fwd[-1] = tied(kv_in, fwd[-1])
         back.append(kv_in)
+    dec_fwd = enc_fwd = fwd
 
     last = count - 1
     dec_self, done = either(
@@ -1234,11 +1257,10 @@
         mine = lax.psum_scatter(stacked, "batch", scatter_dimension=0, tiled=True).astype(F32)
     grad_share, squares = unshifted(shift, jnp.pad(mine, ((0, 8), (0, 0))), share)
 
-    square_sum = jnp.sum(squares)
     if custom:
-        square_sum = over_all(square_sum.reshape(1, 1))[0, 0]
+        square_sum = jnp.sum(over_all(squares))
     else:
-        square_sum = lax.psum(square_sum, ("section", "batch"))
+        square_sum = lax.psum(jnp.sum(squares), ("section", "batch"))
     grad_norm = jnp.sqrt(square_sum)
     clip_factor = MAXNORM / jnp.maximum(grad_norm, MAXNORM)
     param_step, new_first, new_second = adam(clip_factor[None], grad_share, first_moment, second_moment, share)

time: 397 us -> 392 us (0.987)
  local copies, waits for them, and re-layouts: 8.24 us -> 15.8 us
  starting transfers between devices: 92.4 us -> 85 us
  between operations: 10.1 us -> 4.04 us
  Pallas kernels: 150 us -> 155 us
    another operation x5 -> x1, loops' own time: 25.2 us -> 0.22 us  [either(): got = lax.cond(is_decoder, branch(1), branch(0))]
    another operation x0 -> x3, loops' own time: none -> 23.5 us  [either(): got = lax.cond(jnp.logical_not(is_decoder), branch(0), branch(1))]
    unnamed x112 -> x146, local copies, waits for them, and re-layouts: 3.51 us -> 12.5 us
    ppermute x13, waiting for transfers between devices: 17.3 us -> 22.3 us  [line_permute(): return lax.ppermute(value, 'batch', pairs)]
    ppermute x4, waiting for transfers between devices: 10.5 us -> 5.55 us  [swapped(): return lax.ppermute(value, 'section', [(0, 1), (1, 0)])]
    pallas_call x27 -> x26, Pallas kernels: 150 us -> 155 us  [kernel_call(): return lambda *operands: tuple(call(*operands))]
    ppermute x31, waiting for transfers between devices: 57.6 us -> 52.8 us  [plane_permute(): return lax.ppermute(value, 'batch', [(i, i ^ step) for i in range(16)])]
    ppermute x4, starting transfers between devices: 13.4 us -> 9.04 us  [swapped(): return lax.ppermute(value, 'section', [(0, 1), (1, 0)])]
  transfers between devices with their start and end apart: 55 -> 55, of which waited for: 21 -> 25; matrix products, arithmetic and copies ran while one was open for 6% -> 6% of each run, Pallas kernels for 7% -> 11%
where the time goes in v4:
time: 392 us; the launch traced here: 388 us
  Pallas kernels  155 us (40%)
  starting transfers between devices  85 us (22%)
  waiting for transfers between devices  82.4 us (21%)
  loops' own time  23.7 us (6%)
  other arithmetic  22.4 us (6%)
  local copies, waits for them, and re-layouts  15.8 us (4%)
  between operations  4.04 us (1%)
    pallas_call x26, Pallas kernels, kernel_call(): return lambda *operands: tuple(call(*operands))  155 us
    ppermute x31, waiting for transfers between devices, plane_permute(): return lax.ppermute(value, 'batch', [(i, i ^ step) for i in range(16)])  52.8 us
    ppermute x31, starting transfers between devices, plane_permute(): return lax.ppermute(value, 'batch', [(i, i ^ step) for i in range(16)])  41.3 us
    ppermute x13, starting transfers between devices, line_permute(): return lax.ppermute(value, 'batch', pairs)  26.7 us
    another operation x3, loops' own time, either(): got = lax.cond(jnp.logical_not(is_decoder), branch(0), branch(1))  23.5 us
    ppermute x13, waiting for transfers between devices, line_permute(): return lax.ppermute(value, 'batch', pairs)  22.3 us
    unnamed x146, local copies, waits for them, and re-layouts  12.5 us
    ppermute x4, starting transfers between devices, swapped(): return lax.ppermute(value, 'section', [(0, 1), (1, 0)])  9.04 us
  transfers between devices with their start and end apart: 55, of which 25 were waited for; matrix products, arithmetic and copies ran while one was open for 6% of the time, Pallas kernels for 11%

profile of v4, /device:TPU:0, one launch (start us, length us, event | category | flops | bytes accessed | tf_op | source)
XLA Modules:
  0.0 388.3 jit_solution(13236914940649077444)
XLA Ops:
  3.8 5.0 %collective-permute-start.4 = (bf16[1824,128]{1,0:T(8,128)(2,1)S(1)}, bf16[1824,128]{1,0:T(8,128)(2,1)S(1)}, u32[]{:S(2)}, u32[]{:S(2)}) collective-permute-start(bf16[1824,128]{1,0:T(8,128)(2,1)S(1)} %shard_map.135), channel_id=1, source_target_pairs={{0,4},{1,5},{2,6},{3,7},{4,8},{5,9},{6,10},{7,11},{8,12},{9,13},{1... | collective-permute-start | bytes 1400840 | tf_op jit(solution)/shard_map/ppermute | solution.py:1022
  13.3 4.1 %collective-permute-done.2.refs_4_ = bf16[912,128]{1,0:T(8,128)(2,1)S(1)} collective-permute-done((bf16[912,128]{1,0:T(8,128)(2,1)S(1)}, bf16[912,128]{1,0:T(8,128)(2,1)S(1)}, u32[]{:S(2)}, u32[]{:S(2)}) %collective-permute-start.2) | collective-permute-done | bytes 233504 | tf_op jit(solution)/shard_map/ppermute | solution.py:1017
  19.0 3.8 collective-permute-done.5
  28.8 5.0 %collective-permute-done.6.refs_7_ = bf16[912,128]{1,0:T(8,128)(2,1)S(1)} collective-permute-done((bf16[912,128]{1,0:T(8,128)(2,1)S(1)}, bf16[912,128]{1,0:T(8,128)(2,1)S(1)}, u32[]{:S(2)}, u32[]{:S(2)}) %collective-permute-start.6) | collective-permute-done | bytes 233504 | tf_op jit(solution)/shard_map/ppermute | solution.py:1017
  36.1 5.5 %collective-permute-done.7.refs_10_ = bf16[912,128]{1,0:T(8,128)(2,1)S(1)} collective-permute-done((bf16[912,128]{1,0:T(8,128)(2,1)S(1)}, bf16[912,128]{1,0:T(8,128)(2,1)S(1)}, u32[]{:S(2)}, u32[]{:S(2)}) %collective-permute-start.7) | collective-permute-done | bytes 233504 | tf_op jit(solution)/shard_map/ppermute | solution.py:1017
  48.1 9.7 %collective-permute-done.12.refs_13_ = bf16[912,128]{1,0:T(8,128)(2,1)S(1)} collective-permute-done((bf16[912,128]{1,0:T(8,128)(2,1)S(1)}, bf16[912,128]{1,0:T(8,128)(2,1)S(1)}, u32[]{:S(2)}, u32[]{:S(2)}) %collective-permute-start.12) | collective-permute-done | bytes 233504 | tf_op jit(solution)/shard_map/ppermute | solution.py:1017
  59.3 2.3 select_convert_fusion.1
  61.6 2.3 collective-permute-done.13.refs_16_
  71.7 8.0 %collective-permute-done.18.refs_19_ = bf16[912,128]{1,0:T(8,128)(2,1)S(1)} collective-permute-done((bf16[912,128]{1,0:T(8,128)(2,1)S(1)}, bf16[912,128]{1,0:T(8,128)(2,1)S(1)}, u32[]{:S(2)}, u32[]{:S(2)}) %collective-permute-start.18) | collective-permute-done | bytes 233504 | tf_op jit(solution)/shard_map/ppermute | solution.py:1017
  80.3 2.7 collective-permute-start.21
  86.8 2.7 collective-permute-done.21.refs_23_
  91.8 10.0 %shard_map.136 = (bf16[512,1536]{1,0:T(8,128)(2,1)S(1)}, bf16[512,512]{1,0:T(8,128)(2,1)}, bf16[512,1024]{1,0:T(8,128)(2,1)}, bf16[512,2048]{1,0:T(8,128)(2,1)},...) custom-call(s32[7]{0:T(128)} %pad_add_fusion.1.place_ref, bf16[912,128]{1,0:T(8,128)(2,1)} %copy-done.63, ...), custom_call_target="tpu_custom_call" | custom-call | flops 8999999488 | tf_op jit(solution)/shard_map/pallas_call | solution.py:731
  102.5 5.3 %shard_map.137 = (bf16[512,1536]{1,0:T(8,128)(2,1)}, bf16[512,512]{1,0:T(8,128)(2,1)S(1)}, f32[8,512]{1,0:T(8,128)S(1)}) custom-call(s32[1]{0:T(128)} %bitcast.3.causal_ref.dec_ref, bf16[1536,512]{1,0:T(8,128)(2,1)} %bitcast.120, bf16[512,1536]{1,0:T(8,128)(2,1)S(1)} %get-tuple-element.580.wqkv, bf16[1536,128]{1,0:T(8,128)(2,1)S(1)} %fusion.7.fq, ...), custom_call_target="tpu_custom_call" | custom-call | flops 5000000000 | tf_op jit(solution)/shard_map/pallas_call | solution.py:731
  107.9 8.3 %shard_map.138 = (bf16[512,1024]{1,0:T(8,128)(2,1)S(1)}, bf16[512,1024]{1,0:T(8,128)(2,1)S(1)}, bf16[512,2048]{1,0:T(8,128)(2,1)S(1)}, bf16[512,2048]{1,0:T(8,12...) custom-call(bf16[1536,512]{1,0:T(8,128)(2,1)S(1)} %bitcast.128, ...), custom_call_target="tpu_custom_call" | custom-call | flops 8000000000 | tf_op jit(solution)/shard_map/pallas_call | solution.py:731
  118.5 6.4 %shard_map.139 = (bf16[512,1536]{1,0:T(8,128)(2,1)S(1)}, bf16[512,512]{1,0:T(8,128)(2,1)}, f32[8,512]{1,0:T(8,128)S(1)}) custom-call(s32[1]{0:T(128)} %bitcast.3.causal_ref.dec_ref, bf16[1536,512]{1,0:T(8,128)(2,1)} %bitcast.121, bf16[512,1536]{1,0:T(8,128)(2,1)} %copy-done.21, bf16[1536,128]{1,0:T(8,128)(2,1)S(1)} %fusion.7.fq, bf16[1536,128]{1,0:T(8,128)(2,1)S(1)} %fusion.21.fk), custom_call_target="tpu_custom_call" | custom-call | flops 5000000000 | tf_op jit(solution)/shard_map/pallas_call | solution.py:731
  125.0 20.1 %conditional.4 = (bf16[512,1024]{1,0:T(8,128)(2,1)}, bf16[512,2048]{1,0:T(8,128)(2,1)}, bf16[512,1024]{1,0:T(8,128)(2,1)}, f32[512,512]{1,0:T(8,128)}, f32[512,5...) conditional(s32[]{:T(128)} %convert_element_type.421, ...), branch_computations={%region_0.1_spmd, %region_1.2_spmd} | conditional | flops 24000000000 | bytes 96 | solution.py:1009
  132.6 12.4 %branch_1_fun.10 = (bf16[512,1024]{1,0:T(8,128)(2,1)}, bf16[512,1024]{1,0:T(8,128)(2,1)}, bf16[512,2048]{1,0:T(8,128)(2,1)}, bf16[512,2048]{1,0:T(8,128)(2,1)}, f32[512,512]{1,0:T(8,128)}, /*index=5*/f32[512,512]{1,0:T(8,128)}) custom-call(bf16[1536,512]{1,0:T(8,128)(2,1)} %get-tuple-element.192.x_ref, bf16[512,512]{1,0:T(8,128)(2,1)} %get-tuple-element.193.ctx_ref, ...), custom_call_target="tpu_custom_call" | custom-call | flops 8000000000 | tf_op jit(solution)/shard_map/cond/branch_1_fun/pallas_call | solution.py:731
  145.1 6.5 %collective-permute-start.23 = (bf16[512,1024]{1,0:T(8,128)(2,1)}, bf16[512,1024]{1,0:T(8,128)(2,1)}, u32[]{:S(2)}, u32[]{:S(2)}) collective-permute-start(bf16[512,1024]{1,0:T(8,128)(2,1)} %get-tuple-element.596), channel_id=1, source_target_pairs={{0,16},{16,0},{1,17},{17,1},{2,18},{18,2},{3,19},{19,3},{4,20},{20... | collective-permute-start | bytes 3145736 | tf_op jit(solution)/shard_map/ppermute | solution.py:1158
  151.5 6.0 %shard_map.140 = (bf16[512,1536]{1,0:T(8,128)(2,1)S(1)}, bf16[512,512]{1,0:T(8,128)(2,1)}, f32[8,512]{1,0:T(8,128)S(1)}) custom-call(s32[1]{0:T(128)} %bitcast.3.causal_ref.dec_ref, bf16[1536,512]{1,0:T(8,128)(2,1)} %bitcast.124, bf16[512,1536]{1,0:T(8,128)(2,1)S(1)} %copy-done.22, bf16[1536,128]{1,0:T(8,128)(2,1)} %copy-done.26, bf16[1536,128]{1,0:T(8,128)(2,1)} %copy-done.29), custom_call_target="tpu_custom_call" | custom-call | flops 5000000000 | tf_op jit(solution)/shard_map/pallas_call | solution.py:731
  158.7 30.0 %conditional.5 = (bf16[512,1024]{1,0:T(8,128)(2,1)}, bf16[512,2048]{1,0:T(8,128)(2,1)}, bf16[512,1024]{1,0:T(8,128)(2,1)}, f32[512,512]{1,0:T(8,128)}, f32[512,5...) conditional(s32[]{:T(128)} %convert_element_type.421, ...), branch_computations={%region_2.3_spmd, %region_3.4_spmd} | conditional | flops 24000000000 | bytes 39846196 | solution.py:1009
  166.5 13.4 %branch_1_fun.12 = (bf16[512,1024]{1,0:T(8,128)(2,1)}, bf16[512,1024]{1,0:T(8,128)(2,1)}, bf16[512,2048]{1,0:T(8,128)(2,1)}, bf16[512,2048]{1,0:T(8,128)(2,1)}, f32[512,512]{1,0:T(8,128)}, /*index=5*/f32[512,512]{1,0:T(8,128)}) custom-call(bf16[1536,512]{1,0:T(8,128)(2,1)} %get-tuple-element.236.x_ref, bf16[512,512]{1,0:T(8,128)(2,1)} %get-tuple-element.237.ctx_ref, ...), custom_call_target="tpu_custom_call" | custom-call | flops 8000000000 | tf_op jit(solution)/shard_map/cond/branch_1_fun/pallas_call | solution.py:731
  179.9 8.7 %branch_1_fun.13 = (f32[512,512]{1,0:T(8,128)}, bf16[512,512]{1,0:T(8,128)(2,1)}, bf16[512,2048]{1,0:T(8,128)(2,1)}, bf16[512,512]{1,0:T(8,128)(2,1)}, bf16[512,512]{1,0:T(8,128)(2,1)}, /*index=5*/f32[8,512]{1,0:T(8,128)S(1)}) custom-call(bf16[512,1024]{1,0:T(8,128)(2,1)} %get-tuple-element.249.gkv_ref, f32[512,512]{1,0:T(8,128)S(1)} %copy-done.76, ...), custom_call_target="tpu_custom_call" | custom-call | flops 8000000000 | tf_op jit(solution)/shard_map/cond/branch_1_fun/pallas_call | solution.py:731
  188.8 3.0 collective-permute-done.24.refs_10_
  191.7 28.0 %conditional.6 = (bf16[512,512]{1,0:T(8,128)(2,1)}, bf16[512,512]{1,0:T(8,128)(2,1)}, f32[512,512]{1,0:T(8,128)}, bf16[512,2048]{1,0:T(8,128)(2,1)}, f32[8,512]{...) conditional(s32[]{:T(128)} %convert_element_type.421, ...), branch_computations={%region_4.5_spmd, %region_5.6_spmd} | conditional | flops 24000000000 | bytes 96 | solution.py:1009
  199.7 9.7 %branch_1_fun.15 = (f32[512,512]{1,0:T(8,128)}, bf16[512,512]{1,0:T(8,128)(2,1)}, bf16[512,2048]{1,0:T(8,128)(2,1)}, bf16[512,512]{1,0:T(8,128)(2,1)}, bf16[512,512]{1,0:T(8,128)(2,1)}, /*index=5*/f32[8,512]{1,0:T(8,128)S(1)}) custom-call(bf16[512,1024]{1,0:T(8,128)(2,1)} %get-tuple-element.283.gkv_ref, f32[512,512]{1,0:T(8,128)} %get-tuple-element.284.r1_any, ...), custom_call_target="tpu_custom_call" | custom-call | flops 8000000000 | tf_op jit(solution)/shard_map/cond/branch_1_fun/pallas_call | solution.py:731
  209.5 10.3 %branch_1_fun.16 = (bf16[512,512]{1,0:T(8,128)(2,1)}, bf16[512,1536]{1,0:T(8,128)(2,1)}) custom-call(s32[1]{0:T(128)} %get-tuple-element.298.causal_ref, bf16[512,1536]{1,0:T(8,128)(2,1)S(1)} %get-tuple-element.299.wqkv, bf16[1536,128]{1,0:T(8,128)(2,1)} %get-tuple-element.300.fq, bf16[1536,128]{1,0:T(8,128)(2,1)} %get-tuple-element.301.fk, ...), custom_call_target="tpu_custom_call" | custom-call | flops 1000000000 | tf_op jit(solution)/shard_map/cond/branch_1_fun/pallas_call | solution.py:731
  219.8 2.5 collective-permute-start.25
  222.3 2.6 collective-permute-done.25.refs_11_
  224.9 10.0 %conditional.7 = (bf16[512,512]{1,0:T(8,128)(2,1)}, bf16[512,512]{1,0:T(8,128)(2,1)}, f32[512,512]{1,0:T(8,128)}, bf16[512,2048]{1,0:T(8,128)(2,1)}, f32[8,512]{...) conditional(s32[]{:T(128)} %convert_element_type.420, (bf16[512,1024]{1,0:T(8,128)(2,1)}, ...), branch_computations={%region_6.7_spmd, %region_7.8_spmd} | conditional | flops 8999999488 | bytes 56 | solution.py:1011
  225.1 9.8 %branch_0_fun.14 = (f32[512,512]{1,0:T(8,128)}, bf16[512,512]{1,0:T(8,128)(2,1)}, bf16[512,2048]{1,0:T(8,128)(2,1)}, bf16[512,512]{1,0:T(8,128)(2,1)}, bf16[512,512]{1,0:T(8,128)(2,1)}, /*index=5*/f32[8,512]{1,0:T(8,128)S(1)}) custom-call(bf16[512,1024]{1,0:T(8,128)(2,1)} %get-tuple-element.312.gkv_ref, f32[512,512]{1,0:T(8,128)} %get-tuple-element.313.r1_any, ...), custom_call_target="tpu_custom_call" | custom-call | flops 8000000000 | tf_op jit(solution)/shard_map/cond/branch_0_fun/pallas_call | solution.py:731
  236.6 14.6 %shard_map.141.refs_0_.refs_1_ = bf16[16384,128]{1,0:T(8,128)(2,1)} custom-call(s32[1]{0:T(128)} %bitcast.3.causal_ref.dec_ref, bf16[512,512]{1,0:T(8,128)(2,1)} %get-tuple-element.605.refs_0_.refs_13_, bf16[512,512]{1,0:T(8,128)(2,1)} %get-tuple-element.614.refs_1_.refs_14_, bf16[512,512]{1,0:T(8,128)(2,1)} %get-tuple-element.620.refs_2_, ...), custom_call_target="tpu_custom_call" | custom-call | flops 1000000000 | tf_op jit(solution)/shard_map/pallas_call | solution.py:731
  258.7 5.6 %shard_map.143.refs_0_.refs_1_ = bf16[6144,128]{1,0:T(8,128)(2,1)S(1)} custom-call(s32[1]{0:T(128)} %bitcast.3.causal_ref.dec_ref, bf16[512,512]{1,0:T(8,128)(2,1)S(1)} %copy-done.39, bf16[512,512]{1,0:T(8,128)(2,1)} %get-tuple-element.593.refs_1_.refs_13_, bf16[512,512]{1,0:T(8,128)(2,1)} %get-tuple-element.601.refs_2_.refs_14_, f32[512,512]{1,0:T(8,128)S(1)} %copy-done.36, ...), custom_call_target="tpu_custom_call" | custom-call | flops 1000000000 | tf_op jit(solution)/shard_map/pallas_call | solution.py:731
  269.5 10.1 %shard_map.145 = (bf16[512,512]{1,0:T(8,128)(2,1)S(1)}, bf16[512,1536]{1,0:T(8,128)(2,1)S(1)}) custom-call(s32[1]{0:T(128)} %bitcast.3.causal_ref.dec_ref, bf16[512,1536]{1,0:T(8,128)(2,1)} %copy-done.21, bf16[1536,128]{1,0:T(8,128)(2,1)} %copy-done.26, bf16[1536,128]{1,0:T(8,128)(2,1)} %copy-done.29, ...), custom_call_target="tpu_custom_call" | custom-call | flops 1000000000 | tf_op jit(solution)/shard_map/pallas_call | solution.py:731
  279.7 8.1 %shard_map.146 = (bf16[512,512]{1,0:T(8,128)(2,1)S(1)}, bf16[512,1536]{1,0:T(8,128)(2,1)S(1)}) custom-call(s32[1]{0:T(128)} %bitcast.3.causal_ref.dec_ref, bf16[512,1536]{1,0:T(8,128)(2,1)S(1)} %copy-done.23, bf16[1536,128]{1,0:T(8,128)(2,1)S(1)} %copy-done.28, bf16[1536,128]{1,0:T(8,128)(2,1)S(1)} %copy-done.30, bf16[512,1536]{1,0:T(8,128)(2,1)S(1)} %copy-done.3, ...), custom_call_target="tpu_custom_call" | custom-call | flops 1000000000 | tf_op jit(solution)/shard_map/pallas_call | solution.py:731
  287.9 4.2 %shard_map.147.refs_0_ = bf16[6144,128]{1,0:T(8,128)(2,1)S(1)} custom-call(s32[1]{0:T(128)} %bitcast.3.causal_ref.dec_ref, bf16[1536,512]{1,0:T(8,128)(2,1)S(1)} %bitcast.129, bf16[512,1536]{1,0:T(8,128)(2,1)S(1)} %copy-done.44, bf16[512,1536]{1,0:T(8,128)(2,1)S(1)} %get-tuple-element.657.refs_1_.refs_4_, ...), custom_call_target="tpu_custom_call" | custom-call | flops 1000000000 | tf_op jit(solution)/shard_map/pallas_call | solution.py:731
  302.4 7.6 %collective-permute-done.36 = bf16[1,912,128]{2,1,0:T(8,128)(2,1)S(1)} collective-permute-done((bf16[1,912,128]{2,1,0:T(8,128)(2,1)S(1)}, bf16[1,912,128]{2,1,0:T(8,128)(2,1)S(1)}, u32[]{:S(2)}, u32[]{:S(2)}) %collective-permute-start.36) | collective-permute-done | bytes 233504 | tf_op jit(solution)/shard_map/ppermute | solution.py:1017
  315.8 4.2 %collective-permute-done.38 = bf16[2,912,128]{2,1,0:T(8,128)(2,1)S(1)} collective-permute-done((bf16[2,912,128]{2,1,0:T(8,128)(2,1)S(1)}, bf16[2,912,128]{2,1,0:T(8,128)(2,1)S(1)}, u32[]{:S(2)}, u32[]{:S(2)}) %collective-permute-start.38) | collective-permute-done | bytes 466976 | tf_op jit(solution)/shard_map/ppermute | solution.py:1017
  322.5 2.8 collective-permute-start.40
  327.3 4.5 %collective-permute-done.40 = bf16[2,912,128]{2,1,0:T(8,128)(2,1)S(1)} collective-permute-done((bf16[2,912,128]{2,1,0:T(8,128)(2,1)S(1)}, bf16[2,912,128]{2,1,0:T(8,128)(2,1)S(1)}, u32[]{:S(2)}, u32[]{:S(2)}) %collective-permute-start.40) | collective-permute-done | bytes 466976 | tf_op jit(solution)/shard_map/ppermute | solution.py:1022
  332.0 4.4 %collective-permute-start.41 = (bf16[2,912,128]{2,1,0:T(8,128)(2,1)S(1)}, bf16[2,912,128]{2,1,0:T(8,128)(2,1)S(1)}, u32[]{:S(2)}, u32[]{:S(2)}) collective-permute-start(bf16[2,912,128]{2,1,0:T(8,128)(2,1)S(1)} %get-tuple-element.693), channel_id=1, source_target_pairs={{0,4},{1,5},{2,6},{3,7},{4,8},{5,9},{6,10},{7,11},{16,20},{17,21},... | collective-permute-start | bytes 1400840 | tf_op jit(solution)/shard_map/ppermute | solution.py:1022
  338.4 5.6 %collective-permute-done.41 = bf16[2,912,128]{2,1,0:T(8,128)(2,1)S(1)} collective-permute-done((bf16[2,912,128]{2,1,0:T(8,128)(2,1)S(1)}, bf16[2,912,128]{2,1,0:T(8,128)(2,1)S(1)}, u32[]{:S(2)}, u32[]{:S(2)}) %collective-permute-start.41) | collective-permute-done | bytes 466976 | tf_op jit(solution)/shard_map/ppermute | solution.py:1022
  344.4 4.4 %collective-permute-start.42 = (bf16[2,912,128]{2,1,0:T(8,128)(2,1)S(1)}, bf16[2,912,128]{2,1,0:T(8,128)(2,1)S(1)}, u32[]{:S(2)}, u32[]{:S(2)}) collective-permute-start(bf16[2,912,128]{2,1,0:T(8,128)(2,1)S(1)} %get-tuple-element.695), channel_id=1, source_target_pairs={{0,4},{1,5},{2,6},{3,7},{4,8},{5,9},{6,10},{7,11},{8,12},{9,13},{1... | collective-permute-start | bytes 1400840 | tf_op jit(solution)/shard_map/ppermute | solution.py:1022
  350.2 7.2 %collective-permute-done.42 = bf16[2,912,128]{2,1,0:T(8,128)(2,1)S(1)} collective-permute-done((bf16[2,912,128]{2,1,0:T(8,128)(2,1)S(1)}, bf16[2,912,128]{2,1,0:T(8,128)(2,1)S(1)}, u32[]{:S(2)}, u32[]{:S(2)}) %collective-permute-start.42) | collective-permute-done | bytes 466976 | tf_op jit(solution)/shard_map/ppermute | solution.py:1022
  358.0 3.4 shard_map.149
  363.7 2.9 collective-permute-start.47
  372.8 4.2 %collective-permute-start.52 = (f32[8,128]{1,0:T(8,128)S(1)}, f32[8,128]{1,0:T(8,128)S(1)}, u32[]{:S(2)}, u32[]{:S(2)}) collective-permute-start(f32[8,128]{1,0:T(8,128)S(1)} %add_add_fusion), channel_id=1, source_target_pairs={{0,4},{1,5},{2,6},{3,7},{4,0},{5,1},{6,2},{7,3},{8,12},{9,13},{10,... | collective-permute-start | bytes 12296 | tf_op jit(solution)/shard_map/ppermute | solution.py:1017
  377.0 2.4 collective-permute-start.54
  383.8 3.1 shard_map.150
  (313 shorter events, 95.4 us)
Async XLA Ops:
  3.8 15.3 %collective-permute-start.4 = (bf16[1824,128]{1,0:T(8,128)(2,1)S(1)}, bf16[1824,128]{1,0:T(8,128)(2,1)S(1)}, u32[]{:S(2)}, u32[]{:S(2)}) collective-permute-start(bf16[1824,128]{1,0:T(8,128)(2,1)S(1)} %shard_map.135), channel_id=1, source_target_pairs={{0,4},{1,5},{2,6},{3,7},{4,8},{5,9},{6,10},{7,11},{8,12},{9,13},{1... | collective-permute-start | bytes 1400840 | tf_op jit(solution)/shard_map/ppermute | solution.py:1022
  8.7 14.0 %collective-permute-start.5 = (bf16[1824,128]{1,0:T(8,128)(2,1)S(1)}, bf16[1824,128]{1,0:T(8,128)(2,1)S(1)}, u32[]{:S(2)}, u32[]{:S(2)}) collective-permute-start(bf16[1824,128]{1,0:T(8,128)(2,1)S(1)} %shard_map.135), channel_id=1, source_target_pairs={{4,0},{5,1},{6,2},{7,3},{8,4},{9,5},{10,6},{11,7},{12,8},{13,9},{1... | collective-permute-start | bytes 1400840 | tf_op jit(solution)/shard_map/ppermute | solution.py:1022
  10.2 7.2 %collective-permute-start.2 = (bf16[912,128]{1,0:T(8,128)(2,1)S(1)}, bf16[912,128]{1,0:T(8,128)(2,1)S(1)}, u32[]{:S(2)}, u32[]{:S(2)}) collective-permute-start(bf16[912,128]{1,0:T(8,128)(2,1)S(1)} %get-tuple-element.559.refs_3_), channel_id=1, source_target_pairs={{0,2},{1,3},{2,0},{3,1},{4,6},{5,7},{6,4},{7,5},{8,10},{9,11},{10,... | collective-permute-start | bytes 700424 | tf_op jit(solution)/shard_map/ppermute | solution.py:1017
  11.8 7.2 %collective-permute-start = (bf16[912,128]{1,0:T(8,128)(2,1)S(1)}, bf16[912,128]{1,0:T(8,128)(2,1)S(1)}, u32[]{:S(2)}, u32[]{:S(2)}) collective-permute-start(bf16[912,128]{1,0:T(8,128)(2,1)S(1)} %get-tuple-element.556.refs_0_), channel_id=1, source_target_pairs={{0,1},{1,0},{2,3},{3,2},{4,5},{5,4},{6,7},{7,6},{8,9},{9,8},{10,11... | collective-permute-start | bytes 700424 | tf_op jit(solution)/shard_map/ppermute | solution.py:1017
  17.5 24.1 %collective-permute-start.3 = (bf16[2,912,128]{2,1,0:T(8,128)(2,1)S(1)}, bf16[2,912,128]{2,1,0:T(8,128)(2,1)}, u32[]{:S(2)}, u32[]{:S(2)}) collective-permute-start(bf16[2,912,128]{2,1,0:T(8,128)(2,1)S(1)} %pad_maximum_fusion.2), channel_id=1, source_target_pairs={{0,1},{1,0},{2,3},{3,2},{4,5},{5,4},{6,7},{7,6},{8,9},{9,8},{10,11... | collective-permute-start | bytes 1400840 | tf_op jit(solution)/shard_map/ppermute | solution.py:1017
  22.9 10.9 %collective-permute-start.6 = (bf16[912,128]{1,0:T(8,128)(2,1)S(1)}, bf16[912,128]{1,0:T(8,128)(2,1)S(1)}, u32[]{:S(2)}, u32[]{:S(2)}) collective-permute-start(bf16[912,128]{1,0:T(8,128)(2,1)S(1)} %get-tuple-element.562.refs_6_), channel_id=1, source_target_pairs={{0,1},{1,0},{2,3},{3,2},{4,5},{5,4},{6,7},{7,6},{8,9},{9,8},{10,11... | collective-permute-start | bytes 700424 | tf_op jit(solution)/shard_map/ppermute | solution.py:1017
  25.3 16.3 %collective-permute-start.1 = (bf16[2,912,128]{2,1,0:T(8,128)(2,1)}, bf16[2,912,128]{2,1,0:T(8,128)(2,1)}, u32[]{:S(2)}, u32[]{:S(2)}) collective-permute-start(bf16[2,912,128]{2,1,0:T(8,128)(2,1)} %pad_maximum_fusion.1), channel_id=1, source_target_pairs={{0,2},{1,3},{2,0},{3,1},{4,6},{5,7},{6,4},{7,5},{8,10},{9,11},{10,... | collective-permute-start | bytes 1400840 | tf_op jit(solution)/shard_map/ppermute | solution.py:1017
  26.8 15.5 %collective-permute-start.10 = (bf16[1824,128]{1,0:T(8,128)(2,1)S(1)}, bf16[1824,128]{1,0:T(8,128)(2,1)S(1)}, u32[]{:S(2)}, u32[]{:S(2)}) collective-permute-start(bf16[1824,128]{1,0:T(8,128)(2,1)S(1)} %collective-permute-done.4), channel_id=1, source_target_pairs={{4,8},{5,9},{6,10},{7,11},{8,12},{9,13},{10,14},{11,15},{20,24},{2... | collective-permute-start | bytes 1400840 | tf_op jit(solution)/shard_map/ppermute | solution.py:1022
  27.5 14.9 %collective-permute-start.11 = (bf16[1824,128]{1,0:T(8,128)(2,1)S(1)}, bf16[1824,128]{1,0:T(8,128)(2,1)S(1)}, u32[]{:S(2)}, u32[]{:S(2)}) collective-permute-start(bf16[1824,128]{1,0:T(8,128)(2,1)S(1)} %collective-permute-done.5), channel_id=1, source_target_pairs={{4,0},{5,1},{6,2},{7,3},{8,4},{9,5},{10,6},{11,7},{20,16},{21,17},... | collective-permute-start | bytes 1400840 | tf_op jit(solution)/shard_map/ppermute | solution.py:1022
  34.5 7.1 %collective-permute-start.7 = (bf16[912,128]{1,0:T(8,128)(2,1)S(1)}, bf16[912,128]{1,0:T(8,128)(2,1)S(1)}, u32[]{:S(2)}, u32[]{:S(2)}) collective-permute-start(bf16[912,128]{1,0:T(8,128)(2,1)S(1)} %get-tuple-element.565.refs_9_), channel_id=1, source_target_pairs={{0,2},{1,3},{2,0},{3,1},{4,6},{5,7},{6,4},{7,5},{8,10},{9,11},{10,... | collective-permute-start | bytes 700424 | tf_op jit(solution)/shard_map/ppermute | solution.py:1017
  41.7 22.2 %collective-permute-start.9 = (bf16[2,912,128]{2,1,0:T(8,128)(2,1)S(1)}, bf16[2,912,128]{2,1,0:T(8,128)(2,1)S(1)}, u32[]{:S(2)}, u32[]{:S(2)}) collective-permute-start(bf16[2,912,128]{2,1,0:T(8,128)(2,1)S(1)} %pad_maximum_fusion.4), channel_id=1, source_target_pairs={{0,1},{1,0},{2,3},{3,2},{4,5},{5,4},{6,7},{7,6},{8,9},{9,8},{10,11... | collective-permute-start | bytes 1400840 | tf_op jit(solution)/shard_map/ppermute | solution.py:1017
  42.6 15.3 %collective-permute-start.12 = (bf16[912,128]{1,0:T(8,128)(2,1)S(1)}, bf16[912,128]{1,0:T(8,128)(2,1)S(1)}, u32[]{:S(2)}, u32[]{:S(2)}) collective-permute-start(bf16[912,128]{1,0:T(8,128)(2,1)S(1)} %get-tuple-element.568.refs_12_), channel_id=1, source_target_pairs={{0,1},{1,0},{2,3},{3,2},{4,5},{5,4},{6,7},{7,6},{8,9},{9,8},{10,11... | collective-permute-start | bytes 700424 | tf_op jit(solution)/shard_map/ppermute | solution.py:1017
  44.0 19.9 %collective-permute-start.8 = (bf16[2,912,128]{2,1,0:T(8,128)(2,1)S(1)}, bf16[2,912,128]{2,1,0:T(8,128)(2,1)S(1)}, u32[]{:S(2)}, u32[]{:S(2)}) collective-permute-start(bf16[2,912,128]{2,1,0:T(8,128)(2,1)S(1)} %pad_maximum_fusion.3), channel_id=1, source_target_pairs={{0,2},{1,3},{2,0},{3,1},{4,6},{5,7},{6,4},{7,5},{8,10},{9,11},{10,... | collective-permute-start | bytes 1400840 | tf_op jit(solution)/shard_map/ppermute | solution.py:1017
  45.6 21.8 %collective-permute-start.16 = (bf16[1824,128]{1,0:T(8,128)(2,1)S(1)}, bf16[1824,128]{1,0:T(8,128)(2,1)S(1)}, u32[]{:S(2)}, u32[]{:S(2)}) collective-permute-start(bf16[1824,128]{1,0:T(8,128)(2,1)S(1)} %collective-permute-done.10), channel_id=1, source_target_pairs={{8,12},{9,13},{10,14},{11,15},{24,28},{25,29},{26,30},{27,31}} | collective-permute-start | bytes 1400840 | tf_op jit(solution)/shard_map/ppermute | solution.py:1022
  46.3 21.2 %collective-permute-start.17 = (bf16[1824,128]{1,0:T(8,128)(2,1)S(1)}, bf16[1824,128]{1,0:T(8,128)(2,1)S(1)}, u32[]{:S(2)}, u32[]{:S(2)}) collective-permute-start(bf16[1824,128]{1,0:T(8,128)(2,1)S(1)} %collective-permute-done.11), channel_id=1, source_target_pairs={{4,0},{5,1},{6,2},{7,3},{20,16},{21,17},{22,18},{23,19}} | collective-permute-start | bytes 1400840 | tf_op jit(solution)/shard_map/ppermute | solution.py:1022
  57.8 6.1 %collective-permute-start.13 = (bf16[912,128]{1,0:T(8,128)(2,1)S(1)}, bf16[912,128]{1,0:T(8,128)(2,1)S(1)}, u32[]{:S(2)}, u32[]{:S(2)}) collective-permute-start(bf16[912,128]{1,0:T(8,128)(2,1)S(1)} %get-tuple-element.571.refs_15_), channel_id=1, source_target_pairs={{0,2},{1,3},{2,0},{3,1},{4,6},{5,7},{6,4},{7,5},{8,10},{9,11},{10,... | collective-permute-start | bytes 700424 | tf_op jit(solution)/shard_map/ppermute | solution.py:1017
  64.8 15.5 %collective-permute-start.15 = (bf16[2,912,128]{2,1,0:T(8,128)(2,1)S(1)}, bf16[2,912,128]{2,1,0:T(8,128)(2,1)}, u32[]{:S(2)}, u32[]{:S(2)}) collective-permute-start(bf16[2,912,128]{2,1,0:T(8,128)(2,1)S(1)} %pad_maximum_fusion.6), channel_id=1, source_target_pairs={{0,1},{1,0},{2,3},{3,2},{4,5},{5,4},{6,7},{7,6},{8,9},{9,8},{10,11... | collective-permute-start | bytes 1400840 | tf_op jit(solution)/shard_map/ppermute | solution.py:1017
  65.9 14.3 %collective-permute-start.14 = (bf16[2,912,128]{2,1,0:T(8,128)(2,1)}, bf16[2,912,128]{2,1,0:T(8,128)(2,1)}, u32[]{:S(2)}, u32[]{:S(2)}) collective-permute-start(bf16[2,912,128]{2,1,0:T(8,128)(2,1)} %pad_maximum_fusion.5), channel_id=1, source_target_pairs={{0,2},{1,3},{2,0},{3,1},{4,6},{5,7},{6,4},{7,5},{8,10},{9,11},{10,... | collective-permute-start | bytes 1400840 | tf_op jit(solution)/shard_map/ppermute | solution.py:1017
  67.7 12.0 %collective-permute-start.18 = (bf16[912,128]{1,0:T(8,128)(2,1)S(1)}, bf16[912,128]{1,0:T(8,128)(2,1)S(1)}, u32[]{:S(2)}, u32[]{:S(2)}) collective-permute-start(bf16[912,128]{1,0:T(8,128)(2,1)S(1)} %get-tuple-element.574.refs_18_), channel_id=1, source_target_pairs={{0,1},{1,0},{2,3},{3,2},{4,5},{5,4},{6,7},{7,6},{8,9},{9,8},{10,11... | collective-permute-start | bytes 700424 | tf_op jit(solution)/shard_map/ppermute | solution.py:1017
  69.5 10.7 %collective-permute-start.19 = (bf16[912,128]{1,0:T(8,128)(2,1)S(1)}, bf16[912,128]{1,0:T(8,128)(2,1)S(1)}, u32[]{:S(2)}, u32[]{:S(2)}) collective-permute-start(bf16[912,128]{1,0:T(8,128)(2,1)S(1)} %get-tuple-element.577.refs_21_), channel_id=1, source_target_pairs={{0,2},{1,3},{2,0},{3,1},{4,6},{5,7},{6,4},{7,5},{8,10},{9,11},{10,... | collective-permute-start | bytes 700424 | tf_op jit(solution)/shard_map/ppermute | solution.py:1017
  80.3 9.2 %collective-permute-start.21 = (bf16[2,912,128]{2,1,0:T(8,128)(2,1)S(1)}, bf16[2,912,128]{2,1,0:T(8,128)(2,1)S(1)}, u32[]{:S(2)}, u32[]{:S(2)}) collective-permute-start(bf16[2,912,128]{2,1,0:T(8,128)(2,1)S(1)} %pad_maximum_fusion.8), channel_id=1, source_target_pairs={{0,1},{1,0},{2,3},{3,2},{4,5},{5,4},{6,7},{7,6},{8,9},{9,8},{10,11... | collective-permute-start | bytes 1400840 | tf_op jit(solution)/shard_map/ppermute | solution.py:1017
  83.0 8.7 %collective-permute-start.20 = (bf16[2,912,128]{2,1,0:T(8,128)(2,1)S(1)}, bf16[2,912,128]{2,1,0:T(8,128)(2,1)}, u32[]{:S(2)}, u32[]{:S(2)}) collective-permute-start(bf16[2,912,128]{2,1,0:T(8,128)(2,1)S(1)} %pad_maximum_fusion.7), channel_id=1, source_target_pairs={{0,2},{1,3},{2,0},{3,1},{4,6},{5,7},{6,4},{7,5},{8,10},{9,11},{10,... | collective-permute-start | bytes 1400840 | tf_op jit(solution)/shard_map/ppermute | solution.py:1017
  118.5 6.5 %collective-permute-start.22 = (bf16[512,1024]{1,0:T(8,128)(2,1)S(1)}, bf16[512,1024]{1,0:T(8,128)(2,1)}, u32[]{:S(2)}, u32[]{:S(2)}) collective-permute-start(bf16[512,1024]{1,0:T(8,128)(2,1)S(1)} %get-tuple-element.589), channel_id=1, source_target_pairs={{0,16},{16,0},{1,17},{17,1},{2,18},{18,2},{3,19},{19,3},{4,20},{20... | collective-permute-start | bytes 3145736 | tf_op jit(solution)/shard_map/ppermute | solution.py:1158
  145.1 13.6 %collective-permute-start.23 = (bf16[512,1024]{1,0:T(8,128)(2,1)}, bf16[512,1024]{1,0:T(8,128)(2,1)}, u32[]{:S(2)}, u32[]{:S(2)}) collective-permute-start(bf16[512,1024]{1,0:T(8,128)(2,1)} %get-tuple-element.596), channel_id=1, source_target_pairs={{0,16},{16,0},{1,17},{17,1},{2,18},{18,2},{3,19},{19,3},{4,20},{20... | collective-permute-start | bytes 3145736 | tf_op jit(solution)/shard_map/ppermute | solution.py:1158
  255.6 32.3 %collective-permute-start.28 = (bf16[2,2,912,128]{3,2,0,1:T(8,128)(2,1)}, bf16[2,2,912,128]{3,2,0,1:T(8,128)(2,1)}, u32[]{:S(2)}, u32[]{:S(2)}) collective-permute-start(bf16[2,2,912,128]{3,2,0,1:T(8,128)(2,1)} %copy.15), channel_id=1, source_target_pairs={{0,2},{1,3},{2,0},{3,1},{4,6},{5,7},{6,4},{7,5},{8,10},{9,11},{10,... | collective-permute-start | bytes 2801672 | tf_op jit(solution)/shard_map/ppermute | solution.py:1017
  258.1 29.8 %collective-permute-start.29 = (bf16[2,2,912,128]{3,2,0,1:T(8,128)(2,1)}, bf16[2,2,912,128]{3,2,0,1:T(8,128)(2,1)}, u32[]{:S(2)}, u32[]{:S(2)}) collective-permute-start(bf16[2,2,912,128]{3,2,0,1:T(8,128)(2,1)} %copy.16), channel_id=1, source_target_pairs={{0,1},{1,0},{2,3},{3,2},{4,5},{5,4},{6,7},{7,6},{8,9},{9,8},{10,11... | collective-permute-start | bytes 2801672 | tf_op jit(solution)/shard_map/ppermute | solution.py:1017
  267.6 24.6 %collective-permute-start.26 = (bf16[1,2,912,128]{3,2,1,0:T(8,128)(2,1)}, bf16[1,2,912,128]{3,2,1,0:T(8,128)(2,1)}, u32[]{:S(2)}, u32[]{:S(2)}) collective-permute-start(bf16[1,2,912,128]{3,2,1,0:T(8,128)(2,1)} %get-tuple-element.649), channel_id=1, source_target_pairs={{0,2},{1,3},{2,0},{3,1},{4,6},{5,7},{6,4},{7,5},{8,10},{9,11},{10,... | collective-permute-start | bytes 1400840 | tf_op jit(solution)/shard_map/ppermute | solution.py:1017
  268.3 23.9 %collective-permute-start.27 = (bf16[1,2,912,128]{3,2,1,0:T(8,128)(2,1)}, bf16[1,2,912,128]{3,2,1,0:T(8,128)(2,1)}, u32[]{:S(2)}, u32[]{:S(2)}) collective-permute-start(bf16[1,2,912,128]{3,2,1,0:T(8,128)(2,1)} %get-tuple-element.651), channel_id=1, source_target_pairs={{0,1},{1,0},{2,3},{3,2},{4,5},{5,4},{6,7},{7,6},{8,9},{9,8},{10,11... | collective-permute-start | bytes 1400840 | tf_op jit(solution)/shard_map/ppermute | solution.py:1017
  293.0 20.4 %collective-permute-start.30 = (bf16[1,2,912,128]{3,2,1,0:T(8,128)(2,1)S(1)}, bf16[1,2,912,128]{3,2,1,0:T(8,128)(2,1)S(1)}, u32[]{:S(2)}, u32[]{:S(2)}) collective-permute-start(bf16[1,2,912,128]{3,2,1,0:T(8,128)(2,1)S(1)} %get-tuple-element.670), channel_id=1, source_target_pairs={{0,2},{1,3},{2,0},{3,1},{4,6},{5,7},{6,4},{7,5},{8,10},{9,11},{10,... | collective-permute-start | bytes 1400840 | tf_op jit(solution)/shard_map/ppermute | solution.py:1017
  294.6 19.2 %collective-permute-start.32 = (bf16[1,2,912,128]{3,2,1,0:T(8,128)(2,1)S(1)}, bf16[1,2,912,128]{3,2,1,0:T(8,128)(2,1)S(1)}, u32[]{:S(2)}, u32[]{:S(2)}) collective-permute-start(bf16[1,2,912,128]{3,2,1,0:T(8,128)(2,1)S(1)} %get-tuple-element.672), channel_id=1, source_target_pairs={{0,1},{1,0},{2,3},{3,2},{4,5},{5,4},{6,7},{7,6},{8,9},{9,8},{10,11... | collective-permute-start | bytes 1400840 | tf_op jit(solution)/shard_map/ppermute | solution.py:1017
  296.2 13.8 %collective-permute-start.36 = (bf16[1,912,128]{2,1,0:T(8,128)(2,1)S(1)}, bf16[1,912,128]{2,1,0:T(8,128)(2,1)S(1)}, u32[]{:S(2)}, u32[]{:S(2)}) collective-permute-start(bf16[1,912,128]{2,1,0:T(8,128)(2,1)S(1)} %fusion.24), channel_id=1, source_target_pairs={{0,1},{1,0},{2,3},{3,2},{4,5},{5,4},{6,7},{7,6},{8,9},{9,8},{10,11... | collective-permute-start | bytes 700424 | tf_op jit(solution)/shard_map/ppermute | solution.py:1017
  298.7 12.8 %collective-permute-start.37 = (bf16[1,912,128]{2,1,0:T(8,128)(2,1)S(1)}, bf16[1,912,128]{2,1,0:T(8,128)(2,1)S(1)}, u32[]{:S(2)}, u32[]{:S(2)}) collective-permute-start(bf16[1,912,128]{2,1,0:T(8,128)(2,1)S(1)} %fusion.25), channel_id=1, source_target_pairs={{0,2},{1,3},{2,0},{3,1},{4,6},{5,7},{6,4},{7,5},{8,10},{9,11},{10,... | collective-permute-start | bytes 700424 | tf_op jit(solution)/shard_map/ppermute | solution.py:1017
  300.4 19.6 %collective-permute-start.38 = (bf16[2,912,128]{2,1,0:T(8,128)(2,1)S(1)}, bf16[2,912,128]{2,1,0:T(8,128)(2,1)S(1)}, u32[]{:S(2)}, u32[]{:S(2)}) collective-permute-start(bf16[2,912,128]{2,1,0:T(8,128)(2,1)S(1)} %fusion.10), channel_id=1, source_target_pairs={{0,1},{1,0},{2,3},{3,2},{4,5},{5,4},{6,7},{7,6},{8,9},{9,8},{10,11... | collective-permute-start | bytes 1400840 | tf_op jit(solution)/shard_map/ppermute | solution.py:1017
  310.0 11.2 %collective-permute-start.39 = (bf16[2,912,128]{2,1,0:T(8,128)(2,1)S(1)}, bf16[2,912,128]{2,1,0:T(8,128)(2,1)S(1)}, u32[]{:S(2)}, u32[]{:S(2)}) collective-permute-start(bf16[2,912,128]{2,1,0:T(8,128)(2,1)S(1)} %fusion.11), channel_id=1, source_target_pairs={{0,2},{1,3},{2,0},{3,1},{4,6},{5,7},{6,4},{7,5},{8,10},{9,11},{10,... | collective-permute-start | bytes 1400840 | tf_op jit(solution)/shard_map/ppermute | solution.py:1017
  312.7 25.7 %collective-permute-start.43 = (bf16[2,912,128]{2,1,0:T(8,128)(2,1)S(1)}, bf16[2,912,128]{2,1,0:T(8,128)(2,1)S(1)}, u32[]{:S(2)}, u32[]{:S(2)}) collective-permute-start(bf16[2,912,128]{2,1,0:T(8,128)(2,1)S(1)} %maximum_bitcast_fusion.2), channel_id=1, source_target_pairs={{12,8},{13,9},{14,10},{15,11},{28,24},{29,25},{30,26},{31,27}} | collective-permute-start | bytes 1400840 | tf_op jit(solution)/shard_map/ppermute | solution.py:1022
  313.4 11.9 %collective-permute-start.31 = (bf16[1,912,128]{2,1,0:T(8,128)(2,1)S(1)}, bf16[1,912,128]{2,1,0:T(8,128)(2,1)S(1)}, u32[]{:S(2)}, u32[]{:S(2)}) collective-permute-start(bf16[1,912,128]{2,1,0:T(8,128)(2,1)S(1)} %fusion.22), channel_id=1, source_target_pairs={{0,1},{1,0},{2,3},{3,2},{4,5},{5,4},{6,7},{7,6},{8,9},{9,8},{10,11... | collective-permute-start | bytes 700424 | tf_op jit(solution)/shard_map/ppermute | solution.py:1017
  313.8 11.6 %collective-permute-start.33 = (bf16[1,912,128]{2,1,0:T(8,128)(2,1)S(1)}, bf16[1,912,128]{2,1,0:T(8,128)(2,1)S(1)}, u32[]{:S(2)}, u32[]{:S(2)}) collective-permute-start(bf16[1,912,128]{2,1,0:T(8,128)(2,1)S(1)} %fusion.23), channel_id=1, source_target_pairs={{0,2},{1,3},{2,0},{3,1},{4,6},{5,7},{6,4},{7,5},{8,10},{9,11},{10,... | collective-permute-start | bytes 700424 | tf_op jit(solution)/shard_map/ppermute | solution.py:1017
  322.5 9.3 %collective-permute-start.40 = (bf16[2,912,128]{2,1,0:T(8,128)(2,1)S(1)}, bf16[2,912,128]{2,1,0:T(8,128)(2,1)S(1)}, u32[]{:S(2)}, u32[]{:S(2)}) collective-permute-start(bf16[2,912,128]{2,1,0:T(8,128)(2,1)S(1)} %fusion.16), channel_id=1, source_target_pairs={{0,4},{1,5},{2,6},{3,7},{16,20},{17,21},{18,22},{19,23}} | collective-permute-start | bytes 1400840 | tf_op jit(solution)/shard_map/ppermute | solution.py:1022
  325.6 11.3 %collective-permute-start.34 = (bf16[2,912,128]{2,1,0:T(8,128)(2,1)S(1)}, bf16[2,912,128]{2,1,0:T(8,128)(2,1)S(1)}, u32[]{:S(2)}, u32[]{:S(2)}) collective-permute-start(bf16[2,912,128]{2,1,0:T(8,128)(2,1)S(1)} %maximum_bitcast_fusion.1), channel_id=1, source_target_pairs={{4,0},{5,1},{6,2},{7,3},{12,8},{13,9},{14,10},{15,11},{20,16},{21,... | collective-permute-start | bytes 1400840 | tf_op jit(solution)/shard_map/ppermute | solution.py:1022
  332.0 12.0 %collective-permute-start.41 = (bf16[2,912,128]{2,1,0:T(8,128)(2,1)S(1)}, bf16[2,912,128]{2,1,0:T(8,128)(2,1)S(1)}, u32[]{:S(2)}, u32[]{:S(2)}) collective-permute-start(bf16[2,912,128]{2,1,0:T(8,128)(2,1)S(1)} %get-tuple-element.693), channel_id=1, source_target_pairs={{0,4},{1,5},{2,6},{3,7},{4,8},{5,9},{6,10},{7,11},{16,20},{17,21},... | collective-permute-start | bytes 1400840 | tf_op jit(solution)/shard_map/ppermute | solution.py:1022
  337.1 13.1 %collective-permute-start.35 = (bf16[2,912,128]{2,1,0:T(8,128)(2,1)S(1)}, bf16[2,912,128]{2,1,0:T(8,128)(2,1)S(1)}, u32[]{:S(2)}, u32[]{:S(2)}) collective-permute-start(bf16[2,912,128]{2,1,0:T(8,128)(2,1)S(1)} %fusion.5), channel_id=1, source_target_pairs={{8,0},{9,1},{10,2},{11,3},{24,16},{25,17},{26,18},{27,19}} | collective-permute-start | bytes 1400840 | tf_op jit(solution)/shard_map/ppermute | solution.py:1022
  344.4 13.0 %collective-permute-start.42 = (bf16[2,912,128]{2,1,0:T(8,128)(2,1)S(1)}, bf16[2,912,128]{2,1,0:T(8,128)(2,1)S(1)}, u32[]{:S(2)}, u32[]{:S(2)}) collective-permute-start(bf16[2,912,128]{2,1,0:T(8,128)(2,1)S(1)} %get-tuple-element.695), channel_id=1, source_target_pairs={{0,4},{1,5},{2,6},{3,7},{4,8},{5,9},{6,10},{7,11},{8,12},{9,13},{1... | collective-permute-start | bytes 1400840 | tf_op jit(solution)/shard_map/ppermute | solution.py:1022
  348.8 8.6 %collective-permute-start.44 = (bf16[2,912,128]{2,1,0:T(8,128)(2,1)S(1)}, bf16[2,912,128]{2,1,0:T(8,128)(2,1)S(1)}, u32[]{:S(2)}, u32[]{:S(2)}) collective-permute-start(bf16[2,912,128]{2,1,0:T(8,128)(2,1)S(1)} %get-tuple-element.696), channel_id=1, source_target_pairs={{8,4},{9,5},{10,6},{11,7},{12,8},{13,9},{14,10},{15,11},{24,20},{2... | collective-permute-start | bytes 1400840 | tf_op jit(solution)/shard_map/ppermute | solution.py:1022
  361.4 7.0 %collective-permute-start.45 = (f32[8,128]{1,0:T(8,128)S(1)}, f32[8,128]{1,0:T(8,128)S(1)}, u32[]{:S(2)}, u32[]{:S(2)}) collective-permute-start(f32[8,128]{1,0:T(8,128)S(1)} %get-tuple-element.681), channel_id=1, source_target_pairs={{0,1},{1,0},{2,3},{3,2},{4,5},{5,4},{6,7},{7,6},{8,9},{9,8},{10,11... | collective-permute-start | bytes 12296 | tf_op jit(solution)/shard_map/ppermute | solution.py:1037
  362.0 6.9 %collective-permute-start.46 = (f32[8,128]{1,0:T(8,128)S(1)}, f32[8,128]{1,0:T(8,128)S(1)}, u32[]{:S(2)}, u32[]{:S(2)}) collective-permute-start(f32[8,128]{1,0:T(8,128)S(1)} %get-tuple-element.681), channel_id=1, source_target_pairs={{0,2},{1,3},{2,0},{3,1},{4,6},{5,7},{6,4},{7,5},{8,10},{9,11},{10,... | collective-permute-start | bytes 12296 | tf_op jit(solution)/shard_map/ppermute | solution.py:1037
  363.7 7.5 %collective-permute-start.47 = (f32[8,128]{1,0:T(8,128)S(1)}, f32[8,128]{1,0:T(8,128)S(1)}, u32[]{:S(2)}, u32[]{:S(2)}) collective-permute-start(f32[8,128]{1,0:T(8,128)S(1)} %get-tuple-element.681), channel_id=1, source_target_pairs={{0,3},{1,2},{2,1},{3,0},{4,7},{5,6},{6,5},{7,4},{8,11},{9,10},{10,... | collective-permute-start | bytes 12296 | tf_op jit(solution)/shard_map/ppermute | solution.py:1037
  372.8 7.9 %collective-permute-start.52 = (f32[8,128]{1,0:T(8,128)S(1)}, f32[8,128]{1,0:T(8,128)S(1)}, u32[]{:S(2)}, u32[]{:S(2)}) collective-permute-start(f32[8,128]{1,0:T(8,128)S(1)} %add_add_fusion), channel_id=1, source_target_pairs={{0,4},{1,5},{2,6},{3,7},{4,0},{5,1},{6,2},{7,3},{8,12},{9,13},{10,... | collective-permute-start | bytes 12296 | tf_op jit(solution)/shard_map/ppermute | solution.py:1017
  377.0 5.4 %collective-permute-start.54 = (f32[8,128]{1,0:T(8,128)S(1)}, f32[8,128]{1,0:T(8,128)S(1)}, u32[]{:S(2)}, u32[]{:S(2)}) collective-permute-start(f32[8,128]{1,0:T(8,128)S(1)} %add_add_fusion), channel_id=1, source_target_pairs={{0,12},{1,13},{2,14},{3,15},{4,8},{5,9},{6,10},{7,11},{8,4},{9,5},... | collective-permute-start | bytes 12296 | tf_op jit(solution)/shard_map/ppermute | solution.py:1017
  (87 other events, 822.1 us)
